TPU v7x, 32 devices: a whole 2x2x4 slice. The times are simulated.
32 devices in a mesh: dp: 8 (over z, core), sp: 4 (over y, x).
Axes of the slice: x: 2, y: 2, z: 4, core: 2. Of those that a mesh axis runs over, the one named last changes fastest.
Arguments:
- tokens_in: bfloat16 [16, 1024, 1024], P('dp', 'sp'), may hold values from -6 to 6
- expert_ids: int32 [8, 4, 512, 1], P('dp', 'sp'), may hold values from 0 to 7; in each aligned block of 512 rows (0 to 511, 512 to 1023, ..., all dimensions but the last counted through in order) at most 128 rows name the same one
- query_weight: bfloat16 [1024, 1024], replicated, may hold values from -0.1875 to 0.1875
- key_weight: bfloat16 [1024, 1024], replicated, may hold values from -0.1875 to 0.1875
- value_weight: bfloat16 [1024, 1024], replicated, may hold values from -0.1875 to 0.1875
- out_weight: bfloat16 [1024, 1024], replicated, may hold values from -3 to 3
- norm1_gain: float32 [1024], replicated, may hold values from 0.25 to 1.75
- norm1_shift: float32 [1024], replicated, may hold values from -3 to 3
- norm2_gain: float32 [1024], replicated, may hold values from 0.25 to 1.75
- norm2_shift: float32 [1024], replicated, may hold values from -3 to 3
- up_weight: bfloat16 [8, 4096, 1024], P('dp'), may hold values from -0.1875 to 0.1875
- down_weight: bfloat16 [8, 4096, 1024], P('dp'), may hold values from -0.09375 to 0.09375
- out_cotangent: bfloat16 [16, 1024, 1024], P('dp', 'sp'), may hold values from -6 to 6
- load_mean: float32 [8], replicated, may hold values from 0.5 to 2
Outputs:
- block_out: bfloat16 [16, 1024, 1024], P('dp', 'sp')
- tokens_grad: bfloat16 [16, 1024, 1024], P('dp', 'sp')
- query_grad: float32 [1024, 1024], replicated
- key_grad: float32 [1024, 1024], replicated
- value_grad: float32 [1024, 1024], replicated
- out_grad: float32 [1024, 1024], replicated
- norm1_gain_grad: float32 [1024], replicated
- norm1_shift_grad: float32 [1024], replicated
- norm2_gain_grad: float32 [1024], replicated
- norm2_shift_grad: float32 [1024], replicated
- up_grad: float32 [8, 4096, 1024], P('dp', 'sp')
- down_grad: float32 [8, 4096, 1024], P('dp', 'sp')
- load_next: float32 [8], replicated
Inputs may be any that keep to these rules, and one draw needn't show every extreme that they name: `expert_ids`: among the 512 rows of one device no expert is named more than 128 times, and in some device's rows one expert is named exactly 128 times.
All inputs are finite; a program needn't handle non-finite values.
Results may differ from a plain program's by a relative error of at most 0.012.
Values may be sent and summed in bfloat16 or wider, within the bound.
A program may use at most 384 MiB of HBM per device.

v0:
```python
import jax
import jax.numpy as jnp
from jax import lax
from jax.sharding import PartitionSpec as P

HEADS = 16


NORM_EPSILON = 1e-05
GELU_ROOT = 0.7978845608028654
CUBIC_TERM = 0.044715


def smooth(values):
    return (
        0.5
        * values
        * (1.0 + jnp.tanh(GELU_ROOT * (values + CUBIC_TERM * values * values * values)))
    )


def smooth_slope(values):
    inner = jnp.tanh(GELU_ROOT * (values + CUBIC_TERM * values * values * values))
    return 0.5 * (1.0 + inner) + 0.5 * values * (1.0 - inner * inner) * GELU_ROOT * (
        1.0 + 3.0 * CUBIC_TERM * values * values
    )


def norm_forward(values, gain, shift):
    center = jnp.mean(values, axis=-1, keepdims=True)
    offset = values - center
    rstd = lax.rsqrt(jnp.mean(offset * offset, axis=-1, keepdims=True) + NORM_EPSILON)
    unit = offset * rstd
    return (unit * gain + shift, unit, rstd)


def norm_backward(grad, unit, rstd, gain):
    scaled = grad * gain
    inner = (
        scaled
        - jnp.mean(scaled, axis=-1, keepdims=True)
        - unit * jnp.mean(scaled * unit, axis=-1, keepdims=True)
    )
    return (inner * rstd, jnp.sum(grad * unit, axis=0), jnp.sum(grad, axis=0))


def local(
    tokens_in,
    expert_ids,
    query_weight,
    key_weight,
    value_weight,
    out_weight,
    norm1_gain,
    norm1_shift,
    norm2_gain,
    norm2_shift,
    up_weight,
    down_weight,
    out_cotangent,
    load_mean,
):
    seq_count, shard_len, model_width = tokens_in.shape
    row_count = seq_count * shard_len
    head_count = HEADS
    head_dim = model_width // head_count
    sp_ways = lax.axis_size("sp")
    seq_len = shard_len * sp_ways
    experts = load_mean.shape[0]
    slot_count = 2 * row_count // experts
    local_experts = up_weight.shape[0]
    ff_width = up_weight.shape[1]
    score_scale = head_dim ** (-0.5)
    inputs = tokens_in.reshape(row_count, model_width).astype(jnp.float32)
    first_normed, unit1, rstd1 = norm_forward(inputs, norm1_gain, norm1_shift)
    normed1_b = first_normed.astype(jnp.bfloat16)
    query_b = jnp.dot(normed1_b, query_weight, preferred_element_type=jnp.float32).astype(
        jnp.bfloat16
    )
    key_b = jnp.dot(normed1_b, key_weight, preferred_element_type=jnp.float32).astype(jnp.bfloat16)
    value_b = jnp.dot(normed1_b, value_weight, preferred_element_type=jnp.float32).astype(
        jnp.bfloat16
    )
    key_local = key_b.reshape(seq_count, shard_len, model_width)
    value_local = value_b.reshape(seq_count, shard_len, model_width)
    key_all, value_all = (
        lax.all_gather(key_local, "sp", axis=1, tiled=True),
        lax.all_gather(value_local, "sp", axis=1, tiled=True),
    )
    query_pos = lax.axis_index("sp") * shard_len + jnp.arange(shard_len, dtype=jnp.int32)
    visible = jnp.arange(seq_len, dtype=jnp.int32)[None, :] <= query_pos[:, None]
    query_h = query_b.reshape(seq_count, shard_len, head_count, head_dim)

    def scores(key_rows):
        key_h = key_rows.reshape(seq_count, seq_len, head_count, head_dim)
        raw = (
            jnp.einsum("sqhd,skhd->shqk", query_h, key_h, preferred_element_type=jnp.float32)
            * score_scale
        )
        return jnp.where(visible[None, None], raw, -1e30)

    logits = scores(key_all)
    row_max = jnp.max(logits, axis=-1, keepdims=True)
    exp_terms = jnp.exp(logits - row_max)
    total = jnp.sum(exp_terms, axis=-1, keepdims=True)
    attn_prob_b = (exp_terms / total).astype(jnp.bfloat16)
    log_total = row_max + jnp.log(total)
    value_h = value_all.reshape(seq_count, seq_len, head_count, head_dim)
    attention_mixed = jnp.einsum(
        "shqk,skhd->sqhd", attn_prob_b, value_h, preferred_element_type=jnp.float32
    )
    mixed_b = attention_mixed.reshape(row_count, model_width).astype(jnp.bfloat16)
    attn_out = jnp.dot(mixed_b, out_weight, preferred_element_type=jnp.float32)
    residual_stream = inputs + attn_out
    normed2, unit2, rstd2 = norm_forward(residual_stream, norm2_gain, norm2_shift)
    normed2_b = normed2.astype(jnp.bfloat16)
    routes = expert_ids.reshape(row_count)
    one_hot = (routes[:, None] == jnp.arange(experts, dtype=jnp.int32)[None, :]).astype(jnp.int32)
    running = jnp.cumsum(one_hot, axis=0) - 1
    slot_of = jnp.sum(running * one_hot, axis=1)
    target = routes * slot_count + slot_of
    placer = (jnp.arange(experts * slot_count, dtype=jnp.int32)[:, None] == target[None, :]).astype(
        jnp.bfloat16
    )
    outgoing = jnp.dot(placer, normed2_b, preferred_element_type=jnp.float32).astype(jnp.bfloat16)
    outgoing = outgoing.reshape(experts, slot_count, model_width)
    received = lax.all_to_all(outgoing, "dp", split_axis=0, concat_axis=0, tiled=True)
    parts = received.reshape(-1, local_experts, received.shape[1], model_width)
    pre_act = jnp.einsum("sxcd,xfd->sxcf", parts, up_weight, preferred_element_type=jnp.float32)
    hidden_b = smooth(pre_act).astype(jnp.bfloat16)
    expert_out = jnp.einsum(
        "sxcf,xfd->sxcd", hidden_b, down_weight, preferred_element_type=jnp.float32
    ).astype(jnp.bfloat16)
    returned = lax.all_to_all(
        expert_out.reshape(received.shape), "dp", split_axis=0, concat_axis=0, tiled=True
    )
    flat_shape = (received.shape[0], received.shape[1], ff_width)
    returned, received, pre_kept, hidden_kept = (
        returned,
        received,
        pre_act.reshape(flat_shape),
        hidden_b.reshape(flat_shape),
    )
    expert_rows = jnp.einsum(
        "er,ed->rd",
        placer,
        returned.reshape(experts * slot_count, model_width),
        preferred_element_type=jnp.float32,
    )
    block_out = (
        (residual_stream + expert_rows)
        .astype(jnp.bfloat16)
        .reshape(seq_count, shard_len, model_width)
    )
    cot_b = out_cotangent.reshape(row_count, model_width)
    grad_out = cot_b.astype(jnp.float32)
    cot_send = jnp.dot(placer, cot_b, preferred_element_type=jnp.float32).astype(jnp.bfloat16)
    cot_send = cot_send.reshape(experts, slot_count, model_width)
    arrived = lax.all_to_all(cot_send, "dp", split_axis=0, concat_axis=0, tiled=True)
    arrived_p = arrived.reshape(-1, local_experts, slot_count, model_width)
    pre_p = pre_kept.reshape(-1, local_experts, slot_count, ff_width)
    dhidden = jnp.einsum(
        "sxcd,xfd->sxcf", arrived_p, down_weight, preferred_element_type=jnp.float32
    )
    dpre_b = (dhidden * smooth_slope(pre_p)).astype(jnp.bfloat16)
    dnormed_send = jnp.einsum(
        "sxcf,xfd->sxcd", dpre_b, up_weight, preferred_element_type=jnp.float32
    ).astype(jnp.bfloat16)
    dnormed_send = dnormed_send.reshape(-1, slot_count, model_width)
    dnormed_back = lax.all_to_all(dnormed_send, "dp", split_axis=0, concat_axis=0, tiled=True)
    hidden_p = hidden_kept.reshape(-1, local_experts, slot_count, ff_width)
    received_p = received.reshape(-1, local_experts, slot_count, model_width)
    up_full = jnp.einsum("sxcf,sxcd->xfd", dpre_b, received_p, preferred_element_type=jnp.float32)
    down_full = jnp.einsum(
        "sxcf,sxcd->xfd", hidden_p, arrived_p, preferred_element_type=jnp.float32
    )
    up_grad, down_grad = (
        lax.psum_scatter(
            up_full.astype(jnp.bfloat16), "sp", scatter_dimension=1, tiled=True
        ).astype(jnp.float32),
        lax.psum_scatter(
            down_full.astype(jnp.bfloat16), "sp", scatter_dimension=1, tiled=True
        ).astype(jnp.float32),
    )
    dnormed2 = jnp.einsum(
        "er,ed->rd",
        placer,
        dnormed_back.reshape(experts * slot_count, model_width),
        preferred_element_type=jnp.float32,
    )
    dresid_norm, gain_two_grad, shift_two_grad = norm_backward(dnormed2, unit2, rstd2, norm2_gain)
    dresid = grad_out + dresid_norm
    dattn_b = dresid.astype(jnp.bfloat16)
    out_grad = jnp.einsum("rd,re->de", mixed_b, dattn_b, preferred_element_type=jnp.float32)
    dmixed_b = jnp.einsum(
        "re,de->rd", dattn_b, out_weight, preferred_element_type=jnp.float32
    ).astype(jnp.bfloat16)
    key_back, value_back = (
        lax.all_gather(key_local, "sp", axis=1, tiled=True),
        lax.all_gather(value_local, "sp", axis=1, tiled=True),
    )
    logits_back = scores(key_back)
    attn_prob = jnp.exp(logits_back - log_total)
    prob_back_b = attn_prob.astype(jnp.bfloat16)
    key_h = key_back.reshape(seq_count, seq_len, head_count, head_dim)
    value_hb = value_back.reshape(seq_count, seq_len, head_count, head_dim)
    dmixed_h = dmixed_b.reshape(seq_count, shard_len, head_count, head_dim)
    dprob = jnp.einsum("sqhd,skhd->shqk", dmixed_h, value_hb, preferred_element_type=jnp.float32)
    row_delta = jnp.sum(attn_prob * dprob, axis=-1, keepdims=True)
    dlogit_b = (attn_prob * (dprob - row_delta)).astype(jnp.bfloat16)
    dquery = (
        jnp.einsum("shqk,skhd->sqhd", dlogit_b, key_h, preferred_element_type=jnp.float32)
        * score_scale
    )
    dquery_b = dquery.reshape(row_count, model_width).astype(jnp.bfloat16)
    dkey_terms = (
        jnp.einsum("shqk,sqhd->skhd", dlogit_b, query_h, preferred_element_type=jnp.float32)
        * score_scale
    )
    dvalue_terms = jnp.einsum(
        "shqk,sqhd->skhd", prob_back_b, dmixed_h, preferred_element_type=jnp.float32
    )
    dkey, dvalue = (
        lax.psum_scatter(
            dkey_terms.reshape(seq_count, seq_len, model_width),
            "sp",
            scatter_dimension=1,
            tiled=True,
        ),
        lax.psum_scatter(
            dvalue_terms.reshape(seq_count, seq_len, model_width),
            "sp",
            scatter_dimension=1,
            tiled=True,
        ),
    )
    dkey_b = dkey.reshape(row_count, model_width).astype(jnp.bfloat16)
    dvalue_b = dvalue.reshape(row_count, model_width).astype(jnp.bfloat16)
    query_grad = jnp.einsum("rd,re->de", normed1_b, dquery_b, preferred_element_type=jnp.float32)
    key_grad = jnp.einsum("rd,re->de", normed1_b, dkey_b, preferred_element_type=jnp.float32)
    value_grad = jnp.einsum("rd,re->de", normed1_b, dvalue_b, preferred_element_type=jnp.float32)
    dnormed1 = jnp.einsum("re,de->rd", dquery_b, query_weight, preferred_element_type=jnp.float32)
    dnormed1 = dnormed1 + jnp.einsum(
        "re,de->rd", dkey_b, key_weight, preferred_element_type=jnp.float32
    )
    dnormed1 = dnormed1 + jnp.einsum(
        "re,de->rd", dvalue_b, value_weight, preferred_element_type=jnp.float32
    )
    dinput_norm, gain_one_grad, shift_one_grad = norm_backward(dnormed1, unit1, rstd1, norm1_gain)
    tokens_grad = (
        (dresid + dinput_norm).astype(jnp.bfloat16).reshape(seq_count, shard_len, model_width)
    )
    counts = jnp.sum(one_hot, axis=0).astype(jnp.float32)
    summed = lax.psum(
        (
            query_grad,
            key_grad,
            value_grad,
            out_grad,
            gain_one_grad,
            shift_one_grad,
            gain_two_grad,
            shift_two_grad,
            counts,
        ),
        ("dp", "sp"),
    )
    load_now = summed[8] * experts / (row_count * lax.axis_size("dp") * sp_ways)
    load_next = 0.9 * load_mean + 0.1 * load_now
    return (
        block_out,
        tokens_grad,
        summed[0],
        summed[1],
        summed[2],
        summed[3],
        summed[4],
        summed[5],
        summed[6],
        summed[7],
        up_grad,
        down_grad,
        load_next,
    )


def solution(mesh):
    return jax.shard_map(
        local,
        mesh=mesh,
        in_specs=(
            P("dp", "sp", None),
            P("dp", "sp", None, None),
            P(),
            P(),
            P(),
            P(),
            P(),
            P(),
            P(),
            P(),
            P("dp", None, None),
            P("dp", None, None),
            P("dp", "sp", None),
            P(),
        ),
        out_specs=(
            P("dp", "sp", None),
            P("dp", "sp", None),
            P(),
            P(),
            P(),
            P(),
            P(),
            P(),
            P(),
            P(),
            P("dp", "sp", None),
            P("dp", "sp", None),
            P(),
        ),
        check_vma=False,
    )
```

profile of v0, /device:TPU:9, one launch (start us, length us, event | category | flops | bytes accessed | tf_op | source)
XLA Modules:
  0.0 1053.7 jit_solution(11870787457211960923)
XLA Ops:
  31.8 36.2 %all-gather.5.cloned.1.call-done = bf16[2,1024,1024]{2,1,0:T(8,128)(2,1)} async-done(((bf16[2,256,1024]{2,1,0:T(8,128)(2,1)}), bf16[2,1024,1024]{2,1,0:T(8,128)(2,1)}) %all-gather.5.cloned.1.call-update) | async-done | bytes 4194320 | tf_op jit(solution)/shard_map/all_gather | solution.py:87
  74.2 16.0 %fusion.91 = (f32[2,16,256]{2,1,0:T(8,128)S(1)}, f32[2,16,256,1024]{3,2,1,0:T(8,128)}) fusion(bf16[2,256,16,64]{1,3,2,0:T(8,128)(2,1)} %copy.42, bf16[2,1024,16,64]{1,3,2,0:T(8,128)(2,1)} %bitcast.198, pred[256,1024]{1,0:T(8,128)(4,1)S(1)} %iota_compare_fusion.11), kind=kOutput, calls=%fused_computation.131 | convolution fusion | flops 1098899456 | bytes 39092224 | tf_op jit(solution)/shard_map/sqhd,skhd->shqk/dot_general | solution.py:97
  90.2 14.9 %fusion = f32[2,16,256]{2,1,0:T(8,128)S(1)} fusion(f32[2,16,256,1024]{3,2,1,0:T(8,128)} %get-tuple-element.37, f32[2,16,256]{2,1,0:T(8,128)S(1)} %get-tuple-element.36), kind=kLoop, calls=%fused_computation.6 | loop fusion | flops 16769024 | bytes 33619968 | tf_op jit(solution)/shard_map/reduce_sum | solution.py:105
  105.1 18.1 %all-gather.3.cloned.1.call-done = bf16[2,1024,1024]{2,1,0:T(8,128)(2,1)} async-done(((bf16[2,256,1024]{2,1,0:T(8,128)(2,1)}), bf16[2,1024,1024]{2,1,0:T(8,128)(2,1)}) %all-gather.3.cloned.1.call-update) | async-done | bytes 4194320 | tf_op jit(solution)/shard_map/all_gather | solution.py:88
  129.4 16.3 %fusion.67 = bf16[2,256,16,64]{1,3,2,0:T(8,128)(2,1)} fusion(bf16[2,1024,16,64]{1,3,2,0:T(8,128)(2,1)} %bitcast.201, f32[2,16,256,1024]{3,2,1,0:T(8,128)} %get-tuple-element.37, f32[2,16,256]{2,1,0:T(8,128)S(1)} %fusion, f32[2,16,256]{2,1,0:T(8,128)S(1)} %get-tuple-element.36), kind=kOutput, calls=%fused_computation.89 | convolution fusion | flops 1099431936 | bytes 38862848 | tf_op jit(solution)/shard_map/shqk,skhd->sqhd/dot_general | solution.py:109
  161.6 42.9 %all-to-all-done = bf16[8,128,1024]{2,1,0:T(8,128)(2,1)} async-done(((bf16[8,128,1024]{2,1,0:T(8,128)(2,1)}), bf16[8,128,1024]{2,1,0:T(8,128)(2,1)}, u32[]{:S(2)}, u32[]{:S(2)}) %all-to-all-start) | async-done | bytes 2097184 | tf_op jit(solution)/shard_map/all_to_all | solution.py:127
  212.4 16.0 %fusion.22 = f32[8,128,4096]{2,1,0:T(8,128)} fusion(bf16[8,128,1024]{2,1,0:T(8,128)(2,1)} %all-to-all-done, bf16[1,4096,1024]{2,1,0:T(8,128)(2,1)} %param.24), kind=kOutput, calls=%fused_computation.33 | convolution fusion | flops 8589934592 | bytes 27262976 | tf_op jit(solution)/shard_map/sxcd,xfd->sxcf/dot_general | solution.py:129
  228.5 29.5 %all-to-all-done.2 = bf16[8,128,1024]{2,1,0:T(8,128)(2,1)} async-done(((bf16[8,128,1024]{2,1,0:T(8,128)(2,1)}), bf16[8,128,1024]{2,1,0:T(8,128)(2,1)}, u32[]{:S(2)}, u32[]{:S(2)}) %all-to-all-start.2) | async-done | bytes 2097184 | tf_op jit(solution)/shard_map/all_to_all | solution.py:159
  257.9 23.7 %fusion.8 = bf16[8,1,128,4096]{3,2,0,1:T(8,128)(2,1)} fusion(f32[8,128,4096]{2,1,0:T(8,128)} %fusion.22, bf16[8,128,1024]{2,1,0:T(8,128)(2,1)} %all-to-all-done.2, bf16[1,4096,1024]{2,1,0:T(8,128)(2,1)} %param.25), kind=kOutput, calls=%fused_computation.16 | convolution fusion | flops 8669626368 | bytes 35651584 | tf_op jit(solution)/shard_map/sxcd,xfd->sxcf/dot_general | solution.py:162
  281.7 14.8 %fusion.60 = bf16[8,128,1024]{2,1,0:T(8,128)(2,1)} fusion(bf16[1,4096,1024]{2,1,0:T(8,128)(2,1)} %param.24, bf16[8,1,128,4096]{3,2,0,1:T(8,128)(2,1)} %fusion.8), kind=kOutput, calls=%fused_computation.80 | convolution fusion | flops 8590983168 | bytes 18874368 | tf_op jit(solution)/shard_map/sxcf,xfd->sxcd/dot_general | solution.py:166
  304.4 45.5 %all-to-all-done.3 = bf16[8,128,1024]{2,1,0:T(8,128)(2,1)} async-done(((bf16[8,128,1024]{2,1,0:T(8,128)(2,1)}), bf16[8,128,1024]{2,1,0:T(8,128)(2,1)}, u32[]{:S(2)}, u32[]{:S(2)}) %all-to-all-start.3) | async-done | bytes 2097184 | tf_op jit(solution)/shard_map/all_to_all | solution.py:170
  363.2 16.8 %fusion.9 = f32[2,16,64,1024]{3,2,1,0:T(8,128)} fusion(bf16[2,256,16,64]{1,3,2,0:T(8,128)(2,1)S(1)} %copy.45, f32[2,16,256,1024]{3,2,1,0:T(8,128)} %get-tuple-element.37, f32[2,16,256]{2,1,0:T(8,128)S(1)} %log_add_fusion), kind=kOutput, calls=%fused_computation.17 | convolution fusion | flops 1090519040 | bytes 43024384 | tf_op jit(solution)/shard_map/shqk,sqhd->skhd/dot_general | solution.py:220
  388.7 24.7 %multiply_reduce_fusion = (f32[2,16,256]{2,1,0:T(8,128)S(1)}, f32[2,16,256,1024]{3,2,1,0:T(8,128)}) fusion(f32[2,16,256,1024]{3,2,1,0:T(8,128)} %get-tuple-element.37, f32[2,16,256]{2,1,0:T(8,128)S(1)} %log_add_fusion, bf16[2,256,16,64]{1,3,2,0:T(8,128)(2,1)S(1)} %copy.45, bf16[2,1024,16,64]{1,3,2,0:T(8,128)(2,1)} %bitcast.202), kind=kOutput, calls=%fused_computation.1 | convolution fusion | flops 1098899456 | bytes 72417280 | tf_op jit(solution)/shard_map/sqhd,skhd->shqk/dot_general | solution.py:208
  413.4 29.5 %multiply_convert_fusion = bf16[2,16,256,1024]{3,2,1,0:T(8,128)(2,1)} fusion(f32[2,16,256,1024]{3,2,1,0:T(8,128)} %get-tuple-element.42, f32[2,16,256,1024]{3,2,1,0:T(8,128)} %get-tuple-element.37, f32[2,16,256]{2,1,0:T(8,128)S(1)} %get-tuple-element.41, f32[2,16,256]{2,1,0:T(8,128)S(1)} %log_add_fusion), kind=kLoop, calls=%fused_computation | loop fusion | flops 33554432 | bytes 83951616 | tf_op jit(solution)/shard_map/convert_element_type | solution.py:210
  442.9 12.1 %broadcast_multiply_fusion = f32[2,16,64,1024]{3,2,1,0:T(8,128)} fusion(bf16[2,256,16,64]{1,3,2,0:T(8,128)(2,1)S(1)} %copy-done.9, bf16[2,16,256,1024]{3,2,1,0:T(8,128)(2,1)} %multiply_convert_fusion), kind=kOutput, calls=%fused_computation.37 | convolution fusion | flops 1075838976 | bytes 26214400 | tf_op jit(solution)/shard_map/shqk,sqhd->skhd/dot_general | solution.py:217
  464.2 18.1 %fusion.27 = bf16[1,4096,1024]{2,1,0:T(8,128)(2,1)} fusion(bf16[8,128,1024]{2,1,0:T(8,128)(2,1)} %all-to-all-done.2, f32[8,128,4096]{2,1,0:T(8,128)} %fusion.22), kind=kOutput, calls=%fused_computation.36 | convolution fusion | flops 8631877632 | bytes 27262976 | tf_op jit(solution)/shard_map/sxcf,sxcd->xfd/dot_general | solution.py:174
  482.3 15.1 %fusion.24 = bf16[1,4096,1024]{2,1,0:T(8,128)(2,1)} fusion(bf16[8,128,1024]{2,1,0:T(8,128)(2,1)} %all-to-all-done, bf16[8,1,128,4096]{3,2,0,1:T(8,128)(2,1)} %fusion.8), kind=kOutput, calls=%fused_computation.35 | convolution fusion | flops 8594128896 | bytes 18874368 | tf_op jit(solution)/shard_map/sxcf,sxcd->xfd/dot_general | solution.py:173
  500.2 13.9 %fusion.66 = bf16[2,256,16,64]{1,3,2,0:T(8,128)(2,1)} fusion(bf16[2,1024,16,64]{1,3,2,0:T(8,128)(2,1)} %bitcast.199, bf16[2,16,256,1024]{3,2,1,0:T(8,128)(2,1)} %multiply_convert_fusion), kind=kOutput, calls=%fused_computation.88 | convolution fusion | flops 1074790400 | bytes 22020096 | tf_op jit(solution)/shard_map/shqk,skhd->sqhd/dot_general | solution.py:212
  526.2 39.5 %reduce-scatter.5.cloned.1.call-done = f32[2,256,1024]{2,1,0:T(8,128)} async-done(((f32[2,1024,1024]{2,1,0:T(8,128)}), f32[2,256,1024]{2,1,0:T(8,128)}) %reduce-scatter.5.cloned.1.call-update) | async-done | bytes 2097168 | tf_op jit(solution)/shard_map/reduce_scatter | solution.py:224
  574.5 17.9 %fusion.53 = bf16[8,128,1024]{2,1,0:T(8,128)(2,1)} fusion(bf16[1,4096,1024]{2,1,0:T(8,128)(2,1)} %param.25, f32[8,128,4096]{2,1,0:T(8,128)} %fusion.22), kind=kOutput, calls=%fused_computation.77 | convolution fusion | flops 8628731904 | bytes 27262976 | tf_op jit(solution)/shard_map/sxcf,xfd->sxcd/dot_general | solution.py:131
  602.5 40.8 %all-to-all-done.1 = bf16[8,128,1024]{2,1,0:T(8,128)(2,1)} async-done(((bf16[8,128,1024]{2,1,0:T(8,128)(2,1)}), bf16[8,128,1024]{2,1,0:T(8,128)(2,1)}, u32[]{:S(2)}, u32[]{:S(2)}) %all-to-all-start.1) | async-done | bytes 2097184 | tf_op jit(solution)/shard_map/all_to_all | solution.py:134
  659.0 85.6 %reduce-scatter.9.cloned.1.call-done = bf16[1,1024,1024]{2,1,0:T(8,128)(2,1)} async-done(((bf16[1,4096,1024]{2,1,0:T(8,128)(2,1)}), bf16[1,1024,1024]{2,1,0:T(8,128)(2,1)}) %reduce-scatter.9.cloned.1.call-update) | async-done | bytes 2097168 | tf_op jit(solution)/shard_map/reduce_scatter | solution.py:178
  754.0 42.1 %all-reduce = (f32[1024]{0:T(1024)}, f32[1024]{0:T(1024)}, f32[1024]{0:T(1024)}, f32[1024]{0:T(1024)}, f32[8]{0:T(128)S(1)}) all-reduce(f32[1024]{0:T(1024)S(1)} %get-tuple-element.15, f32[1024]{0:T(1024)S(1)} %get-tuple-element.20, f32[1024]{0:T(1024)S(1)} %copy-done.38, ...), channel_id=1, replica_groups=mesh['dp'=8,'sp'=4] {'dp','sp'}, use_global_device_ids=true, to_apply=%region_21.22 | all-reduce | flops 4104 | bytes 32832 | tf_op jit(solution)/shard_map/psum | solution.py:254
  800.9 231.4 %all-reduce.4.cloned.1.call-done = (f32[1024,1024]{1,0:T(8,128)}, f32[1024,1024]{1,0:T(8,128)}, f32[1024,1024]{1,0:T(8,128)}, f32[1024,1024]{1,0:T(8,128)}) async-done(((f32[1024,1024]{1,0:T(8,128)}, f32[1024,1024]{1,0:T(8,128)}, f32[1024,1024]{1,0:T(8,128)}, f32[1024,1024]{1,0:T(8,128)}), (f32[1024,1024]{1,0:T(8,128)}, f32[1024,1024]{1,0:T(8,128)}, f32[1024,1024]{1,0:T(8,128)}, ...) | async-done | bytes 16777232 | tf_op jit(solution)/shard_map/psum | solution.py:254
  (181 shorter events, 177.6 us)
Async XLA Ops:
  7.2 7.1 copy-start
  7.2 60.8 %all-gather.5.cloned.1.call-start = ((), (), s32[]{:S(2)}) async-start(), calls=%async_computation.9 | async-start | bytes 5242880 | tf_op jit(solution)/shard_map/all_gather | solution.py:87
  7.3 4.4 copy-start.43
  8.9 5.1 copy-start.29
  14.0 109.2 %all-gather.3.cloned.1.call-start = ((), (), s32[]{:S(2)}) async-start(), calls=%async_computation.8 | async-start | bytes 5242880 | tf_op jit(solution)/shard_map/all_gather | solution.py:88
  31.6 318.3 %copy-start.40 = (s32[512]{0:T(512)}, s32[512]{0:T(512)S(1)}, u32[]{:S(2)}) copy-start(s32[512]{0:T(512)S(1)} %multiply_add_fusion.2) | copy-start | bytes 6148
  153.4 5.6 copy-start.23
  153.4 51.1 %all-to-all-start = ((bf16[8,128,1024]{2,1,0:T(8,128)(2,1)}), bf16[8,128,1024]{2,1,0:T(8,128)(2,1)}, u32[]{:S(2)}, u32[]{:S(2)}) async-start(bf16[8,128,1024]{2,1,0:T(8,128)(2,1)} %bitcast.208), calls=%async_computation | async-start | bytes 4194304 | tf_op jit(solution)/shard_map/all_to_all | solution.py:127
  204.5 53.4 %all-to-all-start.2 = ((bf16[8,128,1024]{2,1,0:T(8,128)(2,1)}), bf16[8,128,1024]{2,1,0:T(8,128)(2,1)}, u32[]{:S(2)}, u32[]{:S(2)}) async-start(bf16[8,128,1024]{2,1,0:T(8,128)(2,1)} %bitcast.207), calls=%async_computation.2 | async-start | bytes 4194304 | tf_op jit(solution)/shard_map/all_to_all | solution.py:159
  296.5 53.4 %all-to-all-start.3 = ((bf16[8,128,1024]{2,1,0:T(8,128)(2,1)}), bf16[8,128,1024]{2,1,0:T(8,128)(2,1)}, u32[]{:S(2)}, u32[]{:S(2)}) async-start(bf16[8,128,1024]{2,1,0:T(8,128)(2,1)} %fusion.60), calls=%async_computation.3 | async-start | bytes 4194304 | tf_op jit(solution)/shard_map/all_to_all | solution.py:170
  304.4 219.1 %reduce-scatter.7.cloned.1.call-start = ((), (), s32[]{:S(2)}) async-start(), calls=%async_computation.11 | async-start | bytes 10485760 | tf_op jit(solution)/shard_map/reduce_scatter | solution.py:230
  349.9 4.8 copy-start.6
  388.7 176.9 %reduce-scatter.5.cloned.1.call-start = ((), (), s32[]{:S(2)}) async-start(), calls=%async_computation.10 | async-start | bytes 10485760 | tf_op jit(solution)/shard_map/reduce_scatter | solution.py:224
  413.4 29.5 %copy-start.9 = (bf16[2,256,16,64]{1,3,2,0:T(8,128)(2,1)S(1)}, bf16[2,256,16,64]{1,3,2,0:T(8,128)(2,1)}, u32[]{:S(2)}) copy-start(bf16[2,256,16,64]{1,3,2,0:T(8,128)(2,1)} %copy.42) | copy-start | bytes 3145732
  464.1 190.9 %reduce-scatter.11.cloned.1.call-start = ((), (), s32[]{:S(2)}) async-start(), calls=%async_computation.13 | async-start | bytes 10485760 | tf_op jit(solution)/shard_map/reduce_scatter | solution.py:181
  482.3 262.4 %reduce-scatter.9.cloned.1.call-start = ((), (), s32[]{:S(2)}) async-start(), calls=%async_computation.12 | async-start | bytes 10485760 | tf_op jit(solution)/shard_map/reduce_scatter | solution.py:178
  497.5 534.8 %all-reduce.4.cloned.1.call-start = ((), (), s32[]{:S(2)}) async-start(), calls=%async_computation.14 | async-start | bytes 33554432 | tf_op jit(solution)/shard_map/psum | solution.py:254
  592.3 5.5 copy-start.42
  592.3 51.0 %all-to-all-start.1 = ((bf16[8,128,1024]{2,1,0:T(8,128)(2,1)}), bf16[8,128,1024]{2,1,0:T(8,128)(2,1)}, u32[]{:S(2)}, u32[]{:S(2)}) async-start(bf16[8,128,1024]{2,1,0:T(8,128)(2,1)} %fusion.53), calls=%async_computation.1 | async-start | bytes 4194304 | tf_op jit(solution)/shard_map/all_to_all | solution.py:134
  597.9 45.5 %copy-start.41 = (s32[512]{0:T(512)S(1)}, s32[512]{0:T(512)}, u32[]{:S(2)}) copy-start(s32[512]{0:T(512)} %copy-done.40) | copy-start | bytes 6148
  744.6 4.2 copy-start.18
  744.6 4.2 copy-start.44
  750.8 45.3 %copy-start.46 = (f32[8]{0:T(128)S(1)}, f32[8]{0:T(128)}, u32[]{:S(2)}) copy-start(f32[8]{0:T(128)} %param.27) | copy-start | bytes 100
  1032.3 4.9 copy-start.12
  (36 other events, 90.1 us)
Sparse Core Ops, SparseCore 0:
  14.1 53.8 all-gather.4
  70.4 52.6 all-gather.2
  388.8 87.1 reduce-scatter.6
  479.2 86.4 reduce-scatter.4
  568.5 86.3 reduce-scatter.10
  658.2 86.4 reduce-scatter.8
  751.6 280.6 all-reduce.3
where the time goes:
time: 1060 us; the launch traced here: 1050 us
  waiting for transfers between devices  577 us (54%)
  matrix products  255 us (24%)
  other arithmetic  71 us (7%)
  local copies, waits for them, and re-layouts  66.8 us (6%)
  blocking collectives  42.1 us (4%)
  starting transfers between devices  27.4 us (3%)
  between operations  14.8 us (1%)
    psum x1, waiting for transfers between devices, local(): lax.psum((query_grad, key_grad, value_grad, out_grad, gain_one_grad, shif...  231 us
    reduce_scatter x1, waiting for transfers between devices, local(): lax.psum_scatter(up_full.astype(jnp.bfloat16), 'sp', scatter_dimension=1,...  85.6 us
    all_to_all x1, waiting for transfers between devices, local(): lax.all_to_all(dnormed_send, 'dp', split_axis=0, concat_axis=0, tiled=True)  45.5 us
    all_to_all x1, waiting for transfers between devices, local(): lax.all_to_all(outgoing, 'dp', split_axis=0, concat_axis=0, tiled=True)  42.9 us
    psum x1, blocking collectives, local(): lax.psum((query_grad, key_grad, value_grad, out_grad, gain_one_grad, shif...  42.1 us
    all_to_all x1, waiting for transfers between devices, local(): lax.all_to_all(expert_out.reshape(received.shape), 'dp', split_axis=0, co...  40.8 us
    reduce_scatter x1, waiting for transfers between devices, local(): lax.psum_scatter(dkey_terms.reshape(seq_count, seq_len, model_width), 'sp...  39.5 us
    all_gather x1, waiting for transfers between devices, local(): lax.all_gather(key_local, 'sp', axis=1, tiled=True)  36.2 us
  transfers between devices with their start and end apart: 11, of which 10 were waited for; matrix products, arithmetic and copies ran while one was open for 25% of the time, Pallas kernels for 0%

commit v1 on v0

v1 whole, which is shorter than its diff:
```python
import functools

import jax
import jax.numpy as jnp
from jax import lax
from jax.experimental import pallas as pl
from jax.experimental.pallas import tpu as pltpu
from jax.sharding import PartitionSpec as P

HEADS = 16
MESH = pl.DeviceIdType.MESH
BLOCK = 256
LANES = 128
VMEM_BYTES = 60 * 2**20

NORM_EPSILON = 1e-05
GELU_ROOT = 0.7978845608028654
CUBIC_TERM = 0.044715

ROWS_BY_COLS = (((1,), (0,)), ((), ()))
ROWS_BY_ROWS = (((1,), (1,)), ((), ()))
COLS_BY_COLS = (((0,), (0,)), ((), ()))


def smooth(values):
    return (
        0.5
        * values
        * (1.0 + jnp.tanh(GELU_ROOT * (values + CUBIC_TERM * values * values * values)))
    )


def smooth_slope(values):
    inner = jnp.tanh(GELU_ROOT * (values + CUBIC_TERM * values * values * values))
    return 0.5 * (1.0 + inner) + 0.5 * values * (1.0 - inner * inner) * GELU_ROOT * (
        1.0 + 3.0 * CUBIC_TERM * values * values
    )


def norm_forward(values, gain, shift):
    center = jnp.mean(values, axis=-1, keepdims=True)
    offset = values - center
    rstd = lax.rsqrt(jnp.mean(offset * offset, axis=-1, keepdims=True) + NORM_EPSILON)
    unit = offset * rstd
    return (unit * gain + shift, unit, rstd)


def norm_backward(grad, unit, rstd, gain):
    scaled = grad * gain
    inner = (
        scaled
        - jnp.mean(scaled, axis=-1, keepdims=True)
        - unit * jnp.mean(scaled * unit, axis=-1, keepdims=True)
    )
    return (inner * rstd, jnp.sum(grad * unit, axis=0), jnp.sum(grad, axis=0))


def mxu(left, right, dims=ROWS_BY_COLS):
    return lax.dot_general(left, right, dims, preferred_element_type=jnp.float32)


def span(index, size):
    return pl.ds(pl.multiple_of(index * size, size), size)


def greet(peers):
    barrier = pltpu.get_barrier_semaphore()
    for peer in peers:
        pl.semaphore_signal(barrier, inc=1, device_id=peer, device_id_type=MESH)
    pl.semaphore_wait(barrier, len(peers))


def send(source, target, send_sem, recv_sem, peer):
    return pltpu.make_async_remote_copy(
        src_ref=source,
        dst_ref=target,
        send_sem=send_sem,
        recv_sem=recv_sem,
        device_id=peer,
        device_id_type=MESH,
    )


def attend_forward(
    ways,
    head_dim,
    x_ref,
    wq_ref,
    wk_ref,
    wv_ref,
    gain_ref,
    shift_ref,
    normed_ref,
    q_ref,
    k_ref,
    v_ref,
    log_ref,
    mixed_ref,
    x_all,
    mixed_f,
    mixed_h,
    log_s,
    x_send,
    x_recv,
    m_send,
    m_recv,
):
    seqs, shard, _ = x_ref.shape
    seq_len, width = q_ref.shape[1:]
    heads = width // head_dim
    me = lax.axis_index("sp")
    peer = [lax.rem(me + d, ways) for d in range(ways)]
    origin = [lax.rem(me + ways - d, ways) for d in range(ways)]
    greet([{"sp": peer[d]} for d in range(1, ways)])

    def x_copy(s, d):
        return send(
            x_ref.at[s],
            x_all.at[s, span(me, shard)],
            x_send.at[s, d],
            x_recv.at[s, d],
            {"sp": peer[d]},
        )

    def mixed_copy(s, d):
        return send(
            mixed_h.at[s, span(peer[d], shard)],
            mixed_ref.at[s, :, span(me, width)],
            m_send.at[s, d],
            m_recv.at[s, d],
            {"sp": peer[d]},
        )

    lane = lax.broadcasted_iota(jnp.int32, (1, width), 1) // head_dim
    log_lane = lax.broadcasted_iota(jnp.int32, (1, LANES), 1)
    visible = lax.broadcasted_iota(jnp.int32, (BLOCK, BLOCK), 1) <= lax.broadcasted_iota(
        jnp.int32, (BLOCK, BLOCK), 0
    )
    scale = head_dim ** (-0.5)

    def project(s, rows, values):
        normed, _, _ = norm_forward(values.astype(jnp.float32), gain_ref[...], shift_ref[...])
        normed = normed.astype(jnp.bfloat16)
        normed_ref[s, rows, :] = normed
        q_ref[s, rows, :] = mxu(normed, wq_ref[...]).astype(jnp.bfloat16)
        k_ref[s, rows, :] = mxu(normed, wk_ref[...]).astype(jnp.bfloat16)
        v_ref[s, rows, :] = mxu(normed, wv_ref[...]).astype(jnp.bfloat16)

    for d in range(1, ways):
        x_copy(0, d).start()
    for s in range(seqs):
        project(s, span(me, shard), x_ref[s])
        for d in range(1, ways):
            x_copy(s, d).wait_recv()
            if d == ways - 1 and s + 1 < seqs:
                for later in range(1, ways):
                    x_copy(s + 1, later).start()
            rows = span(origin[d], shard)
            project(s, rows, x_all[s, rows, :])
        mixed_f[...] = jnp.zeros_like(mixed_f)
        log_s[...] = jnp.zeros_like(log_s)

        def one_head(h, carry):
            mine = (lane == h).astype(jnp.float32)
            for at in range(0, seq_len, BLOCK):
                rows = slice(at, at + BLOCK)
                query = (q_ref[s, rows, :].astype(jnp.float32) * (mine * scale)).astype(
                    jnp.bfloat16
                )
                near = mxu(query, k_ref[s, rows, :], ROWS_BY_ROWS)
                near = jnp.where(visible, near, -1e30)
                top = jnp.max(near, axis=1, keepdims=True)
                if at:
                    far = mxu(query, k_ref[s, :at, :], ROWS_BY_ROWS)
                    top = jnp.maximum(top, jnp.max(far, axis=1, keepdims=True))
                near = jnp.exp(near - top)
                total = jnp.sum(near, axis=1, keepdims=True)
                if at:
                    far = jnp.exp(far - top)
                    total += jnp.sum(far, axis=1, keepdims=True)
                inverse = 1.0 / total
                out = mxu((near * inverse).astype(jnp.bfloat16), v_ref[s, rows, :])
                if at:
                    out += mxu((far * inverse).astype(jnp.bfloat16), v_ref[s, :at, :])
                mixed_f[rows, :] += out * mine
                log_s[rows, :] = jnp.where(log_lane == h, top + jnp.log(total), log_s[rows, :])
            return carry

        lax.fori_loop(0, heads, one_head, 0)
        log_ref[s] = jnp.transpose(log_s[...])[: log_ref.shape[1], :]
        mixed_h[s] = mixed_f[...].astype(jnp.bfloat16)
        for d in range(1, ways):
            mixed_copy(s, d).start()
        mixed_ref[s, :, span(me, width)] = mixed_h[s, span(me, shard), :]
    for s in range(seqs):
        for d in range(1, ways):
            x_copy(s, d).wait_send()
            mixed_copy(s, d).wait()


def attend_backward(
    ways,
    head_dim,
    dmixed_ref,
    q_ref,
    k_ref,
    v_ref,
    log_ref,
    dq_ref,
    dk_ref,
    dv_ref,
    dq_tok,
    dk_tok,
    dv_tok,
    dmixed_h,
    dq_f,
    dk_f,
    dv_f,
    m_send,
    m_recv,
    g_send,
    g_recv,
):
    seqs, shard, _ = dmixed_ref.shape
    seq_len, width = q_ref.shape[1:]
    heads = width // head_dim
    me = lax.axis_index("sp")
    peer = [lax.rem(me + d, ways) for d in range(ways)]
    greet([{"sp": peer[d]} for d in range(1, ways)])

    def dmixed_copy(s, d):
        return send(
            dmixed_ref.at[s, :, span(peer[d], width)],
            dmixed_h.at[s, span(me, shard)],
            m_send.at[s, d],
            m_recv.at[s, d],
            {"sp": peer[d]},
        )

    pairs = ((dq_ref, dq_tok), (dk_ref, dk_tok), (dv_ref, dv_tok))

    def grad_copy(i, s, d):
        source, target = pairs[i]
        return send(
            source.at[s, span(peer[d], shard)],
            target.at[s, :, span(me, width)],
            g_send.at[i, s, d],
            g_recv.at[i, s, d],
            {"sp": peer[d]},
        )

    for s in range(seqs):
        for d in range(1, ways):
            dmixed_copy(s, d).start()
    lane = lax.broadcasted_iota(jnp.int32, (1, width), 1) // head_dim
    visible = lax.broadcasted_iota(jnp.int32, (BLOCK, BLOCK), 0) <= lax.broadcasted_iota(
        jnp.int32, (BLOCK, BLOCK), 1
    )
    scale = head_dim ** (-0.5)
    for s in range(seqs):
        dmixed_h[s, span(me, shard), :] = dmixed_ref[s, :, span(me, width)]
        for d in range(1, ways):
            dmixed_copy(s, d).wait_recv()
        dq_f[...] = jnp.zeros_like(dq_f)
        dk_f[...] = jnp.zeros_like(dk_f)
        dv_f[...] = jnp.zeros_like(dv_f)

        def one_head(h, carry):
            mine = (lane == h).astype(jnp.float32)
            for at in range(0, seq_len, BLOCK):
                rows = slice(at, at + BLOCK)
                query = (q_ref[s, rows, :].astype(jnp.float32) * (mine * scale)).astype(
                    jnp.bfloat16
                )
                dout = (dmixed_h[s, rows, :].astype(jnp.float32) * mine).astype(jnp.bfloat16)
                log_row = log_ref[s, pl.ds(h, 1), rows]
                parts = [(rows, True)] + ([(slice(0, at), False)] if at else [])
                kept = []
                delta = jnp.zeros((1, BLOCK), jnp.float32)
                for keys, diagonal in parts:
                    prob = jnp.exp(mxu(k_ref[s, keys, :], query, ROWS_BY_ROWS) - log_row)
                    if diagonal:
                        prob = jnp.where(visible, prob, 0.0)
                    dprob = mxu(v_ref[s, keys, :], dout, ROWS_BY_ROWS)
                    delta += jnp.sum(prob * dprob, axis=0, keepdims=True)
                    kept.append((keys, prob, dprob))
                dquery = jnp.zeros((BLOCK, width), jnp.float32)
                for keys, prob, dprob in kept:
                    dv_f[keys, :] += mxu(prob.astype(jnp.bfloat16), dout)
                    dlogit = (prob * (dprob - delta)).astype(jnp.bfloat16)
                    dk_f[keys, :] += mxu(dlogit, query)
                    dquery += mxu(dlogit, k_ref[s, keys, :], COLS_BY_COLS)
                dq_f[rows, :] += dquery * (mine * scale)
            return carry

        lax.fori_loop(0, heads, one_head, 0)
        for i, total in enumerate((dq_f, dk_f, dv_f)):
            source, target = pairs[i]
            source[s] = total[...].astype(jnp.bfloat16)
            for d in range(1, ways):
                grad_copy(i, s, d).start()
            target[s, :, span(me, width)] = source[s, span(me, shard), :]
    for s in range(seqs):
        for d in range(1, ways):
            dmixed_copy(s, d).wait_send()
            for i in range(3):
                grad_copy(i, s, d).wait()


def reduce_everywhere(
    ways,
    columns,
    part_ref,
    small_ref,
    out_ref,
    small_out,
    core_land,
    core_sum,
    column_land,
    piece,
    small_land,
    small_sum,
    core_send,
    core_recv,
    column_send,
    column_recv,
    spread_send,
    spread_recv,
    ring_send,
    ring_recv,
    cross_send,
    cross_recv,
    small_send,
    small_recv,
    local_sem,
):
    rows = part_ref.shape[2]
    width = part_ref.shape[3]
    me = lax.axis_index("sp")
    dp = lax.axis_index("dp")
    core = lax.rem(dp, 2)
    column = dp // 2
    twin = {"dp": dp + 1 - 2 * core}
    column_peer = [lax.rem(column + d, columns) for d in range(columns)]
    sp_peer = [lax.rem(me + d, ways) for d in range(ways)]
    sp_origin = [lax.rem(me + ways - d, ways) for d in range(ways)]
    column_id = [{"dp": 2 * column_peer[d] + core} for d in range(columns)]
    sp_id = [{"sp": sp_peer[d]} for d in range(ways)]
    greet([twin] + column_id[1:] + sp_id[1:])

    first = send(part_ref.at[1 - core], core_land, core_send, core_recv, twin)
    first.start()
    small_first = send(small_ref, small_land.at[0], small_send.at[0], small_recv.at[0], twin)
    small_first.start()
    small_first.wait()
    small_sum[0] = small_ref[...] + small_land[0]

    def small_column(d):
        return send(
            small_sum.at[0],
            small_land.at[d],
            small_send.at[d],
            small_recv.at[d],
            column_id[d],
        )

    def small_ring(d):
        at = columns + d
        return send(
            small_sum.at[1],
            small_land.at[at],
            small_send.at[at],
            small_recv.at[at],
            sp_id[d],
        )

    for d in range(1, columns):
        small_column(d).start()
    first.wait()
    core_sum[...] = (
        part_ref[core].astype(jnp.float32) + core_land[...].astype(jnp.float32)
    ).astype(jnp.bfloat16)

    def column_copy(d):
        return send(
            core_sum.at[column_peer[d]],
            column_land.at[d],
            column_send.at[d],
            column_recv.at[d],
            column_id[d],
        )

    for d in range(1, columns):
        column_copy(d).start()
    for d in range(1, columns):
        small_column(d).wait()
    total = small_sum[0]
    for d in range(1, columns):
        total += small_land[d]
    small_sum[1] = total
    for d in range(1, ways):
        small_ring(d).start()
    total = core_sum[column].astype(jnp.float32)
    for d in range(1, columns):
        column_copy(d).wait()
        total += column_land[d].astype(jnp.float32)
    piece[...] = total.astype(jnp.bfloat16)

    def block(at_core, at_column, at_sp, count=1):
        first_row = pl.multiple_of((at_core * columns + at_column) * rows, rows)
        return out_ref.at[pl.ds(first_row, count * rows), span(at_sp, width)]

    def spread_copy(d):
        return send(
            piece,
            block(core, column, me),
            spread_send.at[d],
            spread_recv.at[d],
            column_id[d],
        )

    for d in range(1, columns):
        spread_copy(d).start()
    own = pltpu.make_async_copy(piece, block(core, column, me), local_sem)
    own.start()
    for d in range(1, ways):
        small_ring(d).wait()
    total = small_sum[1]
    for d in range(1, ways):
        total += small_land[columns + d]
    small_out[...] = total
    own.wait()
    for d in range(1, columns):
        spread_copy(d).wait()

    def ring_copy(d):
        half = block(core, 0, me, columns)
        return send(half, half, ring_send.at[d], ring_recv.at[d], sp_id[d])

    def cross_copy(d):
        half = block(core, 0, sp_origin[d], columns)
        return send(half, half, cross_send.at[d], cross_recv.at[d], twin)

    for d in range(1, ways):
        ring_copy(d).start()
    cross_copy(0).start()
    for d in range(1, ways):
        ring_copy(d).wait_recv()
        cross_copy(d).start()
    for d in range(1, ways):
        ring_copy(d).wait_send()
    for d in range(ways):
        cross_copy(d).wait()


def vmem(count):
    return [pl.BlockSpec(memory_space=pltpu.VMEM)] * count


def params(collective_id):
    return pltpu.CompilerParams(
        collective_id=collective_id, has_side_effects=True, vmem_limit_bytes=VMEM_BYTES
    )


def dma(*shape):
    return pltpu.SemaphoreType.DMA(shape)


def local(
    tokens_in,
    expert_ids,
    query_weight,
    key_weight,
    value_weight,
    out_weight,
    norm1_gain,
    norm1_shift,
    norm2_gain,
    norm2_shift,
    up_weight,
    down_weight,
    out_cotangent,
    load_mean,
):
    seq_count, shard_len, model_width = tokens_in.shape
    row_count = seq_count * shard_len
    head_dim = model_width // HEADS
    dp_ways = lax.axis_size("dp")
    sp_ways = lax.axis_size("sp")
    sp_at = lax.axis_index("sp")
    seq_len = shard_len * sp_ways
    experts = load_mean.shape[0]
    slot_count = 2 * row_count // experts
    local_experts = up_weight.shape[0]
    ff_width = up_weight.shape[1]
    width = model_width // sp_ways
    bf16 = jnp.bfloat16
    f32 = jnp.float32

    def shape(*sizes, dtype=bf16):
        return jax.ShapeDtypeStruct(sizes, dtype)

    routes = expert_ids.reshape(row_count)
    one_hot = (routes[:, None] == jnp.arange(experts, dtype=jnp.int32)[None, :]).astype(jnp.int32)
    running = jnp.cumsum(one_hot, axis=0) - 1
    slot_of = jnp.sum(running * one_hot, axis=1)
    target = routes * slot_count + slot_of
    placer = (jnp.arange(experts * slot_count, dtype=jnp.int32)[:, None] == target[None, :]).astype(
        bf16
    )
    cot_b = out_cotangent.reshape(row_count, model_width)
    cot_send = jnp.dot(placer, cot_b, preferred_element_type=f32).astype(bf16)
    cot_send = cot_send.reshape(experts, slot_count, model_width)
    arrived = lax.all_to_all(cot_send, "dp", split_axis=0, concat_axis=0, tiled=True)

    def columns_of(weight):
        return lax.dynamic_slice_in_dim(weight, sp_at * width, width, axis=1)

    normed_all, query_h, key_h, value_h, log_total, mixed_b = pl.pallas_call(
        functools.partial(attend_forward, sp_ways, head_dim),
        out_shape=[
            shape(seq_count, seq_len, model_width),
            shape(seq_count, seq_len, width),
            shape(seq_count, seq_len, width),
            shape(seq_count, seq_len, width),
            shape(seq_count, 8, seq_len, dtype=f32),
            shape(seq_count, shard_len, model_width),
        ],
        in_specs=vmem(6),
        out_specs=vmem(6),
        scratch_shapes=[
            pltpu.VMEM((seq_count, seq_len, model_width), bf16),
            pltpu.VMEM((seq_len, width), f32),
            pltpu.VMEM((seq_count, seq_len, width), bf16),
            pltpu.VMEM((seq_len, LANES), f32),
            dma(seq_count, sp_ways),
            dma(seq_count, sp_ways),
            dma(seq_count, sp_ways),
            dma(seq_count, sp_ways),
        ],
        compiler_params=params(0),
    )(
        tokens_in,
        columns_of(query_weight),
        columns_of(key_weight),
        columns_of(value_weight),
        norm1_gain.reshape(1, model_width),
        norm1_shift.reshape(1, model_width),
    )
    mixed_b = mixed_b.reshape(row_count, model_width)
    inputs = tokens_in.reshape(row_count, model_width).astype(f32)
    attn_out = jnp.dot(mixed_b, out_weight, preferred_element_type=f32)
    residual_stream = inputs + attn_out
    normed2, unit2, rstd2 = norm_forward(residual_stream, norm2_gain, norm2_shift)
    normed2_b = normed2.astype(bf16)
    outgoing = jnp.dot(placer, normed2_b, preferred_element_type=f32).astype(bf16)
    outgoing = outgoing.reshape(experts, slot_count, model_width)
    received = lax.all_to_all(outgoing, "dp", split_axis=0, concat_axis=0, tiled=True)
    parts = received.reshape(-1, local_experts, slot_count, model_width)
    pre_act = jnp.einsum("sxcd,xfd->sxcf", parts, up_weight, preferred_element_type=f32)
    hidden_b = smooth(pre_act).astype(bf16)
    arrived_p = arrived.reshape(-1, local_experts, slot_count, model_width)
    dhidden = jnp.einsum("sxcd,xfd->sxcf", arrived_p, down_weight, preferred_element_type=f32)
    dpre_b = (dhidden * smooth_slope(pre_act)).astype(bf16)
    dnormed_send = jnp.einsum("sxcf,xfd->sxcd", dpre_b, up_weight, preferred_element_type=f32)
    dnormed_send = dnormed_send.astype(bf16).reshape(-1, slot_count, model_width)
    dnormed_back = lax.all_to_all(dnormed_send, "dp", split_axis=0, concat_axis=0, tiled=True)
    expert_out = jnp.einsum("sxcf,xfd->sxcd", hidden_b, down_weight, preferred_element_type=f32)
    expert_out = expert_out.astype(bf16).reshape(received.shape)
    returned = lax.all_to_all(expert_out, "dp", split_axis=0, concat_axis=0, tiled=True)
    expert_rows = jnp.einsum(
        "er,ed->rd",
        placer,
        returned.reshape(experts * slot_count, model_width),
        preferred_element_type=f32,
    )
    block_out = (residual_stream + expert_rows).astype(bf16)
    block_out = block_out.reshape(seq_count, shard_len, model_width)
    up_full = jnp.einsum("sxcf,sxcd->xfd", dpre_b, parts, preferred_element_type=f32)
    down_full = jnp.einsum("sxcf,sxcd->xfd", hidden_b, arrived_p, preferred_element_type=f32)
    up_grad, down_grad = (
        lax.psum_scatter(grad.astype(bf16), "sp", scatter_dimension=1, tiled=True).astype(f32)
        for grad in (up_full, down_full)
    )
    dnormed2 = jnp.einsum(
        "er,ed->rd",
        placer,
        dnormed_back.reshape(experts * slot_count, model_width),
        preferred_element_type=f32,
    )
    dresid_norm, gain_two_grad, shift_two_grad = norm_backward(dnormed2, unit2, rstd2, norm2_gain)
    dresid = cot_b.astype(f32) + dresid_norm
    dattn_b = dresid.astype(bf16)
    dmixed_b = jnp.einsum("re,de->rd", dattn_b, out_weight, preferred_element_type=f32)
    dmixed_b = dmixed_b.astype(bf16).reshape(seq_count, shard_len, model_width)
    out_grad = jnp.einsum("rd,re->de", mixed_b, dattn_b, preferred_element_type=f32).astype(bf16)
    out_part = lax.psum_scatter(out_grad, "sp", scatter_dimension=1, tiled=True)
    grads = pl.pallas_call(
        functools.partial(attend_backward, sp_ways, head_dim),
        out_shape=[shape(seq_count, seq_len, width)] * 3
        + [shape(seq_count, shard_len, model_width)] * 3,
        in_specs=vmem(5),
        out_specs=vmem(6),
        scratch_shapes=[
            pltpu.VMEM((seq_count, seq_len, width), bf16),
            pltpu.VMEM((seq_len, width), f32),
            pltpu.VMEM((seq_len, width), f32),
            pltpu.VMEM((seq_len, width), f32),
            dma(seq_count, sp_ways),
            dma(seq_count, sp_ways),
            dma(3, seq_count, sp_ways),
            dma(3, seq_count, sp_ways),
        ],
        compiler_params=params(1),
    )(dmixed_b, query_h, key_h, value_h, log_total)
    head_grads, token_grads = grads[:3], grads[3:]
    weight_parts = [
        jnp.einsum("skd,ske->de", normed_all, grad, preferred_element_type=f32).astype(bf16)
        for grad in head_grads
    ]
    dnormed1 = sum(
        jnp.einsum(
            "re,de->rd",
            grad.reshape(row_count, model_width),
            weight,
            preferred_element_type=f32,
        )
        for grad, weight in zip(token_grads, (query_weight, key_weight, value_weight))
    )
    _, unit1, rstd1 = norm_forward(inputs, norm1_gain, norm1_shift)
    dinput_norm, gain_one_grad, shift_one_grad = norm_backward(dnormed1, unit1, rstd1, norm1_gain)
    tokens_grad = (dresid + dinput_norm).astype(bf16)
    tokens_grad = tokens_grad.reshape(seq_count, shard_len, model_width)
    counts = jnp.sum(one_hot, axis=0).astype(f32)
    counts = jnp.pad(counts, (0, model_width - experts))
    small = jnp.stack(
        [gain_one_grad, shift_one_grad, gain_two_grad, shift_two_grad, counts]
        + [jnp.zeros((model_width,), f32)] * 3
    )
    columns = dp_ways // 2
    piece_rows = 4 * model_width // dp_ways
    packed = jnp.concatenate(weight_parts + [out_part], axis=0)
    packed = packed.reshape(2, columns, piece_rows, width)
    gathered, small_sum = pl.pallas_call(
        functools.partial(reduce_everywhere, sp_ways, columns),
        out_shape=[
            shape(4 * model_width, model_width),
            shape(8, model_width, dtype=f32),
        ],
        in_specs=vmem(2),
        out_specs=[pl.BlockSpec(memory_space=pl.ANY), pl.BlockSpec(memory_space=pltpu.VMEM)],
        scratch_shapes=[
            pltpu.VMEM((columns, piece_rows, width), bf16),
            pltpu.VMEM((columns, piece_rows, width), bf16),
            pltpu.VMEM((columns, piece_rows, width), bf16),
            pltpu.VMEM((piece_rows, width), bf16),
            pltpu.VMEM((columns + sp_ways, 8, model_width), f32),
            pltpu.VMEM((2, 8, model_width), f32),
            pltpu.SemaphoreType.DMA,
            pltpu.SemaphoreType.DMA,
            dma(columns),
            dma(columns),
            dma(columns),
            dma(columns),
            dma(sp_ways),
            dma(sp_ways),
            dma(sp_ways),
            dma(sp_ways),
            dma(columns + sp_ways),
            dma(columns + sp_ways),
            pltpu.SemaphoreType.DMA,
        ],
        compiler_params=params(2),
    )(packed, small)
    query_grad, key_grad, value_grad, out_grad = (
        gathered[i * model_width : (i + 1) * model_width].astype(f32) for i in range(4)
    )
    load_now = small_sum[4, :experts] * experts / (row_count * dp_ways * sp_ways)
    load_next = 0.9 * load_mean + 0.1 * load_now
    return (
        block_out,
        tokens_grad,
        query_grad,
        key_grad,
        value_grad,
        out_grad,
        small_sum[0],
        small_sum[1],
        small_sum[2],
        small_sum[3],
        up_grad,
        down_grad,
        load_next,
    )


def solution(mesh):
    return jax.shard_map(
        local,
        mesh=mesh,
        in_specs=(
            P("dp", "sp", None),
            P("dp", "sp", None, None),
            P(),
            P(),
            P(),
            P(),
            P(),
            P(),
            P(),
            P(),
            P("dp", None, None),
            P("dp", None, None),
            P("dp", "sp", None),
            P(),
        ),
        out_specs=(
            P("dp", "sp", None),
            P("dp", "sp", None),
            P(),
            P(),
            P(),
            P(),
            P(),
            P(),
            P(),
            P(),
            P("dp", "sp", None),
            P("dp", "sp", None),
            P(),
        ),
        check_vma=False,
    )
```

time: 1060 us -> 642 us (0.61)
  waiting for transfers between devices: 577 us -> 72.5 us
  Pallas kernels: 0 us -> 285 us
  matrix products: 255 us -> 144 us
  local copies, waits for them, and re-layouts: 66.8 us -> 10.1 us
  other arithmetic: 71 us -> 32.2 us
    pallas_call x0 -> x3, Pallas kernels: none -> 285 us  [the longest x1 132 us: local(): pl.pallas_call(functools.partial(reduce_everywhere, sp_ways, columns), ou...]
    psum x1 -> x0, waiting for transfers between devices: 231 us -> none  [local(): lax.psum((query_grad, key_grad, value_grad, out_grad, gain_one_grad, shif...]
    reduce_scatter x4 -> x3, waiting for transfers between devices: 132 us -> 0.01 us  [the longest x2 0.01 us: local(): lax.psum_scatter(grad.astype(bf16), 'sp', scatter_dimension=1, tiled=True)]
    dot_general x24 -> x15, matrix products: 204 us -> 96.7 us  [the longest x1 22.2 us: local(): jnp.einsum('sxcf,xfd->sxcd', dpre_b, up_weight, preferred_element_type=f32)]
    all_to_all x2 -> x1, waiting for transfers between devices: 86.3 us -> 0.01 us  [local(): lax.all_to_all(expert_out, 'dp', split_axis=0, concat_axis=0, tiled=True)]
    all_gather x2 -> x0, waiting for transfers between devices: 54.3 us -> none  [the longest x1 36.2 us: local(): lax.all_gather(key_local, 'sp', axis=1, tiled=True)]
    all_to_all x0 -> x1, blocking collectives: none -> 52.2 us  [local(): lax.all_to_all(dnormed_send, 'dp', split_axis=0, concat_axis=0, tiled=True)]
    psum x1 -> x0, blocking collectives: 42.1 us -> none  [local(): lax.psum((query_grad, key_grad, value_grad, out_grad, gain_one_grad, shif...]
  transfers between devices with their start and end apart: 11 -> 6, of which waited for: 10 -> 2; matrix products, arithmetic and copies ran while one was open for 25% -> 18% of each run, Pallas kernels for 0% -> 33%
where the time goes in v1:
time: 642 us; the launch traced here: 632 us
  Pallas kernels  285 us (44%)
  matrix products  144 us (22%)
  waiting for transfers between devices  72.5 us (11%)
  blocking collectives  52.2 us (8%)
  other arithmetic  32.2 us (5%)
  starting transfers between devices  21.6 us (3%)
  between operations  14.3 us (2%)
  local copies, waits for them, and re-layouts  10.1 us (2%)
    pallas_call x1, Pallas kernels, local(): pl.pallas_call(functools.partial(reduce_everywhere, sp_ways, columns), ou...  132 us
    pallas_call x1, Pallas kernels, local(): pl.pallas_call(functools.partial(attend_backward, sp_ways, head_dim), out...  79.9 us
    pallas_call x1, Pallas kernels, local(): pl.pallas_call(functools.partial(attend_forward, sp_ways, head_dim), out_...  73.5 us
    all_to_all x1, blocking collectives, local(): lax.all_to_all(dnormed_send, 'dp', split_axis=0, concat_axis=0, tiled=True)  52.2 us
    all_to_all x1, waiting for transfers between devices, local(): lax.all_to_all(outgoing, 'dp', split_axis=0, concat_axis=0, tiled=True)  42.9 us
    all_to_all x1, waiting for transfers between devices, local(): lax.all_to_all(cot_send, 'dp', split_axis=0, concat_axis=0, tiled=True)  29.5 us
    dot_general x1, matrix products, local(): jnp.einsum('sxcd,xfd->sxcf', arrived_p, down_weight, preferred_element_ty...  23.8 us
    dot_general x1, matrix products, local(): jnp.einsum('sxcf,xfd->sxcd', dpre_b, up_weight, preferred_element_type=f32)  22.2 us
  transfers between devices with their start and end apart: 6, of which 2 were waited for; matrix products, arithmetic and copies ran while one was open for 18% of the time, Pallas kernels for 33%

profile of v1, /device:TPU:9, one launch (start us, length us, event | category | flops | bytes accessed | tf_op | source)
XLA Modules:
  0.0 632.1 jit_solution(7343292953223588996)
XLA Ops:
  15.7 73.5 %shard_map.237 = (bf16[2,1024,1024]{2,1,0:T(8,128)(2,1)}, bf16[2,1024,256]{2,1,0:T(8,128)(2,1)}, bf16[2,1024,256]{2,1,0:T(8,128)(2,1)}, bf16[2,1024,256]{2,1,0:T...) custom-call(bf16[2,256,1024]{2,1,0:T(8,128)(2,1)} %x_ref.1, ...), custom_call_target="tpu_custom_call" | custom-call | tf_op jit(solution)/shard_map/pallas_call | solution.py:520
  92.6 2.8 fusion.45
  95.4 5.7 all-to-all-start
  103.7 42.9 %all-to-all-done = bf16[8,128,1024]{2,1,0:T(8,128)(2,1)} async-done(((bf16[8,128,1024]{2,1,0:T(8,128)(2,1)}), bf16[8,128,1024]{2,1,0:T(8,128)(2,1)}, u32[]{:S(2)}, u32[]{:S(2)}) %all-to-all-start) | async-done | bytes 2097184 | tf_op jit(solution)/shard_map/all_to_all | solution.py:559
  146.6 7.9 %all-to-all-start.2 = ((bf16[8,128,1024]{2,1,0:T(8,128)(2,1)}), bf16[8,128,1024]{2,1,0:T(8,128)(2,1)}, u32[]{:S(2)}, u32[]{:S(2)}) async-start(bf16[8,128,1024]{2,1,0:T(8,128)(2,1)} %bitcast.176), calls=%async_computation.2 | async-start | bytes 4194304 | tf_op jit(solution)/shard_map/all_to_all | solution.py:515
  154.5 16.0 %fusion.16 = f32[8,128,4096]{2,1,0:T(8,128)} fusion(bf16[8,128,1024]{2,1,0:T(8,128)(2,1)} %all-to-all-done, bf16[1,4096,1024]{2,1,0:T(8,128)(2,1)} %param.24), kind=kOutput, calls=%fused_computation.22 | convolution fusion | flops 8589934592 | bytes 27262976 | tf_op jit(solution)/shard_map/sxcd,xfd->sxcf/dot_general | solution.py:561
  170.6 29.5 %all-to-all-done.2 = bf16[8,128,1024]{2,1,0:T(8,128)(2,1)} async-done(((bf16[8,128,1024]{2,1,0:T(8,128)(2,1)}), bf16[8,128,1024]{2,1,0:T(8,128)(2,1)}, u32[]{:S(2)}, u32[]{:S(2)}) %all-to-all-start.2) | async-done | bytes 2097184 | tf_op jit(solution)/shard_map/all_to_all | solution.py:515
  200.0 23.8 %fusion.6 = bf16[8,1,128,4096]{3,2,0,1:T(8,128)(2,1)} fusion(f32[8,128,4096]{2,1,0:T(8,128)} %fusion.16, bf16[8,128,1024]{2,1,0:T(8,128)(2,1)} %all-to-all-done.2, bf16[1,4096,1024]{2,1,0:T(8,128)(2,1)} %param.25), kind=kOutput, calls=%fused_computation.8 | convolution fusion | flops 8669626368 | bytes 35651584 | tf_op jit(solution)/shard_map/sxcd,xfd->sxcf/dot_general | solution.py:564
  223.8 22.2 %fusion.47 = bf16[8,128,1024]{2,1,0:T(8,128)(2,1)S(1)} fusion(bf16[1,4096,1024]{2,1,0:T(8,128)(2,1)} %param.24, bf16[8,1,128,4096]{3,2,0,1:T(8,128)(2,1)} %fusion.6), kind=kOutput, calls=%fused_computation.64 | convolution fusion | flops 8590983168 | bytes 18874368 | tf_op jit(solution)/shard_map/sxcf,xfd->sxcd/dot_general | solution.py:566
  246.0 52.2 %all_to_all.20 = bf16[8,128,1024]{2,1,0:T(8,128)(2,1)S(1)} all-to-all(bf16[8,128,1024]{2,1,0:T(8,128)(2,1)S(1)} %fusion.47), channel_id=1, replica_groups=mesh['dp'=8,'sp'=4] {'dp'}, dimensions={0} | all-to-all | bytes 4194304 | tf_op jit(solution)/shard_map/all_to_all | solution.py:568
  304.9 17.8 %fusion.21 = bf16[1,4096,1024]{2,1,0:T(8,128)(2,1)} fusion(bf16[8,128,1024]{2,1,0:T(8,128)(2,1)} %all-to-all-done.2, f32[8,128,4096]{2,1,0:T(8,128)} %fusion.16), kind=kOutput, calls=%fused_computation.25 | convolution fusion | flops 8631877632 | bytes 27262976 | tf_op jit(solution)/shard_map/sxcf,sxcd->xfd/dot_general | solution.py:581
  322.8 15.2 %fusion.18 = bf16[1,4096,1024]{2,1,0:T(8,128)(2,1)} fusion(bf16[8,128,1024]{2,1,0:T(8,128)(2,1)} %all-to-all-done, bf16[8,1,128,4096]{3,2,0,1:T(8,128)(2,1)} %fusion.6), kind=kOutput, calls=%fused_computation.24 | convolution fusion | flops 8594128896 | bytes 18874368 | tf_op jit(solution)/shard_map/sxcf,sxcd->xfd/dot_general | solution.py:580
  338.1 17.1 %fusion.40 = bf16[8,128,1024]{2,1,0:T(8,128)(2,1)} fusion(bf16[1,4096,1024]{2,1,0:T(8,128)(2,1)} %param.25, f32[8,128,4096]{2,1,0:T(8,128)} %fusion.16), kind=kOutput, calls=%fused_computation.60 | convolution fusion | flops 8628731904 | bytes 27262976 | tf_op jit(solution)/shard_map/sxcf,xfd->sxcd/dot_general | solution.py:569
  355.2 7.9 %all-to-all-start.1 = ((bf16[8,128,1024]{2,1,0:T(8,128)(2,1)}), bf16[8,128,1024]{2,1,0:T(8,128)(2,1)}, u32[]{:S(2)}, u32[]{:S(2)}) async-start(bf16[8,128,1024]{2,1,0:T(8,128)(2,1)} %fusion.40), calls=%async_computation.1 | async-start | bytes 4194304 | tf_op jit(solution)/shard_map/all_to_all | solution.py:571
  367.2 79.9 %shard_map.238 = (bf16[2,1024,256]{2,1,0:T(8,128)(2,1)}, bf16[2,1024,256]{2,1,0:T(8,128)(2,1)}, bf16[2,1024,256]{2,1,0:T(8,128)(2,1)}, bf16[2,256,1024]{2,1,0:T(...) custom-call(bf16[2,256,1024]{2,1,0:T(8,128)(2,1)} %bitcast.181, ...), custom_call_target="tpu_custom_call" | custom-call | tf_op jit(solution)/shard_map/pallas_call | solution.py:599
  447.1 3.3 fusion.79
  452.4 3.2 fusion.35
  456.3 4.2 fusion.34
  460.4 4.6 add_convert_fusion
  469.8 2.7 pad_maximum_fusion
  472.5 131.8 %shard_map.239 = (bf16[4096,1024]{1,0:T(8,128)(2,1)}, f32[8,1024]{1,0:T(8,128)}) custom-call(bf16[2,4,512,256]{3,2,1,0:T(8,128)(2,1)} %bitcast.175, f32[8,1024]{1,0:T(8,128)} %stack.27.small_ref), custom_call_target="tpu_custom_call" | custom-call | tf_op jit(solution)/shard_map/pallas_call | solution.py:645
  607.1 10.2 %slice_convert_fusion = (f32[1024,1024]{1,0:T(8,128)}, f32[1024,1024]{1,0:T(8,128)}, f32[1024,1024]{1,0:T(8,128)}, f32[1024,1024]{1,0:T(8,128)}) fusion(bf16[4096,1024]{1,0:T(8,128)(2,1)} %get-tuple-element.39), kind=kLoop, calls=%fused_computation.43 | loop fusion | flops 4194304 | bytes 25165824 | tf_op jit(solution)/shard_map/convert_element_type | solution.py:677
  617.2 4.1 convert_element_type.138
  621.3 4.1 convert_element_type.135
  (93 shorter events, 35.2 us)
Async XLA Ops:
  7.2 82.1 %copy-start = (bf16[1024,1024]{1,0:T(8,128)(2,1)S(1)}, bf16[1024,1024]{1,0:T(8,128)(2,1)}, u32[]{:S(2)}) copy-start(bf16[1024,1024]{1,0:T(8,128)(2,1)} %param.19) | copy-start | bytes 6291460
  13.4 75.9 %copy-start.1 = (bf16[2,256,1024]{2,1,0:T(8,128)(2,1)S(1)}, bf16[2,256,1024]{2,1,0:T(8,128)(2,1)}, u32[]{:S(2)}) copy-start(bf16[2,256,1024]{2,1,0:T(8,128)(2,1)} %x_ref.1) | copy-start | bytes 3145732
  91.8 3.6 copy-start.3
  95.4 5.7 copy-start.7
  95.4 51.2 %all-to-all-start = ((bf16[8,128,1024]{2,1,0:T(8,128)(2,1)}), bf16[8,128,1024]{2,1,0:T(8,128)(2,1)}, u32[]{:S(2)}, u32[]{:S(2)}) async-start(bf16[8,128,1024]{2,1,0:T(8,128)(2,1)} %bitcast.178), calls=%async_computation | async-start | bytes 4194304 | tf_op jit(solution)/shard_map/all_to_all | solution.py:559
  146.6 53.4 %all-to-all-start.2 = ((bf16[8,128,1024]{2,1,0:T(8,128)(2,1)}), bf16[8,128,1024]{2,1,0:T(8,128)(2,1)}, u32[]{:S(2)}, u32[]{:S(2)}) async-start(bf16[8,128,1024]{2,1,0:T(8,128)(2,1)} %bitcast.176), calls=%async_computation.2 | async-start | bytes 4194304 | tf_op jit(solution)/shard_map/all_to_all | solution.py:515
  154.5 315.3 %reduce-scatter.4.cloned.1.call-start = ((), (), s32[]{:S(2)}) async-start(), calls=%async_computation.7 | async-start | bytes 2621440 | tf_op jit(solution)/shard_map/reduce_scatter | solution.py:598
  246.0 52.2 %copy-start.4 = (f32[512,1024]{1,0:T(8,128)S(1)}, f32[512,1024]{1,0:T(8,128)}, u32[]{:S(2)}) copy-start(f32[512,1024]{1,0:T(8,128)} %copy-done.3) | copy-start | bytes 6291460
  300.1 2.2 copy-start.14
  300.9 1.3 copy-start.5
  304.9 312.4 %reduce-scatter.8.cloned.1.call-start = ((), (), s32[]{:S(2)}) async-start(), calls=%async_computation.9 | async-start | bytes 10485760 | tf_op jit(solution)/shard_map/reduce_scatter | solution.py:583
  322.8 298.5 %reduce-scatter.6.cloned.1.call-start = ((), (), s32[]{:S(2)}) async-start(), calls=%async_computation.8 | async-start | bytes 10485760 | tf_op jit(solution)/shard_map/reduce_scatter | solution.py:583
  355.2 7.9 %copy-start.2 = (bf16[2,256,1024]{2,1,0:T(8,128)(2,1)S(1)}, bf16[2,256,1024]{2,1,0:T(8,128)(2,1)}, u32[]{:S(2)}) copy-start(bf16[2,256,1024]{2,1,0:T(8,128)(2,1)} %x_ref.1) | copy-start | bytes 3145732
  355.2 105.2 %all-to-all-start.1 = ((bf16[8,128,1024]{2,1,0:T(8,128)(2,1)}), bf16[8,128,1024]{2,1,0:T(8,128)(2,1)}, u32[]{:S(2)}, u32[]{:S(2)}) async-start(bf16[8,128,1024]{2,1,0:T(8,128)(2,1)} %fusion.40), calls=%async_computation.1 | async-start | bytes 4194304 | tf_op jit(solution)/shard_map/all_to_all | solution.py:571
  363.1 1.8 copy-start.6
  447.1 3.4 copy-start.9
  447.1 3.4 copy-start.19
  450.5 1.6 copy-start.8
  450.5 1.6 copy-start.10
  450.5 1.9 copy-start.18
  460.4 4.7 copy-start.13
  460.4 4.7 copy-start.17
  466.4 1.3 copy-start.15
  472.5 131.9 %copy-start.21 = (f32[8]{0:T(128)S(1)}, f32[8]{0:T(128)}, u32[]{:S(2)}) copy-start(f32[8]{0:T(128)} %param.27) | copy-start | bytes 100
  (4 other events, 3.4 us)
Sparse Core Ops, SparseCore 0:
  305.0 37.1 reduce-scatter.3
  345.6 123.4 reduce-scatter.7
  472.1 128.0 reduce-scatter.5

commit v2 on v1

--- a/solution.py
+++ b/solution.py
@@ -11,6 +11,9 @@
 MESH = pl.DeviceIdType.MESH
 BLOCK = 256
 LANES = 128
+STEP = 512
+ALONG_X = [(0, 1), (1, 0), (2, 3), (3, 2)]
+ALONG_Y = [(0, 2), (2, 0), (1, 3), (3, 1)]
 VMEM_BYTES = 60 * 2**20
 
 NORM_EPSILON = 1e-05
@@ -81,9 +84,34 @@
     )
 
 
+def exchange(others, source, target, send_sem, recv_sem):
+    me = lax.axis_index("dp")
+    return [
+        send(
+            source.at[flip(me, d)],
+            target.at[me],
+            send_sem.at[d],
+            recv_sem.at[d],
+            {"dp": flip(me, d)},
+        )
+        for d in range(1, others)
+    ]
+
+
+def flip(index, bits):
+    bit = 1
+    while bit <= bits:
+        if bits & bit:
+            index = index + bit - 2 * bit * lax.rem(index // bit, 2)
+        bit *= 2
+    return index
+
+
 def attend_forward(
     ways,
+    others,
     head_dim,
+    cot_ref,
     x_ref,
     wq_ref,
     wk_ref,
@@ -96,6 +124,7 @@
     v_ref,
     log_ref,
     mixed_ref,
+    arrived_ref,
     x_all,
     mixed_f,
     mixed_h,
@@ -104,6 +133,9 @@
     x_recv,
     m_send,
     m_recv,
+    c_send,
+    c_recv,
+    local_sem,
 ):
     seqs, shard, _ = x_ref.shape
     seq_len, width = q_ref.shape[1:]
@@ -111,7 +143,14 @@
     me = lax.axis_index("sp")
     peer = [lax.rem(me + d, ways) for d in range(ways)]
     origin = [lax.rem(me + ways - d, ways) for d in range(ways)]
-    greet([{"sp": peer[d]} for d in range(1, ways)])
+    greet(
+        [{"sp": peer[d]} for d in range(1, ways)]
+        + [{"dp": flip(lax.axis_index("dp"), d)} for d in range(1, others)]
+    )
+    background = exchange(others, cot_ref, arrived_ref, c_send, c_recv)
+    own = pltpu.make_async_copy(
+        cot_ref.at[lax.axis_index("dp")], arrived_ref.at[lax.axis_index("dp")], local_sem
+    )
 
     def x_copy(s, d):
         return send(
@@ -148,6 +187,9 @@
 
     for d in range(1, ways):
         x_copy(0, d).start()
+    own.start()
+    for copy in background:
+        copy.start()
     for s in range(seqs):
         project(s, span(me, shard), x_ref[s])
         for d in range(1, ways):
@@ -196,11 +238,16 @@
         for d in range(1, ways):
             x_copy(s, d).wait_send()
             mixed_copy(s, d).wait()
+    own.wait()
+    for copy in background:
+        copy.wait()
 
 
 def attend_backward(
     ways,
+    others,
     head_dim,
+    result_ref,
     dmixed_ref,
     q_ref,
     k_ref,
@@ -212,6 +259,7 @@
     dq_tok,
     dk_tok,
     dv_tok,
+    returned_ref,
     dmixed_h,
     dq_f,
     dk_f,
@@ -220,13 +268,23 @@
     m_recv,
     g_send,
     g_recv,
+    c_send,
+    c_recv,
+    local_sem,
 ):
     seqs, shard, _ = dmixed_ref.shape
     seq_len, width = q_ref.shape[1:]
     heads = width // head_dim
     me = lax.axis_index("sp")
     peer = [lax.rem(me + d, ways) for d in range(ways)]
-    greet([{"sp": peer[d]} for d in range(1, ways)])
+    greet(
+        [{"sp": peer[d]} for d in range(1, ways)]
+        + [{"dp": flip(lax.axis_index("dp"), d)} for d in range(1, others)]
+    )
+    background = exchange(others, result_ref, returned_ref, c_send, c_recv)
+    own = pltpu.make_async_copy(
+        result_ref.at[lax.axis_index("dp")], returned_ref.at[lax.axis_index("dp")], local_sem
+    )
 
     def dmixed_copy(s, d):
         return send(
@@ -252,6 +310,9 @@
     for s in range(seqs):
         for d in range(1, ways):
             dmixed_copy(s, d).start()
+    own.start()
+    for copy in background:
+        copy.start()
     lane = lax.broadcasted_iota(jnp.int32, (1, width), 1) // head_dim
     visible = lax.broadcasted_iota(jnp.int32, (BLOCK, BLOCK), 0) <= lax.broadcasted_iota(
         jnp.int32, (BLOCK, BLOCK), 1
@@ -305,6 +366,177 @@
             dmixed_copy(s, d).wait_send()
             for i in range(3):
                 grad_copy(i, s, d).wait()
+    own.wait()
+    for copy in background:
+        copy.wait()
+
+
+def run_experts(
+    others,
+    ways,
+    outgoing_ref,
+    arrived_ref,
+    up_ref,
+    down_ref,
+    back_ref,
+    result_ref,
+    up_part,
+    down_part,
+    *rest,
+):
+    if ways == 4:
+        land_x, land_y, *rest = rest
+    (
+        received,
+        up_v,
+        down_v,
+        hidden,
+        slope_v,
+        total,
+        dnormed,
+        w_sem,
+        o_sem,
+        a_send,
+        a_recv,
+        b_send,
+        b_recv,
+        *rest,
+    ) = rest
+    slots, width = received.shape[1:]
+    ff = up_v.shape[0]
+    me = lax.axis_index("dp")
+    sp = lax.axis_index("sp")
+    chip = me // 2
+    load_down = pltpu.make_async_copy(down_ref, down_v, w_sem.at[0])
+    load_up = pltpu.make_async_copy(up_ref, up_v, w_sem.at[1])
+    load_down.start()
+    load_up.start()
+    peers = [{"dp": flip(me, d)} for d in range(1, others)]
+    if ways == 4:
+        peers += [{"sp": flip(sp, 1)}, {"sp": flip(sp, 2)}]
+    greet(peers)
+    inward = exchange(others, outgoing_ref, received, a_send, a_recv)
+    outward = exchange(others, dnormed, back_ref, b_send, b_recv)
+    for copy in reversed(inward):
+        copy.start()
+    received[me] = outgoing_ref[me]
+
+    rows = others * slots
+    load_down.wait()
+
+    def cot_step(i, carry):
+        at = span(i, STEP)
+        cot = arrived_ref[...].reshape(rows, width)
+        slope_v[:, at] = mxu(cot, down_v[at, :], ROWS_BY_ROWS).astype(jnp.bfloat16)
+        return carry
+
+    lax.fori_loop(0, ff // STEP, cot_step, 0)
+    load_up.wait()
+    for group in range(others // 2):
+        near = flip(chip, group)
+        for d in (2 * group, 2 * group + 1):
+            if d:
+                inward[d - 1].wait_recv()
+        slab = span(near, 2 * slots)
+        total[...] = jnp.zeros_like(total)
+
+        def up_step(i, carry):
+            at = span(i, STEP)
+            tokens = received[pl.ds(2 * near, 2)].reshape(2 * slots, width)
+            pre = mxu(tokens, up_v[at, :], ROWS_BY_ROWS)
+            square = pre * pre
+            inner = jnp.tanh(GELU_ROOT * pre * (1.0 + CUBIC_TERM * square))
+            half = 0.5 * (1.0 + inner)
+            hidden[slab, at] = (pre * half).astype(jnp.bfloat16)
+            slope = half + (0.5 * GELU_ROOT) * pre * (1.0 - inner * inner) * (
+                1.0 + (3.0 * CUBIC_TERM) * square
+            )
+            dpre = (slope_v[slab, at].astype(jnp.float32) * slope).astype(jnp.bfloat16)
+            slope_v[slab, at] = dpre
+            total[...] += mxu(dpre, up_v[at, :])
+            return carry
+
+        lax.fori_loop(0, ff // STEP, up_step, 0)
+        dnormed[pl.ds(2 * near, 2)] = total[...].reshape(2, slots, width).astype(jnp.bfloat16)
+        for d in (2 * group, 2 * group + 1):
+            if d:
+                outward[d - 1].start()
+            else:
+                back_ref[me] = dnormed[me]
+
+    quarter = ff // 4
+
+    def grad_shard(target, left, right_ref, shard):
+        def grad_step(i, carry):
+            at = pl.ds(pl.multiple_of(shard * quarter + i * STEP, STEP), STEP)
+            right = right_ref[...].reshape(rows, width)
+            target[at, :] = mxu(left[:, at], right, COLS_BY_COLS).astype(jnp.bfloat16)
+            return carry
+
+        lax.fori_loop(0, quarter // STEP, grad_step, 0)
+
+    side = []
+    if ways == 4:
+        x_send, x_recv, y_send, y_recv = rest
+        x_at, y_at = lax.rem(sp, 2), sp // 2
+        half = width // 2
+
+        def to_x(shard, slot, i):
+            return send(
+                up_v.at[span(shard, quarter), 0:half],
+                land_x.at[slot],
+                x_send.at[i],
+                x_recv.at[i],
+                {"sp": flip(sp, 1)},
+            )
+
+        def to_y(shard, slot, i):
+            return send(
+                up_v.at[span(shard, quarter), half:width],
+                land_y.at[slot],
+                y_send.at[i],
+                y_recv.at[i],
+                {"sp": flip(sp, 2)},
+            )
+
+        side = [
+            to_x(flip(sp, 3), 1 - y_at, 0),
+            to_y(flip(sp, 3), 1 - x_at, 0),
+            to_x(flip(sp, 1), y_at, 1),
+            to_y(flip(sp, 2), x_at, 1),
+        ]
+        grad_shard(up_v, hidden, arrived_ref, flip(sp, 3))
+        side[0].start()
+        side[1].start()
+        grad_shard(up_v, hidden, arrived_ref, flip(sp, 1))
+        side[2].start()
+        grad_shard(up_v, hidden, arrived_ref, flip(sp, 2))
+        side[3].start()
+        grad_shard(up_v, hidden, arrived_ref, sp)
+    else:
+        for shard in range(4):
+            grad_shard(up_v, hidden, arrived_ref, shard)
+    store_down = pltpu.make_async_copy(up_v, down_part, o_sem.at[0])
+    store_down.start()
+
+    def out_step(i, carry):
+        slab = span(i, 2 * slots)
+        result_ref[pl.ds(2 * i, 2)] = (
+            mxu(hidden[slab, :], down_v[...]).reshape(2, slots, width).astype(jnp.bfloat16)
+        )
+        return carry
+
+    lax.fori_loop(0, others // 2, out_step, 0)
+    for shard in range(4):
+        grad_shard(down_v, slope_v, received, shard)
+    store_up = pltpu.make_async_copy(down_v, up_part, o_sem.at[1])
+    store_up.start()
+    for copy in inward:
+        copy.wait_send()
+    for copy in outward + side:
+        copy.wait()
+    store_down.wait()
+    store_up.wait()
 
 
 def reduce_everywhere(
@@ -453,6 +685,35 @@
         cross_copy(d).wait()
 
 
+def scatter_halves(x_half, y_half, x_land, y_land, sp_at):
+    x_at, y_at = sp_at % 2, sp_at // 2
+    pick = lax.dynamic_index_in_dim
+    f32 = jnp.float32
+
+    def both(half, land, at, where):
+        return pick(half, where, 0, False).astype(f32) + pick(land, at, 0, False).astype(f32)
+
+    x_out = both(x_half, x_land, 1 - y_at, sp_at + 2 - 4 * y_at).astype(jnp.bfloat16)
+    y_out = both(y_half, y_land, 1 - x_at, sp_at + 1 - 2 * x_at).astype(jnp.bfloat16)
+    x_in = lax.ppermute(x_out, "sp", ALONG_Y)
+    y_in = lax.ppermute(y_out, "sp", ALONG_X)
+    return jnp.concatenate(
+        [
+            both(x_half, x_land, y_at, sp_at) + x_in.astype(f32),
+            both(y_half, y_land, x_at, sp_at) + y_in.astype(f32),
+        ],
+        axis=1,
+    )
+
+
+def first_stage(x_half, y_half, sp_at):
+    x_at, y_at = sp_at % 2, sp_at // 2
+    shape = (2, 2) + x_half.shape[1:]
+    x_out = lax.dynamic_index_in_dim(x_half.reshape(shape), 1 - x_at, 1, False)
+    y_out = lax.dynamic_index_in_dim(y_half.reshape(shape), 1 - y_at, 0, False)
+    return lax.ppermute(x_out, "sp", ALONG_X), lax.ppermute(y_out, "sp", ALONG_Y)
+
+
 def vmem(count):
     return [pl.BlockSpec(memory_space=pltpu.VMEM)] * count
 
@@ -512,13 +773,14 @@
     cot_b = out_cotangent.reshape(row_count, model_width)
     cot_send = jnp.dot(placer, cot_b, preferred_element_type=f32).astype(bf16)
     cot_send = cot_send.reshape(experts, slot_count, model_width)
-    arrived = lax.all_to_all(cot_send, "dp", split_axis=0, concat_axis=0, tiled=True)
 
     def columns_of(weight):
         return lax.dynamic_slice_in_dim(weight, sp_at * width, width, axis=1)
 
-    normed_all, query_h, key_h, value_h, log_total, mixed_b = pl.pallas_call(
-        functools.partial(attend_forward, sp_ways, head_dim),
+    routed = shape(experts, slot_count, model_width)
+    hbm = [pl.BlockSpec(memory_space=pl.ANY)]
+    normed_all, query_h, key_h, value_h, log_total, mixed_b, arrived = pl.pallas_call(
+        functools.partial(attend_forward, sp_ways, dp_ways, head_dim),
         out_shape=[
             shape(seq_count, seq_len, model_width),
             shape(seq_count, seq_len, width),
@@ -526,9 +788,10 @@
             shape(seq_count, seq_len, width),
             shape(seq_count, 8, seq_len, dtype=f32),
             shape(seq_count, shard_len, model_width),
+            routed,
         ],
-        in_specs=vmem(6),
-        out_specs=vmem(6),
+        in_specs=hbm + vmem(6),
+        out_specs=vmem(6) + hbm,
         scratch_shapes=[
             pltpu.VMEM((seq_count, seq_len, model_width), bf16),
             pltpu.VMEM((seq_len, width), f32),
@@ -538,9 +801,13 @@
             dma(seq_count, sp_ways),
             dma(seq_count, sp_ways),
             dma(seq_count, sp_ways),
+            dma(dp_ways),
+            dma(dp_ways),
+            pltpu.SemaphoreType.DMA,
         ],
         compiler_params=params(0),
     )(
+        cot_send,
         tokens_in,
         columns_of(query_weight),
         columns_of(key_weight),
@@ -556,33 +823,46 @@
     normed2_b = normed2.astype(bf16)
     outgoing = jnp.dot(placer, normed2_b, preferred_element_type=f32).astype(bf16)
     outgoing = outgoing.reshape(experts, slot_count, model_width)
-    received = lax.all_to_all(outgoing, "dp", split_axis=0, concat_axis=0, tiled=True)
-    parts = received.reshape(-1, local_experts, slot_count, model_width)
-    pre_act = jnp.einsum("sxcd,xfd->sxcf", parts, up_weight, preferred_element_type=f32)
-    hidden_b = smooth(pre_act).astype(bf16)
-    arrived_p = arrived.reshape(-1, local_experts, slot_count, model_width)
-    dhidden = jnp.einsum("sxcd,xfd->sxcf", arrived_p, down_weight, preferred_element_type=f32)
-    dpre_b = (dhidden * smooth_slope(pre_act)).astype(bf16)
-    dnormed_send = jnp.einsum("sxcf,xfd->sxcd", dpre_b, up_weight, preferred_element_type=f32)
-    dnormed_send = dnormed_send.astype(bf16).reshape(-1, slot_count, model_width)
-    dnormed_back = lax.all_to_all(dnormed_send, "dp", split_axis=0, concat_axis=0, tiled=True)
-    expert_out = jnp.einsum("sxcf,xfd->sxcd", hidden_b, down_weight, preferred_element_type=f32)
-    expert_out = expert_out.astype(bf16).reshape(received.shape)
-    returned = lax.all_to_all(expert_out, "dp", split_axis=0, concat_axis=0, tiled=True)
-    expert_rows = jnp.einsum(
-        "er,ed->rd",
-        placer,
-        returned.reshape(experts * slot_count, model_width),
-        preferred_element_type=f32,
-    )
-    block_out = (residual_stream + expert_rows).astype(bf16)
-    block_out = block_out.reshape(seq_count, shard_len, model_width)
-    up_full = jnp.einsum("sxcf,sxcd->xfd", dpre_b, parts, preferred_element_type=f32)
-    down_full = jnp.einsum("sxcf,sxcd->xfd", hidden_b, arrived_p, preferred_element_type=f32)
-    up_grad, down_grad = (
-        lax.psum_scatter(grad.astype(bf16), "sp", scatter_dimension=1, tiled=True).astype(f32)
-        for grad in (up_full, down_full)
-    )
+    landing = [shape(2, ff_width // 4, model_width // 2)] * 2 if sp_ways == 4 else []
+    side_sems = [dma(2)] * 4 if sp_ways == 4 else []
+    dnormed_back, expert_out, up_part, down_part, *landed = pl.pallas_call(
+        functools.partial(run_experts, dp_ways, sp_ways),
+        out_shape=[routed, routed, shape(ff_width, model_width), shape(ff_width, model_width)]
+        + landing,
+        in_specs=vmem(2) + hbm * 2,
+        out_specs=vmem(2) + hbm * (2 + len(landing)),
+        scratch_shapes=[
+            pltpu.VMEM((experts, slot_count, model_width), bf16),
+            pltpu.VMEM((ff_width, model_width), bf16),
+            pltpu.VMEM((ff_width, model_width), bf16),
+            pltpu.VMEM((experts * slot_count, ff_width), bf16),
+            pltpu.VMEM((experts * slot_count, ff_width), bf16),
+            pltpu.VMEM((2 * slot_count, model_width), f32),
+            pltpu.VMEM((experts, slot_count, model_width), bf16),
+            dma(2),
+            dma(2),
+            dma(dp_ways),
+            dma(dp_ways),
+            dma(dp_ways),
+            dma(dp_ways),
+        ]
+        + side_sems,
+        compiler_params=params(3),
+    )(outgoing, arrived, up_weight[0], down_weight[0])
+    if sp_ways == 4:
+
+        def halves(part):
+            part = part.reshape(4, ff_width // 4, model_width)
+            return part[:, :, : model_width // 2], part[:, :, model_width // 2 :]
+
+        down_grad = scatter_halves(*halves(down_part), *landed, sp_at)[None]
+        landed = first_stage(*halves(up_part), sp_at)
+        up_grad = scatter_halves(*halves(up_part), *landed, sp_at)[None]
+    else:
+        up_grad, down_grad = (
+            lax.psum_scatter(part, "sp", scatter_dimension=0, tiled=True).astype(f32)[None]
+            for part in (up_part, down_part)
+        )
     dnormed2 = jnp.einsum(
         "er,ed->rd",
         placer,
@@ -597,11 +877,12 @@
     out_grad = jnp.einsum("rd,re->de", mixed_b, dattn_b, preferred_element_type=f32).astype(bf16)
     out_part = lax.psum_scatter(out_grad, "sp", scatter_dimension=1, tiled=True)
     grads = pl.pallas_call(
-        functools.partial(attend_backward, sp_ways, head_dim),
+        functools.partial(attend_backward, sp_ways, dp_ways, head_dim),
         out_shape=[shape(seq_count, seq_len, width)] * 3
-        + [shape(seq_count, shard_len, model_width)] * 3,
-        in_specs=vmem(5),
-        out_specs=vmem(6),
+        + [shape(seq_count, shard_len, model_width)] * 3
+        + [routed],
+        in_specs=hbm + vmem(5),
+        out_specs=vmem(6) + hbm,
         scratch_shapes=[
             pltpu.VMEM((seq_count, seq_len, width), bf16),
             pltpu.VMEM((seq_len, width), f32),
@@ -611,10 +892,21 @@
             dma(seq_count, sp_ways),
             dma(3, seq_count, sp_ways),
             dma(3, seq_count, sp_ways),
+            dma(dp_ways),
+            dma(dp_ways),
+            pltpu.SemaphoreType.DMA,
         ],
         compiler_params=params(1),
-    )(dmixed_b, query_h, key_h, value_h, log_total)
-    head_grads, token_grads = grads[:3], grads[3:]
+    )(expert_out, dmixed_b, query_h, key_h, value_h, log_total)
+    head_grads, token_grads, returned = grads[:3], grads[3:6], grads[6]
+    expert_rows = jnp.einsum(
+        "er,ed->rd",
+        placer,
+        returned.reshape(experts * slot_count, model_width),
+        preferred_element_type=f32,
+    )
+    block_out = (residual_stream + expert_rows).astype(bf16)
+    block_out = block_out.reshape(seq_count, shard_len, model_width)
     weight_parts = [
         jnp.einsum("skd,ske->de", normed_all, grad, preferred_element_type=f32).astype(bf16)
         for grad in head_grads

time: 642 us -> 563 us (0.88)
  Pallas kernels: 285 us -> 426 us
  matrix products: 144 us -> 31.5 us
  waiting for transfers between devices: 72.5 us -> 8.67 us
  blocking collectives: 52.2 us -> 0 us
  starting transfers between devices: 21.6 us -> 5.27 us
  other arithmetic: 32.2 us -> 44.6 us
  local copies, waits for them, and re-layouts: 10.1 us -> 22.4 us
    pallas_call x2 -> x3, Pallas kernels: 153 us -> 307 us  [the longest x1 118 us: local(): pl.pallas_call(functools.partial(run_experts, dp_ways, sp_ways), out_shap...]
    dot_general x6 -> x0, matrix products: 112 us -> none  [the longest x1 23.8 us: local(): jnp.einsum('sxcd,xfd->sxcf', arrived_p, down_weight, preferred_element_ty...]
    all_to_all x3 -> x0, waiting for transfers between devices: 72.4 us -> none  [the longest x1 42.9 us: local(): lax.all_to_all(outgoing, 'dp', split_axis=0, concat_axis=0, tiled=True)]
    all_to_all x1 -> x0, blocking collectives: 52.2 us -> none  [local(): lax.all_to_all(dnormed_send, 'dp', split_axis=0, concat_axis=0, tiled=True)]
    all_to_all x3 -> x0, starting transfers between devices: 21.5 us -> none  [the longest x1 7.88 us: local(): lax.all_to_all(cot_send, 'dp', split_axis=0, concat_axis=0, tiled=True)]
    pallas_call x1, Pallas kernels: 132 us -> 119 us  [local(): pl.pallas_call(functools.partial(reduce_everywhere, sp_ways, columns), ou...]
    slice x1 -> x3, local copies, waits for them, and re-layouts: 0.21 us -> 9.87 us  [the longest x2 9.66 us: halves(): return (part[:, :, :model_width // 2], part[:, :, model_width // 2:])]
    add x0 -> x4, other arithmetic: none -> 8.7 us  [the longest x2 4.78 us: scatter_halves(): both(x_half, x_land, y_at, sp_at) + x_in.astype(f32)]
  transfers between devices with their start and end apart: 6 -> 7, of which waited for: 2 -> 2; matrix products, arithmetic and copies ran while one was open for 18% -> 10% of each run, Pallas kernels for 33% -> 21%
where the time goes in v2:
time: 563 us; the launch traced here: 554 us
  Pallas kernels  426 us (76%)
  other arithmetic  44.6 us (8%)
  matrix products  31.5 us (6%)
  local copies, waits for them, and re-layouts  22.4 us (4%)
  between operations  14.9 us (3%)
  waiting for transfers between devices  8.67 us (2%)
    pallas_call x1, Pallas kernels, local(): pl.pallas_call(functools.partial(reduce_everywhere, sp_ways, columns), ou...  119 us
    pallas_call x1, Pallas kernels, local(): pl.pallas_call(functools.partial(run_experts, dp_ways, sp_ways), out_shap...  118 us
    pallas_call x1, Pallas kernels, local(): pl.pallas_call(functools.partial(attend_backward, sp_ways, dp_ways, head_...  114 us
    pallas_call x1, Pallas kernels, local(): pl.pallas_call(functools.partial(attend_forward, sp_ways, dp_ways, head_d...  74.6 us
  transfers between devices with their start and end apart: 7, of which 2 were waited for; matrix products, arithmetic and copies ran while one was open for 10% of the time, Pallas kernels for 21%

profile of v2, /device:TPU:9, one launch (start us, length us, event | category | flops | bytes accessed | tf_op | source)
XLA Modules:
  0.0 553.6 jit_solution(15191133362006290108)
XLA Ops:
  15.2 2.6 fusion.16
  17.8 74.6 %shard_map.237 = (bf16[2,1024,1024]{2,1,0:T(8,128)(2,1)}, bf16[2,1024,256]{2,1,0:T(8,128)(2,1)}, bf16[2,1024,256]{2,1,0:T(8,128)(2,1)}, bf16[2,1024,256]{2,1,0:T...) custom-call(bf16[8,128,1024]{2,1,0:T(8,128)(2,1)} %bitcast.135, ...), custom_call_target="tpu_custom_call" | custom-call | tf_op jit(solution)/shard_map/pallas_call | solution.py:782
  92.4 2.6 fusion.41
  95.7 2.8 fusion.17
  98.5 118.4 %shard_map.238 = (bf16[8,128,1024]{2,1,0:T(8,128)(2,1)}, bf16[8,128,1024]{2,1,0:T(8,128)(2,1)}, bf16[4096,1024]{1,0:T(8,128)(2,1)}, bf16[4096,1024]{1,0:T(8,128)...) custom-call(bf16[8,128,1024]{2,1,0:T(8,128)(2,1)} %bitcast.134, ...), custom_call_target="tpu_custom_call" | custom-call | tf_op jit(solution)/shard_map/pallas_call | solution.py:828
  217.0 5.8 %fusion.38 = (bf16[4,1024,512]{2,1,0:T(8,128)(2,1)}, bf16[4,1024,512]{2,1,0:T(8,128)(2,1)}) fusion(bf16[4,1024,1024]{2,1,0:T(8,128)(2,1)} %bitcast.132), kind=kLoop, calls=%fused_computation.93 | loop fusion | bytes 16777216 | tf_op jit(solution)/shard_map/slice | solution.py:856
  222.8 2.8 fusion.23
  226.9 2.8 fusion.24
  229.9 3.8 fusion.39
  244.0 2.6 convolution_convert_fusion
  246.7 3.9 convolution_convert_fusion.1
  250.7 114.2 %shard_map.239 = (bf16[2,1024,256]{2,1,0:T(8,128)(2,1)}, bf16[2,1024,256]{2,1,0:T(8,128)(2,1)}, bf16[2,1024,256]{2,1,0:T(8,128)(2,1)}, bf16[2,256,1024]{2,1,0:T(...) custom-call(bf16[8,128,1024]{2,1,0:T(8,128)(2,1)} %get-tuple-element.37.res, ...), custom_call_target="tpu_custom_call" | custom-call | tf_op jit(solution)/shard_map/pallas_call | solution.py:879
  365.0 3.3 fusion.42
  375.2 2.3 add_convert_fusion.4
  382.1 2.9 fusion.21
  390.9 2.5 bitcast_add_fusion.1
  395.4 2.5 maximum_bitcast_fusion.1
  397.9 6.3 %collective-permute-done.1 = bf16[1024,512]{1,0:T(8,128)(2,1)} collective-permute-done((bf16[1024,512]{1,0:T(8,128)(2,1)}, bf16[1024,512]{1,0:T(8,128)(2,1)}, u32[]{:S(2)}, u32[]{:S(2)}) %collective-permute-start.1) | collective-permute-done | bytes 1048608 | tf_op jit(solution)/shard_map/ppermute | solution.py:698
  404.2 2.3 bitcast_add_fusion.3
  406.5 2.3 collective-permute-done.3
  410.8 2.5 maximum_bitcast_fusion
  413.2 2.7 pad_maximum_fusion
  415.9 118.9 %shard_map.240 = (bf16[4096,1024]{1,0:T(8,128)(2,1)}, f32[8,1024]{1,0:T(8,128)}) custom-call(bf16[2,4,512,256]{3,2,1,0:T(8,128)(2,1)} %bitcast.133, f32[8,1024]{1,0:T(8,128)} %stack.27.small_ref), custom_call_target="tpu_custom_call" | custom-call | tf_op jit(solution)/shard_map/pallas_call | solution.py:937
  534.8 10.3 %slice_convert_fusion = (f32[1024,1024]{1,0:T(8,128)}, f32[1024,1024]{1,0:T(8,128)}, f32[1024,1024]{1,0:T(8,128)}, f32[1024,1024]{1,0:T(8,128)}) fusion(bf16[4096,1024]{1,0:T(8,128)(2,1)} %get-tuple-element.51), kind=kLoop, calls=%fused_computation.29 | loop fusion | flops 4194304 | bytes 25165824 | tf_op jit(solution)/shard_map/convert_element_type | solution.py:969
  (117 shorter events, 42.9 us)
Async XLA Ops:
  7.2 85.2 %copy-start = (bf16[1024,1024]{1,0:T(8,128)(2,1)S(1)}, bf16[1024,1024]{1,0:T(8,128)(2,1)}, u32[]{:S(2)}) copy-start(bf16[1024,1024]{1,0:T(8,128)(2,1)} %param.19) | copy-start | bytes 6291460
  7.2 8.0 %copy-start.11 = (bf16[2,256,1024]{2,1,0:T(8,128)(2,1)S(1)}, bf16[2,256,1024]{2,1,0:T(8,128)(2,1)}, u32[]{:S(2)}) copy-start(bf16[2,256,1024]{2,1,0:T(8,128)(2,1)} %param.26) | copy-start | bytes 3145732
  7.2 406.0 %reduce-scatter.2.cloned.1.call-start = ((), (), s32[]{:S(2)}) async-start(), calls=%async_computation.1 | async-start | bytes 2621440 | tf_op jit(solution)/shard_map/reduce_scatter | solution.py:878
  17.8 74.6 %copy-start.2 = (bf16[2,256,1024]{2,1,0:T(8,128)(2,1)S(1)}, bf16[2,256,1024]{2,1,0:T(8,128)(2,1)}, u32[]{:S(2)}) copy-start(bf16[2,256,1024]{2,1,0:T(8,128)(2,1)} %x_ref.1) | copy-start | bytes 3145732
  95.0 3.6 copy-start.5
  225.6 165.2 %collective-permute-start.4 = (bf16[1024,512]{1,0:T(8,128)(2,1)}, bf16[1024,512]{1,0:T(8,128)(2,1)}, u32[]{:S(2)}, u32[]{:S(2)}) collective-permute-start(bf16[1024,512]{1,0:T(8,128)(2,1)} %fusion.23), channel_id=1, source_target_pairs={{0,2},{2,0},{1,3},{3,1},{4,6},{6,4},{5,7},{7,5},{8,10},{10,8},{9,1... | collective-permute-start | bytes 3145736 | tf_op jit(solution)/shard_map/ppermute | solution.py:698
  229.6 163.8 %collective-permute-start.5 = (bf16[1024,512]{1,0:T(8,128)(2,1)}, bf16[1024,512]{1,0:T(8,128)(2,1)}, u32[]{:S(2)}, u32[]{:S(2)}) collective-permute-start(bf16[1024,512]{1,0:T(8,128)(2,1)} %fusion.24), channel_id=1, source_target_pairs={{0,1},{1,0},{2,3},{3,2},{4,5},{5,4},{6,7},{7,6},{8,9},{9,8},{10,11... | collective-permute-start | bytes 3145736 | tf_op jit(solution)/shard_map/ppermute | solution.py:699
  233.7 2.9 copy-start.3
  233.7 8.1 %copy-start.4 = (bf16[4,1024,512]{2,1,0:T(8,128)(2,1)}, bf16[4,1024,512]{2,1,0:T(8,128)(2,1)S(1)}, u32[]{:S(2)}) copy-start(bf16[4,1024,512]{2,1,0:T(8,128)(2,1)S(1)} %get-tuple-element.69) | copy-start | bytes 12582916
  235.4 146.7 %collective-permute-start = (bf16[2,1024,512]{2,1,0:T(8,128)(2,1)}, bf16[2,1024,512]{2,1,0:T(8,128)(2,1)}, u32[]{:S(2)}, u32[]{:S(2)}) collective-permute-start(bf16[2,1024,512]{2,1,0:T(8,128)(2,1)} %dynamic-slice_bitcast_fusion.1), channel_id=1, source_target_pairs={{0,1},{1,0},{2,3},{3,2},{4,5},{5,4},{6,7},{7,6},{8,9},{9,8},{10,11... | collective-permute-start | bytes 6291464 | tf_op jit(solution)/shard_map/ppermute | solution.py:714
  236.6 2.7 copy-start.6
  236.6 3.3 copy-start.21
  238.1 149.9 %collective-permute-start.2 = (bf16[2,1024,512]{2,1,0:T(8,128)(2,1)}, bf16[2,1024,512]{2,1,0:T(8,128)(2,1)}, u32[]{:S(2)}, u32[]{:S(2)}) collective-permute-start(bf16[2,1024,512]{2,1,0:T(8,128)(2,1)} %dynamic-slice_bitcast_fusion), channel_id=1, source_target_pairs={{0,2},{2,0},{1,3},{3,1},{4,6},{6,4},{5,7},{7,5},{8,10},{10,8},{9,1... | collective-permute-start | bytes 6291464 | tf_op jit(solution)/shard_map/ppermute | solution.py:714
  365.0 3.4 copy-start.15
  365.0 3.4 copy-start.28
  375.2 2.7 copy-start.25
  382.1 3.5 copy-start.9
  385.0 19.2 %collective-permute-start.1 = (bf16[1024,512]{1,0:T(8,128)(2,1)}, bf16[1024,512]{1,0:T(8,128)(2,1)}, u32[]{:S(2)}, u32[]{:S(2)}) collective-permute-start(bf16[1024,512]{1,0:T(8,128)(2,1)} %fusion.21), channel_id=1, source_target_pairs={{0,2},{2,0},{1,3},{3,1},{4,6},{6,4},{5,7},{7,5},{8,10},{10,8},{9,1... | collective-permute-start | bytes 3145736 | tf_op jit(solution)/shard_map/ppermute | solution.py:698
  389.8 3.6 copy-start.10
  389.8 19.0 %collective-permute-start.3 = (bf16[1024,512]{1,0:T(8,128)(2,1)S(1)}, bf16[1024,512]{1,0:T(8,128)(2,1)S(1)}, u32[]{:S(2)}, u32[]{:S(2)}) collective-permute-start(bf16[1024,512]{1,0:T(8,128)(2,1)S(1)} %fusion.22), channel_id=1, source_target_pairs={{0,1},{1,0},{2,3},{3,2},{4,5},{5,4},{6,7},{7,6},{8,9},{9,8},{10,11... | collective-permute-start | bytes 3145736 | tf_op jit(solution)/shard_map/ppermute | solution.py:699
  410.7 2.5 copy-start.13
  534.8 10.4 %copy-start.18 = (f32[8,1024]{1,0:T(8,128)S(1)}, f32[8,1024]{1,0:T(8,128)}, u32[]{:S(2)}) copy-start(f32[8,1024]{1,0:T(8,128)} %get-tuple-element.52) | copy-start | bytes 98308
  534.8 11.0 %copy-start.30 = (f32[8]{0:T(128)S(1)}, f32[8]{0:T(128)}, u32[]{:S(2)}) copy-start(f32[8]{0:T(128)} %param.27) | copy-start | bytes 100
  534.8 11.5 %copy-start.1 = (bf16[1024,1024]{1,0:T(8,128)(2,1)S(1)}, bf16[1024,1024]{1,0:T(8,128)(2,1)}, u32[]{:S(2)}) copy-start(bf16[1024,1024]{1,0:T(8,128)(2,1)} %param.19) | copy-start | bytes 6291460
  (14 other events, 26.9 us)
Sparse Core Ops, SparseCore 0:
  246.8 56.8 reduce-scatter.1

commit v3 on v2

--- a/solution.py
+++ b/solution.py
@@ -12,8 +12,6 @@
 BLOCK = 256
 LANES = 128
 STEP = 512
-ALONG_X = [(0, 1), (1, 0), (2, 3), (3, 2)]
-ALONG_Y = [(0, 2), (2, 0), (1, 3), (3, 1)]
 VMEM_BYTES = 60 * 2**20
 
 NORM_EPSILON = 1e-05
@@ -248,6 +246,8 @@
     others,
     head_dim,
     result_ref,
+    up_part,
+    down_part,
     dmixed_ref,
     q_ref,
     k_ref,
@@ -260,6 +260,8 @@
     dk_tok,
     dv_tok,
     returned_ref,
+    up_land,
+    down_land,
     dmixed_h,
     dq_f,
     dk_f,
@@ -270,6 +272,8 @@
     g_recv,
     c_send,
     c_recv,
+    s_send,
+    s_recv,
     local_sem,
 ):
     seqs, shard, _ = dmixed_ref.shape
@@ -282,6 +286,19 @@
         + [{"dp": flip(lax.axis_index("dp"), d)} for d in range(1, others)]
     )
     background = exchange(others, result_ref, returned_ref, c_send, c_recv)
+    shards = shards_of(me, ways)
+    size = up_land.shape[1]
+    background += [
+        send(
+            part.at[i * size : (i + 1) * size],
+            land.at[i - 1],
+            s_send.at[j, i],
+            s_recv.at[j, i],
+            {"sp": shards[i]},
+        )
+        for j, (part, land) in enumerate(((up_part, up_land), (down_part, down_land)))
+        for i in range(1, len(shards))
+    ]
     own = pltpu.make_async_copy(
         result_ref.at[lax.axis_index("dp")], returned_ref.at[lax.axis_index("dp")], local_sem
     )
@@ -371,84 +388,138 @@
         copy.wait()
 
 
+def pair_of(sp):
+    core = lax.rem(lax.axis_index("dp"), 2)
+    along_x, along_y = flip(sp, 1), flip(sp, 2)
+    return along_x + core * (along_y - along_x)
+
+
+def shards_of(sp, ways):
+    shards = [sp, flip(pair_of(sp), 3)]
+    bit = 4
+    while bit < ways:
+        shards += [flip(shard, bit) for shard in shards]
+        bit *= 2
+    return shards
+
+
 def run_experts(
     others,
     ways,
     outgoing_ref,
-    arrived_ref,
+    cot_ref,
     up_ref,
     down_ref,
     back_ref,
     result_ref,
     up_part,
     down_part,
-    *rest,
+    received,
+    arrived,
+    up_v,
+    down_v,
+    hidden,
+    slope_v,
+    total,
+    dn_own,
+    dn_pair,
+    dn_land,
+    dnormed,
+    out_pair,
+    out_land,
+    w_sem,
+    o_sem,
+    c_sem,
+    a_send,
+    a_recv,
+    b_send,
+    b_recv,
+    f_send,
+    f_recv,
+    p_send,
+    p_recv,
 ):
-    if ways == 4:
-        land_x, land_y, *rest = rest
-    (
-        received,
-        up_v,
-        down_v,
-        hidden,
-        slope_v,
-        total,
-        dnormed,
-        w_sem,
-        o_sem,
-        a_send,
-        a_recv,
-        b_send,
-        b_recv,
-        *rest,
-    ) = rest
-    slots, width = received.shape[1:]
+    slots, width = received.shape[2:]
+    rows = others * slots
     ff = up_v.shape[0]
+    groups = others // 2
     me = lax.axis_index("dp")
     sp = lax.axis_index("sp")
     chip = me // 2
-    load_down = pltpu.make_async_copy(down_ref, down_v, w_sem.at[0])
-    load_up = pltpu.make_async_copy(up_ref, up_v, w_sem.at[1])
-    load_down.start()
-    load_up.start()
-    peers = [{"dp": flip(me, d)} for d in range(1, others)]
-    if ways == 4:
-        peers += [{"sp": flip(sp, 1)}, {"sp": flip(sp, 2)}]
-    greet(peers)
-    inward = exchange(others, outgoing_ref, received, a_send, a_recv)
+    pair = {"sp": pair_of(sp)}
+    shards = shards_of(sp, ways)
+    size = ff // len(shards)
+    loads = [
+        pltpu.make_async_copy(
+            source.at[span(shard, size)], target.at[i * size : (i + 1) * size], w_sem.at[j, i]
+        )
+        for j, (source, target) in enumerate(((down_ref, down_v), (up_ref, up_v)))
+        for i, shard in enumerate(shards)
+    ]
+    own_cot = pltpu.make_async_copy(cot_ref, arrived.at[0], c_sem)
+    own_cot.start()
+    for copy in loads:
+        copy.start()
+    greet([{"dp": flip(me, d)} for d in range(1, others)] + [pair])
+    inward = exchange(others, outgoing_ref, received.at[0], a_send, a_recv)
     outward = exchange(others, dnormed, back_ref, b_send, b_recv)
-    for copy in reversed(inward):
+    near = [flip(chip, group) for group in range(groups)]
+    chips = [pl.ds(2 * near[group], 2) for group in range(groups)]
+    forward = [
+        send(
+            received.at[0, chips[group]],
+            received.at[1, chips[group]],
+            f_send.at[group],
+            f_recv.at[group],
+            pair,
+        )
+        for group in range(groups)
+    ]
+    cot_copy = send(cot_ref, arrived.at[1], f_send.at[groups], f_recv.at[groups], pair)
+    dn_copy = [
+        send(
+            dn_pair.at[chips[group]],
+            dn_land.at[chips[group]],
+            p_send.at[group],
+            p_recv.at[group],
+            pair,
+        )
+        for group in range(groups)
+    ]
+    out_copy = send(out_pair, out_land, p_send.at[groups], p_recv.at[groups], pair)
+
+    for copy in inward:
         copy.start()
-    received[me] = outgoing_ref[me]
-
-    rows = others * slots
-    load_down.wait()
-
-    def cot_step(i, carry):
-        at = span(i, STEP)
-        cot = arrived_ref[...].reshape(rows, width)
-        slope_v[:, at] = mxu(cot, down_v[at, :], ROWS_BY_ROWS).astype(jnp.bfloat16)
-        return carry
-
-    lax.fori_loop(0, ff // STEP, cot_step, 0)
-    load_up.wait()
-    for group in range(others // 2):
-        near = flip(chip, group)
-        for d in (2 * group, 2 * group + 1):
-            if d:
-                inward[d - 1].wait_recv()
-        slab = span(near, 2 * slots)
+    received[0, me] = outgoing_ref[me]
+    cot_copy.start()
+
+    def slab_of(half, group):
+        return pl.ds(pl.multiple_of(half * rows + near[group] * (2 * slots), 2 * slots), 2 * slots)
+
+    def cot_half(half):
+        def cot_step(i, carry):
+            at = span(i, STEP)
+            cot = arrived[half].reshape(rows, width)
+            slope_v[half * rows : (half + 1) * rows, at] = mxu(
+                cot, down_v[at, :], ROWS_BY_ROWS
+            ).astype(jnp.bfloat16)
+            return carry
+
+        lax.fori_loop(0, ff // STEP, cot_step, 0)
+
+    def up_half(half, group):
+        slab = slab_of(half, group)
         total[...] = jnp.zeros_like(total)
 
         def up_step(i, carry):
             at = span(i, STEP)
-            tokens = received[pl.ds(2 * near, 2)].reshape(2 * slots, width)
+            tokens = received[half, chips[group]].reshape(2 * slots, width)
             pre = mxu(tokens, up_v[at, :], ROWS_BY_ROWS)
             square = pre * pre
             inner = jnp.tanh(GELU_ROOT * pre * (1.0 + CUBIC_TERM * square))
-            half = 0.5 * (1.0 + inner)
-            hidden[slab, at] = (pre * half).astype(jnp.bfloat16)
-            slope = half + (0.5 * GELU_ROOT) * pre * (1.0 - inner * inner) * (
+            gate = 0.5 * (1.0 + inner)
+            hidden[slab, at] = (pre * gate).astype(jnp.bfloat16)
+            slope = gate + (0.5 * GELU_ROOT) * pre * (1.0 - inner * inner) * (
                 1.0 + (3.0 * CUBIC_TERM) * square
             )
             dpre = (slope_v[slab, at].astype(jnp.float32) * slope).astype(jnp.bfloat16)
@@ -457,86 +528,98 @@
             return carry
 
         lax.fori_loop(0, ff // STEP, up_step, 0)
-        dnormed[pl.ds(2 * near, 2)] = total[...].reshape(2, slots, width).astype(jnp.bfloat16)
+        shaped = total[...].reshape(2, slots, width)
+        if half:
+            dn_pair[chips[group]] = shaped.astype(jnp.bfloat16)
+            dn_copy[group].start()
+        else:
+            dn_own[chips[group]] = shaped
+
+    def pass_on(group):
+        for d in (2 * group, 2 * group + 1):
+            if d:
+                inward[d - 1].wait_recv()
+        forward[group].start()
+
+    def finish(group):
+        dn_copy[group].wait_recv()
+        at = chips[group]
+        dnormed[at] = (dn_own[at] + dn_land[at].astype(jnp.float32)).astype(jnp.bfloat16)
         for d in (2 * group, 2 * group + 1):
             if d:
                 outward[d - 1].start()
             else:
                 back_ref[me] = dnormed[me]
 
-    quarter = ff // 4
-
-    def grad_shard(target, left, right_ref, shard):
+    pass_on(0)
+    own_cot.wait()
+    for copy in loads[: len(shards)]:
+        copy.wait()
+    cot_half(0)
+    for copy in loads[len(shards) :]:
+        copy.wait()
+    up_half(0, 0)
+    cot_copy.wait_recv()
+    cot_half(1)
+    forward[0].wait_recv()
+    up_half(1, 0)
+    early = groups // 2
+    for group in range(1, early):
+        pass_on(group)
+        up_half(0, group)
+        forward[group].wait_recv()
+        up_half(1, group)
+    for group in range(early):
+        finish(group)
+    for group in range(early, groups):
+        pass_on(group)
+        up_half(0, group)
+        if group > early:
+            forward[group - 1].wait_recv()
+            up_half(1, group - 1)
+    forward[groups - 1].wait_recv()
+    up_half(1, groups - 1)
+    for group in range(early, groups):
+        finish(group)
+
+    def out_half(half):
+        def out_step(i, carry):
+            slab = pl.ds(pl.multiple_of(half * rows + i * (2 * slots), 2 * slots), 2 * slots)
+            out = mxu(hidden[slab, :], down_v[...]).reshape(2, slots, width)
+            at = pl.ds(2 * i, 2)
+            if half:
+                out_pair[at] = out.astype(jnp.bfloat16)
+            else:
+                result_ref[at] = (out + out_land[at].astype(jnp.float32)).astype(jnp.bfloat16)
+            return carry
+
+        lax.fori_loop(0, groups, out_step, 0)
+
+    def grad(target, left, right_ref):
         def grad_step(i, carry):
-            at = pl.ds(pl.multiple_of(shard * quarter + i * STEP, STEP), STEP)
-            right = right_ref[...].reshape(rows, width)
+            at = span(i, STEP)
+            right = right_ref[...].reshape(2 * rows, width)
             target[at, :] = mxu(left[:, at], right, COLS_BY_COLS).astype(jnp.bfloat16)
             return carry
 
-        lax.fori_loop(0, quarter // STEP, grad_step, 0)
-
-    side = []
-    if ways == 4:
-        x_send, x_recv, y_send, y_recv = rest
-        x_at, y_at = lax.rem(sp, 2), sp // 2
-        half = width // 2
-
-        def to_x(shard, slot, i):
-            return send(
-                up_v.at[span(shard, quarter), 0:half],
-                land_x.at[slot],
-                x_send.at[i],
-                x_recv.at[i],
-                {"sp": flip(sp, 1)},
-            )
-
-        def to_y(shard, slot, i):
-            return send(
-                up_v.at[span(shard, quarter), half:width],
-                land_y.at[slot],
-                y_send.at[i],
-                y_recv.at[i],
-                {"sp": flip(sp, 2)},
-            )
-
-        side = [
-            to_x(flip(sp, 3), 1 - y_at, 0),
-            to_y(flip(sp, 3), 1 - x_at, 0),
-            to_x(flip(sp, 1), y_at, 1),
-            to_y(flip(sp, 2), x_at, 1),
-        ]
-        grad_shard(up_v, hidden, arrived_ref, flip(sp, 3))
-        side[0].start()
-        side[1].start()
-        grad_shard(up_v, hidden, arrived_ref, flip(sp, 1))
-        side[2].start()
-        grad_shard(up_v, hidden, arrived_ref, flip(sp, 2))
-        side[3].start()
-        grad_shard(up_v, hidden, arrived_ref, sp)
-    else:
-        for shard in range(4):
-            grad_shard(up_v, hidden, arrived_ref, shard)
-    store_down = pltpu.make_async_copy(up_v, down_part, o_sem.at[0])
+        lax.fori_loop(0, ff // STEP, grad_step, 0)
+
+    out_half(1)
+    out_copy.start()
+    grad(up_v, slope_v, received)
+    store_up = pltpu.make_async_copy(up_v, up_part, o_sem.at[0])
+    store_up.start()
+    out_copy.wait_recv()
+    out_half(0)
+    grad(down_v, hidden, arrived)
+    store_down = pltpu.make_async_copy(down_v, down_part, o_sem.at[1])
     store_down.start()
-
-    def out_step(i, carry):
-        slab = span(i, 2 * slots)
-        result_ref[pl.ds(2 * i, 2)] = (
-            mxu(hidden[slab, :], down_v[...]).reshape(2, slots, width).astype(jnp.bfloat16)
-        )
-        return carry
-
-    lax.fori_loop(0, others // 2, out_step, 0)
-    for shard in range(4):
-        grad_shard(down_v, slope_v, received, shard)
-    store_up = pltpu.make_async_copy(down_v, up_part, o_sem.at[1])
-    store_up.start()
-    for copy in inward:
+    for copy in inward + forward + [cot_copy] + dn_copy + [out_copy]:
         copy.wait_send()
-    for copy in outward + side:
+    for copy in outward:
         copy.wait()
+    store_up.wait()
     store_down.wait()
-    store_up.wait()
 
 
 def reduce_everywhere(
@@ -685,35 +768,6 @@
         cross_copy(d).wait()
 
 
-def scatter_halves(x_half, y_half, x_land, y_land, sp_at):
-    x_at, y_at = sp_at % 2, sp_at // 2
-    pick = lax.dynamic_index_in_dim
-    f32 = jnp.float32
-
-    def both(half, land, at, where):
-        return pick(half, where, 0, False).astype(f32) + pick(land, at, 0, False).astype(f32)
-
-    x_out = both(x_half, x_land, 1 - y_at, sp_at + 2 - 4 * y_at).astype(jnp.bfloat16)
-    y_out = both(y_half, y_land, 1 - x_at, sp_at + 1 - 2 * x_at).astype(jnp.bfloat16)
-    x_in = lax.ppermute(x_out, "sp", ALONG_Y)
-    y_in = lax.ppermute(y_out, "sp", ALONG_X)
-    return jnp.concatenate(
-        [
-            both(x_half, x_land, y_at, sp_at) + x_in.astype(f32),
-            both(y_half, y_land, x_at, sp_at) + y_in.astype(f32),
-        ],
-        axis=1,
-    )
-
-
-def first_stage(x_half, y_half, sp_at):
-    x_at, y_at = sp_at % 2, sp_at // 2
-    shape = (2, 2) + x_half.shape[1:]
-    x_out = lax.dynamic_index_in_dim(x_half.reshape(shape), 1 - x_at, 1, False)
-    y_out = lax.dynamic_index_in_dim(y_half.reshape(shape), 1 - y_at, 0, False)
-    return lax.ppermute(x_out, "sp", ALONG_X), lax.ppermute(y_out, "sp", ALONG_Y)
-
-
 def vmem(count):
     return [pl.BlockSpec(memory_space=pltpu.VMEM)] * count
 
@@ -823,46 +877,41 @@
     normed2_b = normed2.astype(bf16)
     outgoing = jnp.dot(placer, normed2_b, preferred_element_type=f32).astype(bf16)
     outgoing = outgoing.reshape(experts, slot_count, model_width)
-    landing = [shape(2, ff_width // 4, model_width // 2)] * 2 if sp_ways == 4 else []
-    side_sems = [dma(2)] * 4 if sp_ways == 4 else []
-    dnormed_back, expert_out, up_part, down_part, *landed = pl.pallas_call(
+    ff_own = ff_width // 2
+    part = shape(ff_own, model_width)
+    dnormed_back, expert_out, up_part, down_part = pl.pallas_call(
         functools.partial(run_experts, dp_ways, sp_ways),
-        out_shape=[routed, routed, shape(ff_width, model_width), shape(ff_width, model_width)]
-        + landing,
-        in_specs=vmem(2) + hbm * 2,
-        out_specs=vmem(2) + hbm * (2 + len(landing)),
+        out_shape=[routed, routed, part, part],
+        in_specs=vmem(1) + hbm * 3,
+        out_specs=vmem(2) + hbm * 2,
         scratch_shapes=[
-            pltpu.VMEM((experts, slot_count, model_width), bf16),
-            pltpu.VMEM((ff_width, model_width), bf16),
-            pltpu.VMEM((ff_width, model_width), bf16),
-            pltpu.VMEM((experts * slot_count, ff_width), bf16),
-            pltpu.VMEM((experts * slot_count, ff_width), bf16),
+            pltpu.VMEM((2,) + routed.shape, bf16),
+            pltpu.VMEM((2,) + routed.shape, bf16),
+            pltpu.VMEM((ff_own, model_width), bf16),
+            pltpu.VMEM((ff_own, model_width), bf16),
+            pltpu.VMEM((2 * experts * slot_count, ff_own), bf16),
+            pltpu.VMEM((2 * experts * slot_count, ff_own), bf16),
             pltpu.VMEM((2 * slot_count, model_width), f32),
-            pltpu.VMEM((experts, slot_count, model_width), bf16),
+            pltpu.VMEM(routed.shape, f32),
+            pltpu.VMEM(routed.shape, bf16),
+            pltpu.VMEM(routed.shape, bf16),
+            pltpu.VMEM(routed.shape, bf16),
+            pltpu.VMEM(routed.shape, bf16),
+            pltpu.VMEM(routed.shape, bf16),
+            dma(2, sp_ways // 2),
             dma(2),
-            dma(2),
+            pltpu.SemaphoreType.DMA,
             dma(dp_ways),
             dma(dp_ways),
             dma(dp_ways),
             dma(dp_ways),
-        ]
-        + side_sems,
+            dma(dp_ways // 2 + 1),
+            dma(dp_ways // 2 + 1),
+            dma(dp_ways // 2 + 1),
+            dma(dp_ways // 2 + 1),
+        ],
         compiler_params=params(3),
     )(outgoing, arrived, up_weight[0], down_weight[0])
-    if sp_ways == 4:
-
-        def halves(part):
-            part = part.reshape(4, ff_width // 4, model_width)
-            return part[:, :, : model_width // 2], part[:, :, model_width // 2 :]
-
-        down_grad = scatter_halves(*halves(down_part), *landed, sp_at)[None]
-        landed = first_stage(*halves(up_part), sp_at)
-        up_grad = scatter_halves(*halves(up_part), *landed, sp_at)[None]
-    else:
-        up_grad, down_grad = (
-            lax.psum_scatter(part, "sp", scatter_dimension=0, tiled=True).astype(f32)[None]
-            for part in (up_part, down_part)
-        )
     dnormed2 = jnp.einsum(
         "er,ed->rd",
         placer,
@@ -876,13 +925,14 @@
     dmixed_b = dmixed_b.astype(bf16).reshape(seq_count, shard_len, model_width)
     out_grad = jnp.einsum("rd,re->de", mixed_b, dattn_b, preferred_element_type=f32).astype(bf16)
     out_part = lax.psum_scatter(out_grad, "sp", scatter_dimension=1, tiled=True)
+    landing = shape(sp_ways // 2 - 1, ff_width // sp_ways, model_width)
     grads = pl.pallas_call(
         functools.partial(attend_backward, sp_ways, dp_ways, head_dim),
         out_shape=[shape(seq_count, seq_len, width)] * 3
         + [shape(seq_count, shard_len, model_width)] * 3
-        + [routed],
-        in_specs=hbm + vmem(5),
-        out_specs=vmem(6) + hbm,
+        + [routed, landing, landing],
+        in_specs=hbm * 3 + vmem(5),
+        out_specs=vmem(6) + hbm * 3,
         scratch_shapes=[
             pltpu.VMEM((seq_count, seq_len, width), bf16),
             pltpu.VMEM((seq_len, width), f32),
@@ -894,11 +944,17 @@
             dma(3, seq_count, sp_ways),
             dma(dp_ways),
             dma(dp_ways),
+            dma(2, sp_ways // 2),
+            dma(2, sp_ways // 2),
             pltpu.SemaphoreType.DMA,
         ],
         compiler_params=params(1),
-    )(expert_out, dmixed_b, query_h, key_h, value_h, log_total)
-    head_grads, token_grads, returned = grads[:3], grads[3:6], grads[6]
+    )(expert_out, up_part, down_part, dmixed_b, query_h, key_h, value_h, log_total)
+    head_grads, token_grads, returned, *landed = grads[:3], grads[3:6], *grads[6:]
+    up_grad, down_grad = (
+        part[: ff_width // sp_ways].astype(f32)[None] + jnp.sum(land.astype(f32), axis=0)[None]
+        for part, land in zip((up_part, down_part), landed)
+    )
     expert_rows = jnp.einsum(
         "er,ed->rd",
         placer,

time: 563 us -> 540 us (0.959)
  Pallas kernels: 426 us -> 441 us
  other arithmetic: 44.6 us -> 29.6 us
  local copies, waits for them, and re-layouts: 22.4 us -> 12 us
  waiting for transfers between devices: 8.67 us -> 0.04 us
    pallas_call x1, Pallas kernels: 118 us -> 140 us  [local(): pl.pallas_call(functools.partial(run_experts, dp_ways, sp_ways), out_shap...]
    pallas_call x1, Pallas kernels: 119 us -> 108 us  [local(): pl.pallas_call(functools.partial(reduce_everywhere, sp_ways, columns), ou...]
    convert_element_type x4 -> x0, other arithmetic: 10.4 us -> none  [the longest x2 5.76 us: scatter_halves(): both(x_half, x_land, 1 - y_at, sp_at + 2 - 4 * y_at).astype(jnp.bfloat16)]
    slice x3 -> x1, local copies, waits for them, and re-layouts: 9.87 us -> 0.21 us  [the longest x2 9.66 us: halves(): return (part[:, :, :model_width // 2], part[:, :, model_width // 2:])]
    ppermute x6 -> x0, waiting for transfers between devices: 8.66 us -> none  [the longest x2 6.35 us: scatter_halves(): x_in = lax.ppermute(x_out, 'sp', ALONG_Y)]
  transfers between devices with their start and end apart: 7 -> 1, of which waited for: 2 -> 0; matrix products, arithmetic and copies ran while one was open for 10% -> 6% of each run, Pallas kernels for 21% -> 22%
where the time goes in v3:
time: 540 us; the launch traced here: 530 us
  Pallas kernels  441 us (82%)
  matrix products  32.9 us (6%)
  other arithmetic  29.6 us (5%)
  between operations  14.8 us (3%)
  local copies, waits for them, and re-layouts  12 us (2%)
    pallas_call x1, Pallas kernels, local(): pl.pallas_call(functools.partial(run_experts, dp_ways, sp_ways), out_shap...  140 us
    pallas_call x1, Pallas kernels, local(): pl.pallas_call(functools.partial(attend_backward, sp_ways, dp_ways, head_...  118 us
    pallas_call x1, Pallas kernels, local(): pl.pallas_call(functools.partial(reduce_everywhere, sp_ways, columns), ou...  108 us
    pallas_call x1, Pallas kernels, local(): pl.pallas_call(functools.partial(attend_forward, sp_ways, dp_ways, head_d...  74.5 us
  transfers between devices with their start and end apart: 1, of which 0 were waited for; matrix products, arithmetic and copies ran while one was open for 6% of the time, Pallas kernels for 22%

profile of v3, /device:TPU:9, one launch (start us, length us, event | category | flops | bytes accessed | tf_op | source)
XLA Modules:
  0.0 530.1 jit_solution(11420394843352943130)
XLA Ops:
  11.1 1.9 constant_dynamic-slice_fusion.2.wq_ref
  12.9 2.2 constant_dynamic-slice_fusion
  15.2 2.6 fusion.18
  17.8 74.5 %shard_map.237 = (bf16[2,1024,1024]{2,1,0:T(8,128)(2,1)}, bf16[2,1024,256]{2,1,0:T(8,128)(2,1)}, bf16[2,1024,256]{2,1,0:T(8,128)(2,1)}, bf16[2,1024,256]{2,1,0:T...) custom-call(bf16[8,128,1024]{2,1,0:T(8,128)(2,1)} %bitcast.111, ...), custom_call_target="tpu_custom_call" | custom-call | tf_op jit(solution)/shard_map/pallas_call | solution.py:836
  92.3 2.6 fusion.37
  95.6 2.8 fusion.19
  98.4 140.4 %shard_map.238 = (bf16[8,128,1024]{2,1,0:T(8,128)(2,1)}, bf16[8,128,1024]{2,1,0:T(8,128)(2,1)}, bf16[2048,1024]{1,0:T(8,128)(2,1)}, bf16[2048,1024]{1,0:T(8,128)(2,1)}) custom-call(bf16[8,128,1024]{2,1,0:T(8,128)(2,1)} %bitcast.110, bf16[8,128,1024]{2,1,0:T(8,128)(2,1)} %get-tuple-element.36.cot_ref, bf16[4096,1024]{1,0:T(8,128)(2,1)} %bitcast.107, ...), custom_call_target="tpu_custom_call" | custom-call | tf_op jit(solution)/shard_map/pallas_call | solution.py:882
  238.8 4.2 multiply_reduce_fusion
  245.2 2.6 convolution_convert_fusion
  248.1 3.8 convolution_convert_fusion.1
  252.3 118.0 %shard_map.239 = (bf16[2,1024,256]{2,1,0:T(8,128)(2,1)}, bf16[2,1024,256]{2,1,0:T(8,128)(2,1)}, bf16[2,1024,256]{2,1,0:T(8,128)(2,1)}, bf16[2,256,1024]{2,1,0:T(...) custom-call(bf16[8,128,1024]{2,1,0:T(8,128)(2,1)} %get-tuple-element, ...), custom_call_target="tpu_custom_call" | custom-call | tf_op jit(solution)/shard_map/pallas_call | solution.py:929
  370.4 3.3 fusion.38
  375.6 3.2 fusion.13
  379.5 4.1 fusion.12
  383.6 2.3 add_convert_fusion
  386.8 3.1 fusion
  389.9 1.3 copy-done.9
  391.2 3.1 fusion.1
  396.5 1.3 fusion.21
  397.8 1.6 fusion.22
  399.4 2.5 pad_maximum_fusion
  401.9 107.8 %shard_map.240 = (bf16[4096,1024]{1,0:T(8,128)(2,1)}, f32[8,1024]{1,0:T(8,128)}) custom-call(bf16[2,4,512,256]{3,2,1,0:T(8,128)(2,1)} %bitcast.109, f32[8,1024]{1,0:T(8,128)} %stack.27.small_ref), custom_call_target="tpu_custom_call" | custom-call | tf_op jit(solution)/shard_map/pallas_call | solution.py:993
  509.8 1.5 fusion.36
  512.5 10.3 %slice_convert_fusion = (f32[1024,1024]{1,0:T(8,128)}, f32[1024,1024]{1,0:T(8,128)}, f32[1024,1024]{1,0:T(8,128)}, f32[1024,1024]{1,0:T(8,128)}) fusion(bf16[4096,1024]{1,0:T(8,128)(2,1)} %get-tuple-element.53), kind=kLoop, calls=%fused_computation.21 | loop fusion | flops 4194304 | bytes 25165824 | tf_op jit(solution)/shard_map/convert_element_type | solution.py:1025
  (85 shorter events, 14.3 us)
Async XLA Ops:
  7.2 85.1 %copy-start = (bf16[1024,1024]{1,0:T(8,128)(2,1)S(1)}, bf16[1024,1024]{1,0:T(8,128)(2,1)}, u32[]{:S(2)}) copy-start(bf16[1024,1024]{1,0:T(8,128)(2,1)} %param.19) | copy-start | bytes 6291460
  7.2 8.0 %copy-start.11 = (bf16[2,256,1024]{2,1,0:T(8,128)(2,1)S(1)}, bf16[2,256,1024]{2,1,0:T(8,128)(2,1)}, u32[]{:S(2)}) copy-start(bf16[2,256,1024]{2,1,0:T(8,128)(2,1)} %param.26) | copy-start | bytes 3145732
  7.2 392.2 %reduce-scatter.2.cloned.1.call-start = ((), (), s32[]{:S(2)}) async-start(), calls=%async_computation.1 | async-start | bytes 2621440 | tf_op jit(solution)/shard_map/reduce_scatter | solution.py:927
  17.8 74.5 %copy-start.2 = (bf16[2,256,1024]{2,1,0:T(8,128)(2,1)S(1)}, bf16[2,256,1024]{2,1,0:T(8,128)(2,1)}, u32[]{:S(2)}) copy-start(bf16[2,256,1024]{2,1,0:T(8,128)(2,1)} %x_ref.1) | copy-start | bytes 3145732
  94.8 3.6 copy-start.5
  238.8 4.2 copy-start.6
  238.8 4.2 copy-start.12
  243.1 2.1 copy-start.22
  370.4 3.4 copy-start.13
  370.4 3.4 copy-start.24
  373.7 1.6 copy-start.14
  373.8 1.6 copy-start.15
  373.8 1.9 copy-start.23
  379.5 4.1 copy-start.7
  379.5 4.1 copy-start.18
  383.5 2.3 copy-start.4
  383.5 3.2 copy-start.10
  386.8 3.1 copy-start.3
  386.8 4.4 copy-start.9
  391.2 3.1 copy-start.17
  391.2 4.0 copy-start.21
  396.5 1.3 copy-start.19
  401.9 109.4 %copy-start.26 = (f32[8]{0:T(128)S(1)}, f32[8]{0:T(128)}, u32[]{:S(2)}) copy-start(f32[8]{0:T(128)} %param.27) | copy-start | bytes 100
  512.5 10.3 %copy-start.1 = (bf16[1024,1024]{1,0:T(8,128)(2,1)S(1)}, bf16[1024,1024]{1,0:T(8,128)(2,1)}, u32[]{:S(2)}) copy-start(bf16[1024,1024]{1,0:T(8,128)(2,1)} %param.19) | copy-start | bytes 6291460
  (4 other events, 4.1 us)
Sparse Core Ops, SparseCore 0:
  248.0 58.8 reduce-scatter.1

commit v4 on v3

--- a/solution.py
+++ b/solution.py
@@ -236,153 +236,6 @@
         for d in range(1, ways):
             x_copy(s, d).wait_send()
             mixed_copy(s, d).wait()
-    own.wait()
-    for copy in background:
-        copy.wait()
-
-
-def attend_backward(
-    ways,
-    others,
-    head_dim,
-    result_ref,
-    up_part,
-    down_part,
-    dmixed_ref,
-    q_ref,
-    k_ref,
-    v_ref,
-    log_ref,
-    dq_ref,
-    dk_ref,
-    dv_ref,
-    dq_tok,
-    dk_tok,
-    dv_tok,
-    returned_ref,
-    up_land,
-    down_land,
-    dmixed_h,
-    dq_f,
-    dk_f,
-    dv_f,
-    m_send,
-    m_recv,
-    g_send,
-    g_recv,
-    c_send,
-    c_recv,
-    s_send,
-    s_recv,
-    local_sem,
-):
-    seqs, shard, _ = dmixed_ref.shape
-    seq_len, width = q_ref.shape[1:]
-    heads = width // head_dim
-    me = lax.axis_index("sp")
-    peer = [lax.rem(me + d, ways) for d in range(ways)]
-    greet(
-        [{"sp": peer[d]} for d in range(1, ways)]
-        + [{"dp": flip(lax.axis_index("dp"), d)} for d in range(1, others)]
-    )
-    background = exchange(others, result_ref, returned_ref, c_send, c_recv)
-    shards = shards_of(me, ways)
-    size = up_land.shape[1]
-    background += [
-        send(
-            part.at[i * size : (i + 1) * size],
-            land.at[i - 1],
-            s_send.at[j, i],
-            s_recv.at[j, i],
-            {"sp": shards[i]},
-        )
-        for j, (part, land) in enumerate(((up_part, up_land), (down_part, down_land)))
-        for i in range(1, len(shards))
-    ]
-    own = pltpu.make_async_copy(
-        result_ref.at[lax.axis_index("dp")], returned_ref.at[lax.axis_index("dp")], local_sem
-    )
-
-    def dmixed_copy(s, d):
-        return send(
-            dmixed_ref.at[s, :, span(peer[d], width)],
-            dmixed_h.at[s, span(me, shard)],
-            m_send.at[s, d],
-            m_recv.at[s, d],
-            {"sp": peer[d]},
-        )
-
-    pairs = ((dq_ref, dq_tok), (dk_ref, dk_tok), (dv_ref, dv_tok))
-
-    def grad_copy(i, s, d):
-        source, target = pairs[i]
-        return send(
-            source.at[s, span(peer[d], shard)],
-            target.at[s, :, span(me, width)],
-            g_send.at[i, s, d],
-            g_recv.at[i, s, d],
-            {"sp": peer[d]},
-        )
-
-    for s in range(seqs):
-        for d in range(1, ways):
-            dmixed_copy(s, d).start()
-    own.start()
-    for copy in background:
-        copy.start()
-    lane = lax.broadcasted_iota(jnp.int32, (1, width), 1) // head_dim
-    visible = lax.broadcasted_iota(jnp.int32, (BLOCK, BLOCK), 0) <= lax.broadcasted_iota(
-        jnp.int32, (BLOCK, BLOCK), 1
-    )
-    scale = head_dim ** (-0.5)
-    for s in range(seqs):
-        dmixed_h[s, span(me, shard), :] = dmixed_ref[s, :, span(me, width)]
-        for d in range(1, ways):
-            dmixed_copy(s, d).wait_recv()
-        dq_f[...] = jnp.zeros_like(dq_f)
-        dk_f[...] = jnp.zeros_like(dk_f)
-        dv_f[...] = jnp.zeros_like(dv_f)
-
-        def one_head(h, carry):
-            mine = (lane == h).astype(jnp.float32)
-            for at in range(0, seq_len, BLOCK):
-                rows = slice(at, at + BLOCK)
-                query = (q_ref[s, rows, :].astype(jnp.float32) * (mine * scale)).astype(
-                    jnp.bfloat16
-                )
-                dout = (dmixed_h[s, rows, :].astype(jnp.float32) * mine).astype(jnp.bfloat16)
-                log_row = log_ref[s, pl.ds(h, 1), rows]
-                parts = [(rows, True)] + ([(slice(0, at), False)] if at else [])
-                kept = []
-                delta = jnp.zeros((1, BLOCK), jnp.float32)
-                for keys, diagonal in parts:
-                    prob = jnp.exp(mxu(k_ref[s, keys, :], query, ROWS_BY_ROWS) - log_row)
-                    if diagonal:
-                        prob = jnp.where(visible, prob, 0.0)
-                    dprob = mxu(v_ref[s, keys, :], dout, ROWS_BY_ROWS)
-                    delta += jnp.sum(prob * dprob, axis=0, keepdims=True)
-                    kept.append((keys, prob, dprob))
-                dquery = jnp.zeros((BLOCK, width), jnp.float32)
-                for keys, prob, dprob in kept:
-                    dv_f[keys, :] += mxu(prob.astype(jnp.bfloat16), dout)
-                    dlogit = (prob * (dprob - delta)).astype(jnp.bfloat16)
-                    dk_f[keys, :] += mxu(dlogit, query)
-                    dquery += mxu(dlogit, k_ref[s, keys, :], COLS_BY_COLS)
-                dq_f[rows, :] += dquery * (mine * scale)
-            return carry
-
-        lax.fori_loop(0, heads, one_head, 0)
-        for i, total in enumerate((dq_f, dk_f, dv_f)):
-            source, target = pairs[i]
-            source[s] = total[...].astype(jnp.bfloat16)
-            for d in range(1, ways):
-                grad_copy(i, s, d).start()
-            target[s, :, span(me, width)] = source[s, span(me, shard), :]
-    for s in range(seqs):
-        for d in range(1, ways):
-            dmixed_copy(s, d).wait_send()
-            for i in range(3):
-                grad_copy(i, s, d).wait()
     own.wait()
     for copy in background:
         copy.wait()
@@ -622,150 +475,407 @@
     store_down.wait()
 
 
-def reduce_everywhere(
+class Reduction:
+    def __init__(self, ways, columns, part, out, scratch):
+        (
+            self.core_land,
+            self.core_sum,
+            self.column_land,
+            self.piece,
+            core_send,
+            core_recv,
+            column_send,
+            column_recv,
+            spread_send,
+            spread_recv,
+            ring_send,
+            ring_recv,
+            cross_send,
+            cross_recv,
+            own_sem,
+        ) = scratch
+        me = lax.axis_index("sp")
+        dp = lax.axis_index("dp")
+        core = lax.rem(dp, 2)
+        column = dp // 2
+        twin = {"dp": dp + 1 - 2 * core}
+        self.ways, self.columns, self.part = ways, columns, part
+        self.core, self.column = core, column
+        rows, width = self.piece.shape
+        self.rows = rows
+
+        def beside(d):
+            return {"dp": 2 * lax.rem(column + d, columns) + core}
+
+        def block(at_core, at_column, at_sp, count):
+            first = pl.multiple_of((at_core * columns + at_column) * rows, rows)
+            return out.at[pl.ds(first, count * rows), span(at_sp, width)]
+
+        self.core_copy = send(
+            part.at[span(1 - core, columns * rows)], self.core_land, core_send, core_recv, twin
+        )
+        self.column_copy = [
+            send(
+                self.core_sum.at[span(lax.rem(column + d, columns), rows)],
+                self.column_land.at[d - 1],
+                column_send.at[d],
+                column_recv.at[d],
+                beside(d),
+            )
+            for d in range(1, columns)
+        ]
+        spot = block(core, column, me, 1)
+        self.own = pltpu.make_async_copy(self.piece, spot, own_sem)
+        self.spread_copy = [
+            send(self.piece, spot, spread_send.at[d], spread_recv.at[d], beside(d))
+            for d in range(1, columns)
+        ]
+        half = [block(core, 0, lax.rem(me + ways - d, ways), columns) for d in range(ways)]
+        self.ring_copy = [
+            send(
+                half[0],
+                half[0],
+                ring_send.at[d],
+                ring_recv.at[d],
+                {"sp": lax.rem(me + d, ways)},
+            )
+            for d in range(1, ways)
+        ]
+        self.cross_copy = [
+            send(half[d], half[d], cross_send.at[d], cross_recv.at[d], twin) for d in range(ways)
+        ]
+
+    def add_core(self):
+        self.core_copy.wait()
+        self.core_sum[...] = (
+            self.part[span(self.core, self.columns * self.rows), :].astype(jnp.float32)
+            + self.core_land[...].astype(jnp.float32)
+        ).astype(jnp.bfloat16)
+        for copy in self.column_copy:
+            copy.start()
+
+    def add_column(self):
+        total = self.core_sum[span(self.column, self.rows), :].astype(jnp.float32)
+        for d, copy in enumerate(self.column_copy):
+            copy.wait()
+            total += self.column_land[d].astype(jnp.float32)
+        return total
+
+    def spread(self):
+        self.own.start()
+        for copy in self.spread_copy:
+            copy.start()
+
+    def ring(self):
+        self.own.wait()
+        for copy in self.spread_copy:
+            copy.wait()
+        for copy in self.ring_copy:
+            copy.start()
+        self.cross_copy[0].start()
+
+    def cross(self):
+        for ring, cross in zip(self.ring_copy, self.cross_copy[1:]):
+            ring.wait_recv()
+            cross.start()
+
+    def finish(self):
+        for copy in self.ring_copy:
+            copy.wait_send()
+        for copy in self.cross_copy:
+            copy.wait()
+
+
+def backward(
     ways,
-    columns,
-    part_ref,
+    others,
+    head_dim,
+    result_ref,
+    up_part,
+    down_part,
+    normed_ref,
+    wq_ref,
+    wk_ref,
+    wv_ref,
+    dmixed_ref,
+    mixed_ref,
+    dattn_ref,
+    q_ref,
+    k_ref,
+    v_ref,
+    log_ref,
+    x_ref,
+    dresid_ref,
+    gain_ref,
     small_ref,
-    out_ref,
+    out_qkv,
+    out_o,
+    returned_ref,
+    up_land,
+    down_land,
+    tokens_ref,
     small_out,
-    core_land,
-    core_sum,
-    column_land,
-    piece,
+    dmixed_h,
+    dq_f,
+    dk_f,
+    dv_f,
+    grads_h,
+    grads_tok,
+    normed_v,
+    weights_v,
+    part_o,
+    part_w,
+    o_land,
+    small_own,
     small_land,
     small_sum,
-    core_send,
-    core_recv,
-    column_send,
-    column_recv,
-    spread_send,
-    spread_recv,
-    ring_send,
-    ring_recv,
-    cross_send,
-    cross_recv,
+    m_send,
+    m_recv,
+    g_send,
+    g_recv,
+    c_send,
+    c_recv,
+    s_send,
+    s_recv,
+    o_send,
+    o_recv,
     small_send,
     small_recv,
-    local_sem,
+    load_sem,
+    *scratch,
 ):
-    rows = part_ref.shape[2]
-    width = part_ref.shape[3]
+    seqs, shard, model = dmixed_ref.shape
+    seq_len, width = q_ref.shape[1:]
+    heads = width // head_dim
+    columns = others // 2
     me = lax.axis_index("sp")
     dp = lax.axis_index("dp")
     core = lax.rem(dp, 2)
-    column = dp // 2
-    twin = {"dp": dp + 1 - 2 * core}
-    column_peer = [lax.rem(column + d, columns) for d in range(columns)]
-    sp_peer = [lax.rem(me + d, ways) for d in range(ways)]
-    sp_origin = [lax.rem(me + ways - d, ways) for d in range(ways)]
-    column_id = [{"dp": 2 * column_peer[d] + core} for d in range(columns)]
-    sp_id = [{"sp": sp_peer[d]} for d in range(ways)]
-    greet([twin] + column_id[1:] + sp_id[1:])
-
-    first = send(part_ref.at[1 - core], core_land, core_send, core_recv, twin)
-    first.start()
-    small_first = send(small_ref, small_land.at[0], small_send.at[0], small_recv.at[0], twin)
-    small_first.start()
-    small_first.wait()
-    small_sum[0] = small_ref[...] + small_land[0]
-
-    def small_column(d):
+    peer = [lax.rem(me + d, ways) for d in range(ways)]
+    loads = [
+        pltpu.make_async_copy(source, target, load_sem.at[i])
+        for i, (source, target) in enumerate(
+            [(normed_ref, normed_v)]
+            + [(source, weights_v.at[i]) for i, source in enumerate((wq_ref, wk_ref, wv_ref))]
+            + [(result_ref.at[dp], returned_ref.at[dp])]
+        )
+    ]
+    for copy in loads:
+        copy.start()
+    greet(
+        [{"sp": peer[d]} for d in range(1, ways)]
+        + [{"dp": flip(dp, d)} for d in range(1, others)]
+    )
+
+    def dmixed_copy(s, d):
         return send(
-            small_sum.at[0],
-            small_land.at[d],
-            small_send.at[d],
-            small_recv.at[d],
-            column_id[d],
+            dmixed_ref.at[s, :, span(peer[d], width)],
+            dmixed_h.at[s, span(me, shard)],
+            m_send.at[s, d],
+            m_recv.at[s, d],
+            {"sp": peer[d]},
         )
 
-    def small_ring(d):
-        at = columns + d
+    def grad_copy(s, d):
         return send(
-            small_sum.at[1],
-            small_land.at[at],
-            small_send.at[at],
-            small_recv.at[at],
-            sp_id[d],
+            grads_h.at[s, span(peer[d], shard)],
+            grads_tok.at[s, :, span(me, 3 * width)],
+            g_send.at[s, d],
+            g_recv.at[s, d],
+            {"sp": peer[d]},
         )
 
-    for d in range(1, columns):
-        small_column(d).start()
-    first.wait()
-    core_sum[...] = (
-        part_ref[core].astype(jnp.float32) + core_land[...].astype(jnp.float32)
-    ).astype(jnp.bfloat16)
-
-    def column_copy(d):
-        return send(
-            core_sum.at[column_peer[d]],
-            column_land.at[d],
-            column_send.at[d],
-            column_recv.at[d],
-            column_id[d],
+    for s in range(seqs):
+        for d in range(1, ways):
+            dmixed_copy(s, d).start()
+    routed_back = exchange(others, result_ref, returned_ref, c_send, c_recv)
+    for copy in routed_back[: others // 2 - 1]:
+        copy.start()
+    shards = shards_of(me, ways)
+    size = up_land.shape[1]
+    scatter = [
+        send(
+            part.at[i * size : (i + 1) * size],
+            land.at[i - 1],
+            s_send.at[j, i],
+            s_recv.at[j, i],
+            {"sp": shards[i]},
         )
-
-    for d in range(1, columns):
-        column_copy(d).start()
-    for d in range(1, columns):
-        small_column(d).wait()
-    total = small_sum[0]
-    for d in range(1, columns):
-        total += small_land[d]
-    small_sum[1] = total
-    for d in range(1, ways):
-        small_ring(d).start()
-    total = core_sum[column].astype(jnp.float32)
-    for d in range(1, columns):
-        column_copy(d).wait()
-        total += column_land[d].astype(jnp.float32)
-    piece[...] = total.astype(jnp.bfloat16)
-
-    def block(at_core, at_column, at_sp, count=1):
-        first_row = pl.multiple_of((at_core * columns + at_column) * rows, rows)
-        return out_ref.at[pl.ds(first_row, count * rows), span(at_sp, width)]
-
-    def spread_copy(d):
-        return send(
-            piece,
-            block(core, column, me),
-            spread_send.at[d],
-            spread_recv.at[d],
-            column_id[d],
+        for j, (part, land) in enumerate(((up_part, up_land), (down_part, down_land)))
+        for i in range(1, len(shards))
+    ]
+    sum_o = Reduction(ways, columns, part_o, out_o, scratch[:15])
+    sum_w = Reduction(ways, columns, part_w, out_qkv, scratch[15:])
+
+    def out_step(i, carry):
+        at = span(i, BLOCK)
+        left = mixed_ref[:, :, at].reshape(seqs * shard, BLOCK)
+        part_o[at, :] = mxu(left, dattn_ref[...], COLS_BY_COLS).astype(jnp.bfloat16)
+        return carry
+
+    lax.fori_loop(0, model // BLOCK, out_step, 0)
+    sum_o.core_copy.start()
+
+    lane = lax.broadcasted_iota(jnp.int32, (1, width), 1) // head_dim
+    visible = lax.broadcasted_iota(jnp.int32, (BLOCK, BLOCK), 0) <= lax.broadcasted_iota(
+        jnp.int32, (BLOCK, BLOCK), 1
+    )
+    scale = head_dim ** (-0.5)
+    for s in range(seqs):
+        dmixed_h[s, span(me, shard), :] = dmixed_ref[s, :, span(me, width)]
+        for d in range(1, ways):
+            dmixed_copy(s, d).wait_recv()
+        if s == 0:
+            sum_o.add_core()
+            for copy in scatter:
+                copy.start()
+        dq_f[...] = jnp.zeros_like(dq_f)
+        dk_f[...] = jnp.zeros_like(dk_f)
+        dv_f[...] = jnp.zeros_like(dv_f)
+
+        def one_head(h, carry):
+            mine = (lane == h).astype(jnp.float32)
+            for at in range(0, seq_len, BLOCK):
+                rows = slice(at, at + BLOCK)
+                query = (q_ref[s, rows, :].astype(jnp.float32) * (mine * scale)).astype(
+                    jnp.bfloat16
+                )
+                dout = (dmixed_h[s, rows, :].astype(jnp.float32) * mine).astype(jnp.bfloat16)
+                log_row = log_ref[s, pl.ds(h, 1), rows]
+                parts = [(rows, True)] + ([(slice(0, at), False)] if at else [])
+                kept = []
+                delta = jnp.zeros((1, BLOCK), jnp.float32)
+                for keys, diagonal in parts:
+                    prob = jnp.exp(mxu(k_ref[s, keys, :], query, ROWS_BY_ROWS) - log_row)
+                    if diagonal:
+                        prob = jnp.where(visible, prob, 0.0)
+                    dprob = mxu(v_ref[s, keys, :], dout, ROWS_BY_ROWS)
+                    delta += jnp.sum(prob * dprob, axis=0, keepdims=True)
+                    kept.append((keys, prob, dprob))
+                dquery = jnp.zeros((BLOCK, width), jnp.float32)
+                for keys, prob, dprob in kept:
+                    dv_f[keys, :] += mxu(prob.astype(jnp.bfloat16), dout)
+                    dlogit = (prob * (dprob - delta)).astype(jnp.bfloat16)
+                    dk_f[keys, :] += mxu(dlogit, query)
+                    dquery += mxu(dlogit, k_ref[s, keys, :], COLS_BY_COLS)
+                dq_f[rows, :] += dquery * (mine * scale)
+            return carry
+
+        lax.fori_loop(0, heads, one_head, 0)
+        for i, total in enumerate((dq_f, dk_f, dv_f)):
+            grads_h[s, :, i * width : (i + 1) * width] = total[...].astype(jnp.bfloat16)
+        for d in range(1, ways):
+            grad_copy(s, d).start()
+        grads_tok[s, :, span(me, 3 * width)] = grads_h[s, span(me, shard), :]
+
+    loads[0].wait()
+
+    def weight_step(i, carry):
+        at = span(i, BLOCK)
+        grad = mxu(normed_v[0, :, at], grads_h[0], COLS_BY_COLS)
+        for s in range(1, seqs):
+            grad += mxu(normed_v[s, :, at], grads_h[s], COLS_BY_COLS)
+        for j in range(3):
+            rows = pl.ds(pl.multiple_of(j * model + i * BLOCK, BLOCK), BLOCK)
+            part_w[rows, :] = grad[:, j * width : (j + 1) * width].astype(jnp.bfloat16)
+        return carry
+
+    lax.fori_loop(0, model // BLOCK, weight_step, 0)
+    sum_w.core_copy.start()
+
+    o_land[0] = sum_o.add_column().astype(jnp.bfloat16)
+    o_copy = [
+        send(
+            o_land.at[0, :, span(peer[d], width)],
+            o_land.at[d, :, 0:width],
+            o_send.at[d],
+            o_recv.at[d],
+            {"sp": peer[d]},
         )
-
-    for d in range(1, columns):
-        spread_copy(d).start()
-    own = pltpu.make_async_copy(piece, block(core, column, me), local_sem)
-    own.start()
-    for d in range(1, ways):
-        small_ring(d).wait()
-    total = small_sum[1]
-    for d in range(1, ways):
-        total += small_land[columns + d]
-    small_out[...] = total
-    own.wait()
-    for d in range(1, columns):
-        spread_copy(d).wait()
-
-    def ring_copy(d):
-        half = block(core, 0, me, columns)
-        return send(half, half, ring_send.at[d], ring_recv.at[d], sp_id[d])
-
-    def cross_copy(d):
-        half = block(core, 0, sp_origin[d], columns)
-        return send(half, half, cross_send.at[d], cross_recv.at[d], twin)
-
-    for d in range(1, ways):
-        ring_copy(d).start()
-    cross_copy(0).start()
-    for d in range(1, ways):
-        ring_copy(d).wait_recv()
-        cross_copy(d).start()
-    for d in range(1, ways):
-        ring_copy(d).wait_send()
-    for d in range(ways):
-        cross_copy(d).wait()
+        for d in range(1, ways)
+    ]
+    for copy in o_copy:
+        copy.start()
+    sum_w.add_core()
+    total = o_land[0, :, span(me, width)].astype(jnp.float32)
+    for d, copy in enumerate(o_copy):
+        copy.wait()
+        total += o_land[d + 1, :, 0:width].astype(jnp.float32)
+    sum_o.piece[...] = total.astype(jnp.bfloat16)
+    sum_o.spread()
+    sum_w.piece[...] = sum_w.add_column().astype(jnp.bfloat16)
+    sum_w.spread()
+    for copy in routed_back[others // 2 - 1 :]:
+        copy.start()
+    small_own[...] = small_ref[...]
+
+    def norm_grad(s):
+        for d in range(1, ways):
+            grad_copy(s, d).wait()
+        dnormed = jnp.zeros((shard, model), jnp.float32)
+        for j in range(ways):
+            for i in range(3):
+                at = (3 * j + i) * width
+                dnormed += mxu(
+                    grads_tok[s, :, at : at + width],
+                    weights_v[i, :, j * width : (j + 1) * width],
+                    ROWS_BY_ROWS,
+                )
+        values = x_ref[s].astype(jnp.float32)
+        gain = gain_ref[...]
+        _, unit, rstd = norm_forward(values, gain, jnp.zeros_like(gain))
+        dinput, gain_grad, shift_grad = norm_backward(dnormed, unit, rstd, gain)
+        tokens_ref[s] = (dresid_ref[s] + dinput).astype(jnp.bfloat16)
+        small_own[0:1, :] += gain_grad.reshape(1, model)
+        small_own[1:2, :] += shift_grad.reshape(1, model)
+
+    for copy in loads[1:4]:
+        copy.wait()
+    for s in range(seqs - 1):
+        norm_grad(s)
+    sum_o.ring()
+    sum_w.ring()
+    norm_grad(seqs - 1)
+
+    steps = [[{"dp": dp + 1 - 2 * core}]]
+    steps.append([{"dp": 2 * lax.rem(dp // 2 + d, columns) + core} for d in range(1, columns)])
+    steps.append([{"sp": peer[d]} for d in range(1, ways)])
+    slot = 0
+    source = small_own
+    for number, peers in enumerate(steps):
+        copies = [
+            send(
+                source,
+                small_land.at[slot + i],
+                small_send.at[slot + i],
+                small_recv.at[slot + i],
+                device,
+            )
+            for i, device in enumerate(peers)
+        ]
+        for copy in copies:
+            copy.start()
+        if number == 0:
+            sum_o.cross()
+        total = source[...]
+        for i, copy in enumerate(copies):
+            copy.wait()
+            total += small_land[slot + i]
+        slot += len(peers)
+        if number == len(steps) - 1:
+            small_out[...] = total
+        else:
+            small_sum[number] = total
+            source = small_sum.at[number]
+    sum_w.cross()
+    for s in range(seqs):
+        for d in range(1, ways):
+            dmixed_copy(s, d).wait_send()
+    for copy in routed_back + scatter:
+        copy.wait()
+    loads[4].wait()
+    sum_o.finish()
+    sum_w.finish()
 
 
 def vmem(count):
@@ -922,89 +1032,21 @@
     dresid = cot_b.astype(f32) + dresid_norm
     dattn_b = dresid.astype(bf16)
     dmixed_b = jnp.einsum("re,de->rd", dattn_b, out_weight, preferred_element_type=f32)
-    dmixed_b = dmixed_b.astype(bf16).reshape(seq_count, shard_len, model_width)
-    out_grad = jnp.einsum("rd,re->de", mixed_b, dattn_b, preferred_element_type=f32).astype(bf16)
-    out_part = lax.psum_scatter(out_grad, "sp", scatter_dimension=1, tiled=True)
-    landing = shape(sp_ways // 2 - 1, ff_width // sp_ways, model_width)
-    grads = pl.pallas_call(
-        functools.partial(attend_backward, sp_ways, dp_ways, head_dim),
-        out_shape=[shape(seq_count, seq_len, width)] * 3
-        + [shape(seq_count, shard_len, model_width)] * 3
-        + [routed, landing, landing],
-        in_specs=hbm * 3 + vmem(5),
-        out_specs=vmem(6) + hbm * 3,
-        scratch_shapes=[
-            pltpu.VMEM((seq_count, seq_len, width), bf16),
-            pltpu.VMEM((seq_len, width), f32),
-            pltpu.VMEM((seq_len, width), f32),
-            pltpu.VMEM((seq_len, width), f32),
-            dma(seq_count, sp_ways),
-            dma(seq_count, sp_ways),
-            dma(3, seq_count, sp_ways),
-            dma(3, seq_count, sp_ways),
-            dma(dp_ways),
-            dma(dp_ways),
-            dma(2, sp_ways // 2),
-            dma(2, sp_ways // 2),
-            pltpu.SemaphoreType.DMA,
-        ],
-        compiler_params=params(1),
-    )(expert_out, up_part, down_part, dmixed_b, query_h, key_h, value_h, log_total)
-    head_grads, token_grads, returned, *landed = grads[:3], grads[3:6], *grads[6:]
-    up_grad, down_grad = (
-        part[: ff_width // sp_ways].astype(f32)[None] + jnp.sum(land.astype(f32), axis=0)[None]
-        for part, land in zip((up_part, down_part), landed)
-    )
-    expert_rows = jnp.einsum(
-        "er,ed->rd",
-        placer,
-        returned.reshape(experts * slot_count, model_width),
-        preferred_element_type=f32,
-    )
-    block_out = (residual_stream + expert_rows).astype(bf16)
-    block_out = block_out.reshape(seq_count, shard_len, model_width)
-    weight_parts = [
-        jnp.einsum("skd,ske->de", normed_all, grad, preferred_element_type=f32).astype(bf16)
-        for grad in head_grads
-    ]
-    dnormed1 = sum(
-        jnp.einsum(
-            "re,de->rd",
-            grad.reshape(row_count, model_width),
-            weight,
-            preferred_element_type=f32,
-        )
-        for grad, weight in zip(token_grads, (query_weight, key_weight, value_weight))
-    )
-    _, unit1, rstd1 = norm_forward(inputs, norm1_gain, norm1_shift)
-    dinput_norm, gain_one_grad, shift_one_grad = norm_backward(dnormed1, unit1, rstd1, norm1_gain)
-    tokens_grad = (dresid + dinput_norm).astype(bf16)
-    tokens_grad = tokens_grad.reshape(seq_count, shard_len, model_width)
     counts = jnp.sum(one_hot, axis=0).astype(f32)
     counts = jnp.pad(counts, (0, model_width - experts))
-    small = jnp.stack(
-        [gain_one_grad, shift_one_grad, gain_two_grad, shift_two_grad, counts]
-        + [jnp.zeros((model_width,), f32)] * 3
-    )
+    zeros = jnp.zeros((model_width,), f32)
+    small = jnp.stack([zeros, zeros, gain_two_grad, shift_two_grad, counts, zeros, zeros, zeros])
     columns = dp_ways // 2
-    piece_rows = 4 * model_width // dp_ways
-    packed = jnp.concatenate(weight_parts + [out_part], axis=0)
-    packed = packed.reshape(2, columns, piece_rows, width)
-    gathered, small_sum = pl.pallas_call(
-        functools.partial(reduce_everywhere, sp_ways, columns),
-        out_shape=[
-            shape(4 * model_width, model_width),
-            shape(8, model_width, dtype=f32),
-        ],
-        in_specs=vmem(2),
-        out_specs=[pl.BlockSpec(memory_space=pl.ANY), pl.BlockSpec(memory_space=pltpu.VMEM)],
-        scratch_shapes=[
-            pltpu.VMEM((columns, piece_rows, width), bf16),
-            pltpu.VMEM((columns, piece_rows, width), bf16),
-            pltpu.VMEM((columns, piece_rows, width), bf16),
-            pltpu.VMEM((piece_rows, width), bf16),
-            pltpu.VMEM((columns + sp_ways, 8, model_width), f32),
-            pltpu.VMEM((2, 8, model_width), f32),
+    rows_o, rows_w = model_width // dp_ways, 3 * model_width // dp_ways
+    landing = shape(sp_ways // 2 - 1, ff_width // sp_ways, model_width)
+    token_shape = (seq_count, shard_len, model_width)
+
+    def reduction(rows, part_width):
+        return [
+            pltpu.VMEM((columns * rows, part_width), bf16),
+            pltpu.VMEM((columns * rows, part_width), bf16),
+            pltpu.VMEM((columns - 1, rows, part_width), bf16),
+            pltpu.VMEM((rows, width), bf16),
             pltpu.SemaphoreType.DMA,
             pltpu.SemaphoreType.DMA,
             dma(columns),
@@ -1015,15 +1057,91 @@
             dma(sp_ways),
             dma(sp_ways),
             dma(sp_ways),
-            dma(columns + sp_ways),
-            dma(columns + sp_ways),
             pltpu.SemaphoreType.DMA,
+        ]
+
+    small_slots = 1 + (columns - 1) + (sp_ways - 1)
+    out_qkv, out_o, returned, up_land, down_land, tokens_grad, small_sum = pl.pallas_call(
+        functools.partial(backward, sp_ways, dp_ways, head_dim),
+        out_shape=[
+            shape(3 * model_width, model_width),
+            shape(model_width, model_width),
+            routed,
+            landing,
+            landing,
+            shape(*token_shape),
+            shape(8, model_width, dtype=f32),
         ],
-        compiler_params=params(2),
-    )(packed, small)
-    query_grad, key_grad, value_grad, out_grad = (
-        gathered[i * model_width : (i + 1) * model_width].astype(f32) for i in range(4)
-    )
+        in_specs=hbm * 7 + vmem(11),
+        out_specs=hbm * 5 + vmem(2),
+        scratch_shapes=[
+            pltpu.VMEM((seq_count, seq_len, width), bf16),
+            pltpu.VMEM((seq_len, width), f32),
+            pltpu.VMEM((seq_len, width), f32),
+            pltpu.VMEM((seq_len, width), f32),
+            pltpu.VMEM((seq_count, seq_len, 3 * width), bf16),
+            pltpu.VMEM((seq_count, shard_len, 3 * model_width), bf16),
+            pltpu.VMEM((seq_count, seq_len, model_width), bf16),
+            pltpu.VMEM((3, model_width, model_width), bf16),
+            pltpu.VMEM((model_width, model_width), bf16),
+            pltpu.VMEM((3 * model_width, width), bf16),
+            pltpu.VMEM((sp_ways, rows_o, model_width), bf16),
+            pltpu.VMEM((8, model_width), f32),
+            pltpu.VMEM((small_slots, 8, model_width), f32),
+            pltpu.VMEM((2, 8, model_width), f32),
+            dma(seq_count, sp_ways),
+            dma(seq_count, sp_ways),
+            dma(seq_count, sp_ways),
+            dma(seq_count, sp_ways),
+            dma(dp_ways),
+            dma(dp_ways),
+            dma(2, sp_ways // 2),
+            dma(2, sp_ways // 2),
+            dma(sp_ways),
+            dma(sp_ways),
+            dma(small_slots),
+            dma(small_slots),
+            dma(5),
+        ]
+        + reduction(rows_o, model_width)
+        + reduction(rows_w, width),
+        compiler_params=params(1),
+    )(
+        expert_out,
+        up_part,
+        down_part,
+        normed_all,
+        query_weight,
+        key_weight,
+        value_weight,
+        dmixed_b.astype(bf16).reshape(token_shape),
+        mixed_b.reshape(token_shape),
+        dattn_b,
+        query_h,
+        key_h,
+        value_h,
+        log_total,
+        tokens_in,
+        dresid.reshape(token_shape),
+        norm1_gain.reshape(1, model_width),
+        small,
+    )
+    up_grad, down_grad = (
+        (part[: ff_width // sp_ways].astype(f32) + jnp.sum(land.astype(f32), axis=0))[None]
+        for part, land in ((up_part, up_land), (down_part, down_land))
+    )
+    expert_rows = jnp.einsum(
+        "er,ed->rd",
+        placer,
+        returned.reshape(experts * slot_count, model_width),
+        preferred_element_type=f32,
+    )
+    block_out = (residual_stream + expert_rows).astype(bf16)
+    block_out = block_out.reshape(token_shape)
+    query_grad, key_grad, value_grad = (
+        out_qkv[i * model_width : (i + 1) * model_width].astype(f32) for i in range(3)
+    )
+    out_grad = out_o.astype(f32)
     load_now = small_sum[4, :experts] * experts / (row_count * dp_ways * sp_ways)
     load_next = 0.9 * load_mean + 0.1 * load_now
     return (

time: 540 us -> 470 us (0.87)
  Pallas kernels: 441 us -> 412 us
  matrix products: 32.9 us -> 17.8 us
  between operations: 14.8 us -> 1.03 us
    pallas_call x2 -> x1, Pallas kernels: 226 us -> 197 us  [local(): pl.pallas_call(functools.partial(backward, sp_ways, dp_ways, head_dim), o...]
    dot_general x7 -> x0, matrix products: 14.6 us -> none  [the longest x3 7.79 us: local(): jnp.einsum('re,de->rd', grad.reshape(row_count, model_width), weight, pre...]
    broadcast_in_dim x0 -> x2, other arithmetic: none -> 8.37 us  [local(): (part[:ff_width // sp_ways].astype(f32) + jnp.sum(land.astype(f32), axis=...]
    add x3 -> x0, other arithmetic: 6.91 us -> none  [the longest x2 6.11 us: local(): part[:ff_width // sp_ways].astype(f32)[None]]
    convert_element_type x2 -> x3, other arithmetic: 14.4 us -> 11.9 us  [the longest x1 5.12 us: local(): out_qkv[i * model_width:(i + 1) * model_width].astype(f32)]
  transfers between devices with their start and end apart: 1 -> 0, of which waited for: 0 -> 0; matrix products, arithmetic and copies ran while one was open for 6% -> 0% of each run, Pallas kernels for 22% -> 0%
where the time goes in v4:
time: 470 us; the launch traced here: 462 us
  Pallas kernels  412 us (88%)
  other arithmetic  24.7 us (5%)
  matrix products  17.8 us (4%)
  local copies, waits for them, and re-layouts  7.03 us (1%)
    pallas_call x1, Pallas kernels, local(): pl.pallas_call(functools.partial(backward, sp_ways, dp_ways, head_dim), o...  197 us
    pallas_call x1, Pallas kernels, local(): pl.pallas_call(functools.partial(run_experts, dp_ways, sp_ways), out_shap...  140 us
    pallas_call x1, Pallas kernels, local(): pl.pallas_call(functools.partial(attend_forward, sp_ways, dp_ways, head_d...  74.5 us

profile of v4, /device:TPU:9, one launch (start us, length us, event | category | flops | bytes accessed | tf_op | source)
XLA Modules:
  0.0 462.1 jit_solution(7525394321024135436)
XLA Ops:
  0.7 0.8 fusion.17
  1.5 1.1 reduce-window.6
  2.9 0.9 convert_reduce_fusion
  3.8 0.7 multiply_add_fusion.1
  4.5 1.9 constant_dynamic-slice_fusion.2.wq_ref
  6.4 2.2 constant_dynamic-slice_fusion
  8.6 2.6 fusion.6
  11.2 74.5 %shard_map.237 = (bf16[2,1024,1024]{2,1,0:T(8,128)(2,1)}, bf16[2,1024,256]{2,1,0:T(8,128)(2,1)}, bf16[2,1024,256]{2,1,0:T(8,128)(2,1)}, bf16[2,1024,256]{2,1,0:T...) custom-call(bf16[8,128,1024]{2,1,0:T(8,128)(2,1)} %bitcast.58, ...), custom_call_target="tpu_custom_call" | custom-call | tf_op jit(solution)/shard_map/pallas_call | solution.py:946
  85.7 2.6 fusion.20
  89.0 2.8 fusion.7
  91.8 140.1 %shard_map.238 = (bf16[8,128,1024]{2,1,0:T(8,128)(2,1)}, bf16[8,128,1024]{2,1,0:T(8,128)(2,1)}, bf16[2048,1024]{1,0:T(8,128)(2,1)}, bf16[2048,1024]{1,0:T(8,128)(2,1)}) custom-call(bf16[8,128,1024]{2,1,0:T(8,128)(2,1)} %bitcast.57, bf16[8,128,1024]{2,1,0:T(8,128)(2,1)} %get-tuple-element.32.cot_ref, bf16[4096,1024]{1,0:T(8,128)(2,1)} %bitcast.52, ...), custom_call_target="tpu_custom_call" | custom-call | tf_op jit(solution)/shard_map/pallas_call | solution.py:992
  232.0 5.3 %multiply_reduce_fusion = (f32[1024]{0:T(1024)S(1)}, f32[512]{0:T(512)S(1)}, f32[512]{0:T(512)S(1)}, f32[1024]{0:T(1024)S(1)}, f32[512,1024]{1,0:T(8,128)}) fusion(f32[512,1024]{1,0:T(8,128)} %copy-done.3, f32[512]{0:T(512)S(1)} %add_rsqrt_fusion, f32[512]{0:T(512)S(1)} %broadcast_multiply_fusion.2, f32[1024]{0:T(1024)S(1)} %copy-done.13, ...), kind=kOutput, calls=%fused_computation.9 | convolution fusion | flops 1078981632 | bytes 6313984 | tf_op jit(solution)/shard_map/er,ed->rd/dot_general | solution.py:1025
  237.3 0.7 stack.15.small_ref
  238.0 4.3 fusion.18
  242.3 2.3 convolution_convert_fusion
  244.5 196.9 %shard_map.239 = (bf16[3072,1024]{1,0:T(8,128)(2,1)}, bf16[1024,1024]{1,0:T(8,128)(2,1)}, bf16[8,128,1024]{2,1,0:T(8,128)(2,1)}, bf16[1,1024,1024]{2,1,0:T(8,128...) custom-call(bf16[8,128,1024]{2,1,0:T(8,128)(2,1)} %get-tuple-element.33.result_ref, ...), custom_call_target="tpu_custom_call" | custom-call | tf_op jit(solution)/shard_map/pallas_call | solution.py:1064
  441.5 5.3 %fusion = f32[1,1024,1024]{2,1,0:T(8,128)} fusion(bf16[1,1024,1024]{2,1,0:T(8,128)(2,1)} %get-tuple-element.48, bf16[2048,1024]{1,0:T(8,128)(2,1)} %get-tuple-element.35.down_part), kind=kLoop, calls=%fused_computation.1 | loop fusion | flops 3145728 | bytes 8388608 | tf_op jit(solution)/shard_map/broadcast_in_dim | solution.py:1130
  446.8 3.1 fusion.1
  449.9 2.3 add_convert_fusion
  452.2 0.5 bitcast_add_fusion
  452.7 0.6 fusion.19
  453.3 2.5 convert_element_type.75
  455.8 5.1 %slice_convert_fusion = (f32[1024,1024]{1,0:T(8,128)}, f32[1024,1024]{1,0:T(8,128)}, f32[1024,1024]{1,0:T(8,128)}) fusion(bf16[3072,1024]{1,0:T(8,128)(2,1)S(1)} %bitcast.55), kind=kLoop, calls=%fused_computation.5 | loop fusion | flops 3145728 | bytes 18874368 | tf_op jit(solution)/shard_map/convert_element_type | solution.py:1142
  461.0 1.0 copy.28
  (51 shorter events, 1.1 us)
Async XLA Ops:
  0.6 85.1 %copy-start = (bf16[1024,1024]{1,0:T(8,128)(2,1)S(1)}, bf16[1024,1024]{1,0:T(8,128)(2,1)}, u32[]{:S(2)}) copy-start(bf16[1024,1024]{1,0:T(8,128)(2,1)} %param.19) | copy-start | bytes 6291460
  0.7 7.9 %copy-start.9 = (bf16[2,256,1024]{2,1,0:T(8,128)(2,1)S(1)}, bf16[2,256,1024]{2,1,0:T(8,128)(2,1)}, u32[]{:S(2)}) copy-start(bf16[2,256,1024]{2,1,0:T(8,128)(2,1)} %param.26) | copy-start | bytes 3145732
  11.2 74.5 %copy-start.6 = (bf16[2,256,1024]{2,1,0:T(8,128)(2,1)S(1)}, bf16[2,256,1024]{2,1,0:T(8,128)(2,1)}, u32[]{:S(2)}) copy-start(bf16[2,256,1024]{2,1,0:T(8,128)(2,1)} %x_ref.3) | copy-start | bytes 3145732
  88.3 3.6 copy-start.3
  88.3 0.7 copy-start.13
  88.3 0.7 copy-start.15
  232.0 6.0 %copy-start.10 = (bf16[2,256,1024]{2,1,0:T(8,128)(2,1)S(1)}, bf16[2,256,1024]{2,1,0:T(8,128)(2,1)}, u32[]{:S(2)}) copy-start(bf16[2,256,1024]{2,1,0:T(8,128)(2,1)} %param.26) | copy-start | bytes 3145732
  242.3 2.3 copy-start.5
  441.5 5.3 %copy-start.2 = (bf16[2048,1024]{1,0:T(8,128)(2,1)S(1)}, bf16[2048,1024]{1,0:T(8,128)(2,1)}, u32[]{:S(2)}) copy-start(bf16[2048,1024]{1,0:T(8,128)(2,1)} %get-tuple-element.34.up_part) | copy-start | bytes 12582916
  441.5 5.3 %copy-start.8 = (bf16[1,1024,1024]{2,1,0:T(8,128)(2,1)S(1)}, bf16[1,1024,1024]{2,1,0:T(8,128)(2,1)}, u32[]{:S(2)}) copy-start(bf16[1,1024,1024]{2,1,0:T(8,128)(2,1)} %get-tuple-element.47) | copy-start | bytes 6291460
  446.8 3.1 copy-start.4
  446.8 3.1 copy-start.14
  446.8 9.0 %slice-start = ((s8[6291456]{0:T(1024)(128)(4,1)}), s8[4194304]{0:T(1024)(128)(4,1)S(1)}, s32[]{:S(2)}) async-start(s8[6291456]{0:T(1024)(128)(4,1)} %bitcast.54), calls=%async_computation | async-start | bytes 8388608
  449.9 2.3 copy-start.12
  449.9 2.3 copy-start.16
  449.9 3.4 copy-start.7
  449.9 5.9 %slice-start.1 = ((s8[6291456]{0:T(1024)(128)(4,1)}), s8[2097152]{0:T(1024)(128)(4,1)S(1)}, s32[]{:S(2)}) async-start(s8[6291456]{0:T(1024)(128)(4,1)} %bitcast.54), calls=%async_computation.1 | async-start | bytes 4194304
  455.8 5.1 %copy-start.11 = (bf16[2,256,1024]{2,1,0:T(8,128)(2,1)S(1)}, bf16[2,256,1024]{2,1,0:T(8,128)(2,1)}, u32[]{:S(2)}) copy-start(bf16[2,256,1024]{2,1,0:T(8,128)(2,1)} %get-tuple-element.83) | copy-start | bytes 3145732
  455.8 6.1 %copy-start.1 = (bf16[1024,1024]{1,0:T(8,128)(2,1)S(1)}, bf16[1024,1024]{1,0:T(8,128)(2,1)}, u32[]{:S(2)}) copy-start(bf16[1024,1024]{1,0:T(8,128)(2,1)} %param.19) | copy-start | bytes 6291460

commit v5 on v4

--- a/solution.py
+++ b/solution.py
@@ -267,6 +267,7 @@
     result_ref,
     up_part,
     down_part,
+    up_land,
     received,
     arrived,
     up_v,
@@ -291,8 +292,10 @@
     f_recv,
     p_send,
     p_recv,
+    s_send,
+    s_recv,
 ):
-    slots, width = received.shape[2:]
+    slots, width = received.shape[1:]
     rows = others * slots
     ff = up_v.shape[0]
     groups = others // 2
@@ -313,15 +316,19 @@
     own_cot.start()
     for copy in loads:
         copy.start()
-    greet([{"dp": flip(me, d)} for d in range(1, others)] + [pair])
-    inward = exchange(others, outgoing_ref, received.at[0], a_send, a_recv)
+    greet(
+        [{"dp": flip(me, d)} for d in range(1, others)]
+        + [pair]
+        + [{"sp": shard} for shard in shards[1:]]
+    )
+    inward = exchange(others, outgoing_ref, received.at[0:others], a_send, a_recv)
     outward = exchange(others, dnormed, back_ref, b_send, b_recv)
     near = [flip(chip, group) for group in range(groups)]
     chips = [pl.ds(2 * near[group], 2) for group in range(groups)]
     forward = [
         send(
-            received.at[0, chips[group]],
-            received.at[1, chips[group]],
+            received.at[chips[group]],
+            received.at[pl.ds(others + 2 * near[group], 2)],
             f_send.at[group],
             f_recv.at[group],
             pair,
@@ -341,9 +348,12 @@
     ]
     out_copy = send(out_pair, out_land, p_send.at[groups], p_recv.at[groups], pair)
 
-    for copy in inward:
+    early = range(groups // 2)
+    middle = range(groups // 2, 3 * groups // 4)
+    late = range(3 * groups // 4, groups)
+    for copy in inward[: 2 * late[0] - 1]:
         copy.start()
-    received[0, me] = outgoing_ref[me]
+    received[me] = outgoing_ref[me]
     cot_copy.start()
 
     def slab_of(half, group):
@@ -366,7 +376,7 @@
 
         def up_step(i, carry):
             at = span(i, STEP)
-            tokens = received[half, chips[group]].reshape(2 * slots, width)
+            tokens = received[pl.ds(half * others + 2 * near[group], 2)].reshape(2 * slots, width)
             pre = mxu(tokens, up_v[at, :], ROWS_BY_ROWS)
             square = pre * pre
             inner = jnp.tanh(GELU_ROOT * pre * (1.0 + CUBIC_TERM * square))
@@ -404,6 +414,10 @@
             else:
                 back_ref[me] = dnormed[me]
 
+    def up_pair(group):
+        forward[group].wait_recv()
+        up_half(1, group)
+
     pass_on(0)
     own_cot.wait()
     for copy in loads[: len(shards)]:
@@ -412,28 +426,33 @@
     for copy in loads[len(shards) :]:
         copy.wait()
     up_half(0, 0)
+    for group in early[1:]:
+        pass_on(group)
+    for copy in inward[2 * middle[0] - 1 : 2 * late[0] - 1]:
+        copy.wait_send()
+    for copy in inward[2 * late[0] - 1 :]:
+        copy.start()
     cot_copy.wait_recv()
     cot_half(1)
-    forward[0].wait_recv()
-    up_half(1, 0)
-    early = groups // 2
-    for group in range(1, early):
+    for group in middle:
+        pass_on(group)
+    up_pair(0)
+    for group in early[1:]:
+        up_half(0, group)
+        up_pair(group)
+    for group in middle:
+        up_half(0, group)
+    for group in early:
+        finish(group)
+    for group in middle:
+        up_pair(group)
+    for group in late:
         pass_on(group)
         up_half(0, group)
-        forward[group].wait_recv()
-        up_half(1, group)
-    for group in range(early):
+    for group in middle:
         finish(group)
-    for group in range(early, groups):
-        pass_on(group)
-        up_half(0, group)
-        if group > early:
-            forward[group - 1].wait_recv()
-            up_half(1, group - 1)
-    forward[groups - 1].wait_recv()
-    up_half(1, groups - 1)
-    for group in range(early, groups):
-        finish(group)
+    for group in late:
+        up_pair(group)
 
     def out_half(half):
         def out_step(i, carry):
@@ -448,28 +467,51 @@
 
         lax.fori_loop(0, groups, out_step, 0)
 
-    def grad(target, left, right_ref):
+    def grad(target, left, right_ref, block=0):
         def grad_step(i, carry):
             at = span(i, STEP)
             right = right_ref[...].reshape(2 * rows, width)
-            target[at, :] = mxu(left[:, at], right, COLS_BY_COLS).astype(jnp.bfloat16)
+            out = mxu(left[:, at], right, COLS_BY_COLS).astype(jnp.bfloat16)
+            if block:
+                target[span(i, STEP // block)] = out.reshape(STEP // block, block, width)
+            else:
+                target[at, :] = out
             return carry
 
         lax.fori_loop(0, ff // STEP, grad_step, 0)
 
     out_half(1)
     out_copy.start()
-    grad(up_v, slope_v, received)
-    store_up = pltpu.make_async_copy(up_v, up_part, o_sem.at[0])
+    for group in late:
+        finish(group)
+    grad(up_v, slope_v, received.at[0 : 2 * others])
+    store_up = pltpu.make_async_copy(up_v.at[0:size], up_part, o_sem.at[0])
     store_up.start()
+    scatter = [
+        send(
+            up_v.at[i * size : (i + 1) * size],
+            up_land.at[i - 1],
+            s_send.at[i],
+            s_recv.at[i],
+            {"sp": shards[i]},
+        )
+        for i in range(1, len(shards))
+    ]
+    for copy in scatter:
+        copy.start()
+    for copy in forward:
+        copy.wait_send()
+    grad(received, hidden, arrived, slots)
+    down_g = received.at[0 : ff // slots]
+    store_down = pltpu.make_async_copy(down_g, down_part, o_sem.at[1])
+    store_down.start()
     out_copy.wait_recv()
     out_half(0)
-    grad(down_v, hidden, arrived)
-    store_down = pltpu.make_async_copy(down_v, down_part, o_sem.at[1])
-    store_down.start()
-    for copy in inward + forward + [cot_copy] + dn_copy + [out_copy]:
+    for copy in inward[: 2 * middle[0] - 1] + inward[2 * late[0] - 1 :]:
         copy.wait_send()
-    for copy in outward:
+    for copy in [cot_copy] + dn_copy + [out_copy]:
+        copy.wait_send()
+    for copy in outward + scatter:
         copy.wait()
     store_up.wait()
     store_down.wait()
@@ -591,7 +633,6 @@
     others,
     head_dim,
     result_ref,
-    up_part,
     down_part,
     normed_ref,
     wq_ref,
@@ -611,7 +652,6 @@
     out_qkv,
     out_o,
     returned_ref,
-    up_land,
     down_land,
     tokens_ref,
     small_out,
@@ -692,16 +732,15 @@
     for copy in routed_back[: others // 2 - 1]:
         copy.start()
     shards = shards_of(me, ways)
-    size = up_land.shape[1]
+    size = down_part.shape[0] // len(shards)
     scatter = [
         send(
-            part.at[i * size : (i + 1) * size],
-            land.at[i - 1],
-            s_send.at[j, i],
-            s_recv.at[j, i],
+            down_part.at[i * size : (i + 1) * size],
+            down_land.at[i - 1],
+            s_send.at[i],
+            s_recv.at[i],
             {"sp": shards[i]},
         )
-        for j, (part, land) in enumerate(((up_part, up_land), (down_part, down_land)))
         for i in range(1, len(shards))
     ]
     sum_o = Reduction(ways, columns, part_o, out_o, scratch[:15])
@@ -988,14 +1027,18 @@
     outgoing = jnp.dot(placer, normed2_b, preferred_element_type=f32).astype(bf16)
     outgoing = outgoing.reshape(experts, slot_count, model_width)
     ff_own = ff_width // 2
-    part = shape(ff_own, model_width)
-    dnormed_back, expert_out, up_part, down_part = pl.pallas_call(
+    received_blocks = max(2 * experts, ff_own // slot_count)
+    part = shape(ff_own // slot_count, slot_count, model_width)
+    landing = shape(sp_ways // 2 - 1, ff_width // sp_ways, model_width)
+    down_landing = shape(sp_ways // 2 - 1, part.shape[0] * 2 // sp_ways, slot_count, model_width)
+    own_part = shape(ff_width // sp_ways, model_width)
+    dnormed_back, expert_out, up_part, down_part, up_land = pl.pallas_call(
         functools.partial(run_experts, dp_ways, sp_ways),
-        out_shape=[routed, routed, part, part],
+        out_shape=[routed, routed, own_part, part, landing],
         in_specs=vmem(1) + hbm * 3,
-        out_specs=vmem(2) + hbm * 2,
+        out_specs=vmem(2) + hbm * 3,
         scratch_shapes=[
-            pltpu.VMEM((2,) + routed.shape, bf16),
+            pltpu.VMEM((received_blocks, slot_count, model_width), bf16),
             pltpu.VMEM((2,) + routed.shape, bf16),
             pltpu.VMEM((ff_own, model_width), bf16),
             pltpu.VMEM((ff_own, model_width), bf16),
@@ -1019,6 +1062,8 @@
             dma(dp_ways // 2 + 1),
             dma(dp_ways // 2 + 1),
             dma(dp_ways // 2 + 1),
+            dma(sp_ways // 2),
+            dma(sp_ways // 2),
         ],
         compiler_params=params(3),
     )(outgoing, arrived, up_weight[0], down_weight[0])
@@ -1038,7 +1083,6 @@
     small = jnp.stack([zeros, zeros, gain_two_grad, shift_two_grad, counts, zeros, zeros, zeros])
     columns = dp_ways // 2
     rows_o, rows_w = model_width // dp_ways, 3 * model_width // dp_ways
-    landing = shape(sp_ways // 2 - 1, ff_width // sp_ways, model_width)
     token_shape = (seq_count, shard_len, model_width)
 
     def reduction(rows, part_width):
@@ -1061,19 +1105,18 @@
         ]
 
     small_slots = 1 + (columns - 1) + (sp_ways - 1)
-    out_qkv, out_o, returned, up_land, down_land, tokens_grad, small_sum = pl.pallas_call(
+    out_qkv, out_o, returned, down_land, tokens_grad, small_sum = pl.pallas_call(
         functools.partial(backward, sp_ways, dp_ways, head_dim),
         out_shape=[
             shape(3 * model_width, model_width),
             shape(model_width, model_width),
             routed,
-            landing,
-            landing,
+            down_landing,
             shape(*token_shape),
             shape(8, model_width, dtype=f32),
         ],
-        in_specs=hbm * 7 + vmem(11),
-        out_specs=hbm * 5 + vmem(2),
+        in_specs=hbm * 6 + vmem(11),
+        out_specs=hbm * 4 + vmem(2),
         scratch_shapes=[
             pltpu.VMEM((seq_count, seq_len, width), bf16),
             pltpu.VMEM((seq_len, width), f32),
@@ -1095,8 +1138,8 @@
             dma(seq_count, sp_ways),
             dma(dp_ways),
             dma(dp_ways),
-            dma(2, sp_ways // 2),
-            dma(2, sp_ways // 2),
+            dma(sp_ways // 2),
+            dma(sp_ways // 2),
             dma(sp_ways),
             dma(sp_ways),
             dma(small_slots),
@@ -1108,7 +1151,6 @@
         compiler_params=params(1),
     )(
         expert_out,
-        up_part,
         down_part,
         normed_all,
         query_weight,
@@ -1126,8 +1168,9 @@
         norm1_gain.reshape(1, model_width),
         small,
     )
+    down_part = down_part.reshape(ff_own, model_width)[: ff_width // sp_ways]
     up_grad, down_grad = (
-        (part[: ff_width // sp_ways].astype(f32) + jnp.sum(land.astype(f32), axis=0))[None]
+        (part.astype(f32) + jnp.sum(land.reshape(landing.shape).astype(f32), axis=0))[None]
         for part, land in ((up_part, up_land), (down_part, down_land))
     )
     expert_rows = jnp.einsum(

time: 470 us -> 441 us (0.938)
  Pallas kernels: 412 us -> 382 us
    pallas_call x1, Pallas kernels: 197 us -> 170 us  [local(): pl.pallas_call(functools.partial(backward, sp_ways, dp_ways, head_dim), o...]
    broadcast_in_dim x2 -> x1, other arithmetic: 8.37 us -> 2.93 us  [local(): (part.astype(f32) + jnp.sum(land.reshape(landing.shape).astype(f32), axis...]
where the time goes in v5:
time: 441 us; the launch traced here: 433 us
  Pallas kernels  382 us (87%)
  other arithmetic  22.5 us (5%)
  matrix products  17.8 us (4%)
  local copies, waits for them, and re-layouts  10.4 us (2%)
    pallas_call x1, Pallas kernels, local(): pl.pallas_call(functools.partial(backward, sp_ways, dp_ways, head_dim), o...  170 us
    pallas_call x1, Pallas kernels, local(): pl.pallas_call(functools.partial(run_experts, dp_ways, sp_ways), out_shap...  137 us
    pallas_call x1, Pallas kernels, local(): pl.pallas_call(functools.partial(attend_forward, sp_ways, dp_ways, head_d...  74.4 us

profile of v5, /device:TPU:9, one launch (start us, length us, event | category | flops | bytes accessed | tf_op | source)
XLA Modules:
  0.0 433.2 jit_solution(17869483573229113045)
XLA Ops:
  0.7 0.8 fusion.16
  1.5 1.1 reduce-window.6
  2.9 0.9 convert_reduce_fusion
  3.8 0.7 multiply_add_fusion.1
  4.5 1.9 constant_dynamic-slice_fusion.2.wq_ref
  6.4 2.2 constant_dynamic-slice_fusion
  8.6 2.6 fusion.5
  11.2 74.4 %shard_map.237 = (bf16[2,1024,1024]{2,1,0:T(8,128)(2,1)}, bf16[2,1024,256]{2,1,0:T(8,128)(2,1)}, bf16[2,1024,256]{2,1,0:T(8,128)(2,1)}, bf16[2,1024,256]{2,1,0:T...) custom-call(bf16[8,128,1024]{2,1,0:T(8,128)(2,1)} %bitcast.61, ...), custom_call_target="tpu_custom_call" | custom-call | tf_op jit(solution)/shard_map/pallas_call | solution.py:985
  85.6 2.6 fusion.19
  88.9 2.8 fusion.6
  91.7 137.5 %shard_map.238 = (bf16[8,128,1024]{2,1,0:T(8,128)(2,1)}, bf16[8,128,1024]{2,1,0:T(8,128)(2,1)}, bf16[1024,1024]{1,0:T(8,128)(2,1)}, bf16[16,128,1024]{2,1,0:T(8,128)(2,1)}, bf16[1,1024,1024]{2,1,0:T(8,128)(2,1)}) custom-call(bf16[8,128,1024]{2,1,0:T(8,128)(2,1)} %bitcast.60, bf16[8,128,1024]{2,1,0:T(8,128)(2,1)} %get-tuple-element.32.cot_ref, ...), custom_call_target="tpu_custom_call" | custom-call | tf_op jit(solution)/shard_map/pallas_call | solution.py:1035
  229.2 5.3 %multiply_reduce_fusion = (f32[1024]{0:T(1024)S(1)}, f32[512]{0:T(512)S(1)}, f32[512]{0:T(512)S(1)}, f32[1024]{0:T(1024)S(1)}, f32[512,1024]{1,0:T(8,128)}) fusion(f32[512,1024]{1,0:T(8,128)} %copy-done.2, f32[512]{0:T(512)S(1)} %add_rsqrt_fusion, f32[512]{0:T(512)S(1)} %broadcast_multiply_fusion.2, f32[1024]{0:T(1024)S(1)} %copy-done.14, ...), kind=kOutput, calls=%fused_computation.8 | convolution fusion | flops 1078981632 | bytes 6313984 | tf_op jit(solution)/shard_map/er,ed->rd/dot_general | solution.py:1070
  234.5 0.7 stack.15.small_ref
  235.2 4.3 fusion.17
  239.5 2.3 convolution_convert_fusion
  241.8 169.7 %shard_map.239 = (bf16[3072,1024]{1,0:T(8,128)(2,1)}, bf16[1024,1024]{1,0:T(8,128)(2,1)}, bf16[8,128,1024]{2,1,0:T(8,128)(2,1)}, bf16[1,8,128,1024]{3,2,1,0:T(8,...) custom-call(bf16[8,128,1024]{2,1,0:T(8,128)(2,1)} %get-tuple-element.33.result_ref, ...), custom_call_target="tpu_custom_call" | custom-call | tf_op jit(solution)/shard_map/pallas_call | solution.py:1108
  411.4 1.9 slice.43
  413.6 0.6 copy-done.15
  414.3 2.3 add_convert_fusion
  417.7 3.1 convert_add_fusion
  420.8 2.6 convert_element_type.100
  423.4 2.9 fusion
  426.9 5.1 %slice_convert_fusion = (f32[1024,1024]{1,0:T(8,128)}, f32[1024,1024]{1,0:T(8,128)}, f32[1024,1024]{1,0:T(8,128)}) fusion(bf16[3072,1024]{1,0:T(8,128)(2,1)S(1)} %bitcast.58), kind=kLoop, calls=%fused_computation.4 | loop fusion | flops 3145728 | bytes 18874368 | tf_op jit(solution)/shard_map/convert_element_type | solution.py:1185
  432.0 1.0 copy.28
  (54 shorter events, 3.0 us)
Async XLA Ops:
  0.6 84.9 %copy-start = (bf16[1024,1024]{1,0:T(8,128)(2,1)S(1)}, bf16[1024,1024]{1,0:T(8,128)(2,1)}, u32[]{:S(2)}) copy-start(bf16[1024,1024]{1,0:T(8,128)(2,1)} %param.19) | copy-start | bytes 6291460
  0.7 7.9 %copy-start.10 = (bf16[2,256,1024]{2,1,0:T(8,128)(2,1)S(1)}, bf16[2,256,1024]{2,1,0:T(8,128)(2,1)}, u32[]{:S(2)}) copy-start(bf16[2,256,1024]{2,1,0:T(8,128)(2,1)} %param.26) | copy-start | bytes 3145732
  11.2 74.4 %copy-start.5 = (bf16[2,256,1024]{2,1,0:T(8,128)(2,1)S(1)}, bf16[2,256,1024]{2,1,0:T(8,128)(2,1)}, u32[]{:S(2)}) copy-start(bf16[2,256,1024]{2,1,0:T(8,128)(2,1)} %x_ref.3) | copy-start | bytes 3145732
  88.1 3.6 copy-start.2
  88.1 0.7 copy-start.14
  88.1 0.7 copy-start.16
  229.2 6.0 %copy-start.11 = (bf16[2,256,1024]{2,1,0:T(8,128)(2,1)S(1)}, bf16[2,256,1024]{2,1,0:T(8,128)(2,1)}, u32[]{:S(2)}) copy-start(bf16[2,256,1024]{2,1,0:T(8,128)(2,1)} %param.26) | copy-start | bytes 3145732
  239.5 2.3 copy-start.4
  411.4 2.2 copy-start.3
  411.4 2.8 copy-start.15
  414.3 2.3 copy-start.13
  414.3 2.3 copy-start.17
  414.3 3.4 copy-start.9
  417.7 3.1 copy-start.6
  417.7 5.7 %copy-start.8 = (bf16[1,1024,1024]{2,1,0:T(8,128)(2,1)S(1)}, bf16[1,1024,1024]{2,1,0:T(8,128)(2,1)}, u32[]{:S(2)}) copy-start(bf16[1,1024,1024]{2,1,0:T(8,128)(2,1)} %get-tuple-element.47) | copy-start | bytes 6291460
  420.8 2.6 copy-start.7
  420.8 5.5 %slice-start = ((s8[6291456]{0:T(1024)(128)(4,1)}), s8[4194304]{0:T(1024)(128)(4,1)S(1)}, s32[]{:S(2)}) async-start(s8[6291456]{0:T(1024)(128)(4,1)} %bitcast.57), calls=%async_computation | async-start | bytes 8388608
  423.4 3.5 slice-start.1
  426.9 5.1 %copy-start.12 = (bf16[2,256,1024]{2,1,0:T(8,128)(2,1)S(1)}, bf16[2,256,1024]{2,1,0:T(8,128)(2,1)}, u32[]{:S(2)}) copy-start(bf16[2,256,1024]{2,1,0:T(8,128)(2,1)} %get-tuple-element.83) | copy-start | bytes 3145732
  426.9 6.1 %copy-start.1 = (bf16[1024,1024]{1,0:T(8,128)(2,1)S(1)}, bf16[1024,1024]{1,0:T(8,128)(2,1)}, u32[]{:S(2)}) copy-start(bf16[1024,1024]{1,0:T(8,128)(2,1)} %param.19) | copy-start | bytes 6291460
